TPU v7x, 256 devices: a whole 4x4x8 slice. The times are simulated.
256 devices in a mesh: dp: 16 (over z, x_hi), tensor: 16 (over y, x_lo, core).
Axes of the slice: x: 4 (x_hi: 2, x_lo: 2; x = x_hi * 2 + x_lo), y: 4, z: 8, core: 2. Of those that a mesh axis runs over, the one named last changes fastest.
Arguments:
- tokens: bfloat16 [8192, 6144], P('dp', 'tensor'), may hold values from -24 to 24
- upstream: bfloat16 [8192, 24576], P('dp', 'tensor'), may hold values from -0.15625 to 0.15625
- master_weights: float32 [128, 960, 128], P('dp', 'tensor'), may hold values from -0.03 to 0.03
- first_moment: float32 [128, 960, 128], P('dp', 'tensor'), may hold values from -0.5 to 0.5
- second_moment: float32 [128, 960, 128], P('dp', 'tensor'), may hold values from 0.05 to 0.5
- old_blocks: int32 [16, 60], replicated, may hold values from 0 to 9215, as said below
- new_blocks: int32 [16, 60], replicated, may hold values from 0 to 9215, as said below
- new_columns: int32 [16, 12], replicated, may hold values from 0 to 191, as said below
Outputs:
- hidden_out: bfloat16 [8192, 24576], P('dp', 'tensor')
- master_out: float32 [128, 960, 128], P('dp', 'tensor')
- first_out: float32 [128, 960, 128], P('dp', 'tensor')
- second_out: float32 [128, 960, 128], P('dp', 'tensor')
- weight_copy: bfloat16 [128, 960, 128], P(None, 'tensor')
Inputs may be any that keep to these rules, and one draw needn't show every extreme that they name: `old_blocks`: row i lists the 60 blocks owner i holds before the reset, in no particular order: all blocks of 12 block columns, 5 in each column; every block number appears at most once in the whole array and the owners' column sets are disjoint and cover all 192 columns. `new_blocks`: row i lists the 60 blocks owner i holds after the reset, in no particular order: all blocks of the columns new_columns[i]. Each column keeps 3 of its old blocks and gains from 0 to 4 blocks that were not there before, 2 a column on average over each owner's columns; every block number appears at most once. `new_columns`: row i lists owner i's 12 block columns after the reset, in the order in which they stand in upstream and hidden_out; every column once. Each owner hands 6 of its former columns to 6 different owners and receives 6 columns from 6 different owners, so between two owners exactly 3 surviving blocks or none change hands.
All inputs are finite; a program needn't handle non-finite values.
Results may differ from a plain program's by a relative error of at most 0.005.
Values may be sent and summed in bfloat16 or wider, within the bound.
No kernel may reach another device: no remote copies, remote signals or barrier semaphores. Data moves between devices by JAX's collectives and lax.ppermute only.
A program may use at most 128 MiB of HBM per device.

v0:
```python
import itertools

import jax
import jax.numpy as jnp
from jax import lax
from jax.experimental import pallas as pl
from jax.experimental.pallas import tpu as pltpu
from jax.sharding import PartitionSpec as P

STEP = 20
tanh_scale = 0.7978845608
cubic_coef = 0.044715
beta_one = 0.9
beta_two = 0.95
adam_eps = 1e-08
learn_rate = 0.002
weight_decay = 0.1

OWNERS = 16
SLOTS = 60
KEEP = 3
COLS = 12
KEPT = COLS * KEEP
B = 128
ROWS = 8
NBC = 192
ZN = 8
F32 = jnp.float32
BF16 = jnp.bfloat16
PARAMS = pltpu.CompilerParams(vmem_limit_bytes=56 * 1024 * 1024)

SEND, PLACE, BROW, BCOL, LIST, RANK = range(6)


def vmem():
    return pl.BlockSpec(memory_space=pltpu.VMEM)


def smem():
    return pl.BlockSpec(memory_space=pltpu.SMEM)


def sd(shape, dtype):
    return jax.ShapeDtypeStruct(shape, dtype)


def routing_table(me, old_ref, new_ref, cols_ref):
    n = SLOTS
    sub = lax.broadcasted_iota(jnp.int32, (n, n), 0)
    lane = lax.broadcasted_iota(jnp.int32, (n, n), 1)
    eye = sub == lane
    wide = lax.broadcasted_iota(jnp.int32, (n, 128), 1).astype(F32)
    slot = lax.broadcasted_iota(jnp.int32, (n, 128), 0).astype(F32)

    def to_col(row):
        return jnp.sum(jnp.where(eye, row, 0.0), axis=1, keepdims=True)

    def to_row(col):
        return jnp.sum(jnp.where(eye, col, 0.0), axis=0, keepdims=True)

    old_all = old_ref[...].astype(F32)
    new_all = new_ref[...].astype(F32)
    old_row = old_ref[pl.ds(me, 1), :].astype(F32)
    new_row = new_ref[pl.ds(me, 1), :].astype(F32)
    old_col = to_col(old_row)
    new_col = to_col(new_row)
    lane_f = lane.astype(F32)
    me_f = me.astype(F32) + 1.0
    zero = jnp.zeros((n, n), F32)
    target = zero
    source = zero
    source_slot = zero
    for o in range(OWNERS):
        target = target + jnp.where(old_col == new_all[o : o + 1, :], o + 1.0, 0.0)
        hit = new_col == old_all[o : o + 1, :]
        source = source + jnp.where(hit, o + 1.0, 0.0)
        source_slot = source_slot + jnp.where(hit, lane_f, 0.0)
    target = jnp.sum(target, axis=1, keepdims=True)
    source = jnp.sum(source, axis=1, keepdims=True)
    source_slot = jnp.sum(source_slot, axis=1, keepdims=True)

    def rank(kind_col, id_row, id_col):
        same = (to_row(kind_col) == kind_col) & (id_row < id_col)
        return jnp.sum(jnp.where(same, 1.0, 0.0), axis=1, keepdims=True)

    def listing(entry_col):
        return n + jnp.sum(jnp.where(entry_col == wide, slot - n, 0.0), axis=0, keepdims=True)

    moving = (target > 0.0) & (target != me_f)
    packet = jnp.where(moving, (target - 1.0) * KEEP + rank(target, old_row, old_col), -1.0)

    arrived = n + 1.0 + (source - 1.0) * KEEP + rank(source, new_row, new_col)
    kept = source > 0.0
    place = jnp.where(kept, jnp.where(source == me_f, source_slot, arrived), float(n))

    block_row = jnp.floor((new_col + 0.5) * (1.0 / NBC))
    block_col = new_col - block_row * NBC
    mine = cols_ref[pl.ds(me, 1), :].astype(F32)
    order = lax.broadcasted_iota(jnp.int32, (n, COLS), 1).astype(F32)
    kth = jnp.sum(jnp.where(block_col == mine, order, 0.0), axis=1, keepdims=True)
    kept_kth = jnp.where(kept, kth, -1.0)
    within = rank(kept_kth, lane_f[0:1, :], slot[:, 0:1])
    entry = jnp.where(kept, kth * KEEP + within, float(KEPT))

    def spread(col):
        return jnp.sum(jnp.where(slot == wide, col, 0.0), axis=0, keepdims=True)

    return [
        listing(packet), spread(place), spread(block_row), spread(kth), listing(entry), spread(entry),
    ]


def pack_kernel(
    me_ref, old_ref, new_ref, cols_ref, master_ref, first_ref, second_ref, table_ref, out_ref, scalars, sem
):
    rows = routing_table(me_ref[0], old_ref, new_ref, cols_ref)
    for i, row in enumerate(rows):
        table_ref[i : i + 1, :] = row.astype(jnp.int32)
    table_ref[len(rows) : 8, :] = jnp.zeros((8 - len(rows), 128), jnp.int32)
    copy = pltpu.make_async_copy(table_ref, scalars, sem)
    copy.start()
    copy.wait()

    def step(q, carry):
        slot = scalars[SEND, q]
        at = jnp.minimum(slot, SLOTS - 1)
        some = (jnp.zeros((ROWS, B), jnp.int32) + slot) < SLOTS
        for state, ref in enumerate((master_ref, first_ref, second_ref)):
            out_ref[q, state] = jnp.where(some, ref[at], 0.0)
        return carry

    lax.fori_loop(0, OWNERS * KEEP, step, 0, unroll=8)


def place_kernel(
    table_ref, master_in, first_in, second_in, arrived_ref,
    copy_ref, master_ref, first_ref, second_ref, mask_ref, scratch,
):
    def step(s, carry):
        index = table_ref[PLACE, s]
        here = jnp.minimum(index, SLOTS - 1)
        there = jnp.maximum(index - SLOTS - 1, 0)
        tag = jnp.zeros((ROWS, B), jnp.int32) + index
        kept = tag != SLOTS
        at = pl.ds(pl.multiple_of(s * ROWS, ROWS), ROWS)
        for state, (ref, out) in enumerate(
            ((master_in, master_ref), (first_in, first_ref), (second_in, second_ref))
        ):
            tile = jnp.where(tag < SLOTS, ref[here], arrived_ref[there, state])
            out[at, :] = jnp.where(kept, tile, 0.0)
        mask_ref[at, :] = jnp.where(kept, 1.0, 0.0)
        return carry

    lax.fori_loop(0, SLOTS, step, 0, unroll=6)

    def pick(i, carry):
        at = pl.ds(pl.multiple_of(table_ref[LIST, i] * ROWS, ROWS), ROWS)
        scratch[pl.ds(pl.multiple_of(i * ROWS, ROWS), ROWS), :] = master_ref[at, :]
        return carry

    lax.fori_loop(0, KEPT, pick, 0, unroll=6)
    copy_ref[...] = scratch[...].astype(BF16)


def assemble(pieces, z, xh, weights):
    for index, piece in enumerate(pieces):
        rel, other = divmod(index, 2)
        source = lax.rem(z + rel, ZN) * 2 + lax.rem(xh + other, 2)
        at = pl.ds(pl.multiple_of(source * ROWS, ROWS), ROWS)
        weights[:, at, :] = piece[...].astype(F32).reshape(KEPT, ROWS, B)


def main_kernel(*refs):
    table_ref, where_ref, tokens_ref, upstream_ref = refs[:4]
    pieces = refs[4:20]
    hidden_ref, keep_ref, send_ref = refs[20:23]
    weights, local_grad, grads = refs[23:]
    z = where_ref[0]
    xh = where_ref[1]
    sign = where_ref[2]
    assemble(pieces, z, xh, weights)

    def block(row):
        lanes = pl.ds(pl.multiple_of(lax.rem(row, 3) * B, B), B)
        return tokens_ref[row // 3, :, lanes]

    def forward(k, carry):
        xs = [block(table_ref[BROW, table_ref[LIST, k * KEEP + j]]) for j in range(KEEP)]
        w = jnp.concatenate([weights[k * KEEP + j] for j in range(KEEP)], axis=0).astype(BF16)
        total = jnp.dot(jnp.concatenate(xs, axis=1), w, preferred_element_type=F32)
        lanes = pl.ds(pl.multiple_of(k * B, B), B)
        square = total * total
        tangent = jnp.tanh(tanh_scale * (total + cubic_coef * square * total))
        half = 0.5 * (1.0 + tangent)
        hidden_ref[:, lanes] = (total * half).astype(BF16)
        slope = half + 0.5 * total * (1.0 - tangent * tangent) * tanh_scale * (
            1.0 + 3.0 * cubic_coef * square
        )
        local_grad[k] = (upstream_ref[:, lanes].astype(F32) * slope).astype(BF16)
        return carry

    lax.fori_loop(0, COLS, forward, 0)

    def backward(p, carry):
        for half in range(2):
            s = 2 * p + half
            x = block(table_ref[BROW, s])
            g = local_grad[table_ref[BCOL, s]]
            grads[half * B : (half + 1) * B, :] = lax.dot_general(
                x, g, (((0,), (0,)), ((), ())), preferred_element_type=F32
            )
        at = pl.ds(pl.multiple_of(p * 16, 16), 16)
        for rel in range(ZN):
            base = lax.rem(z + sign * rel + ZN, ZN) * 16

            def pair(start):
                a = grads[pl.ds(pl.multiple_of(start, ROWS), ROWS), :]
                b = grads[pl.ds(pl.multiple_of(start + B, ROWS), ROWS), :]
                return jnp.concatenate([a, b], axis=0)

            keep_ref[rel, at, :] = pair(base + xh * ROWS)
            send_ref[rel, at, :] = pair(base + (1 - xh) * ROWS).astype(BF16)
        return carry

    lax.fori_loop(0, SLOTS // 2, backward, 0)


def adam_kernel(
    table_ref, own_ref, got_ref, near_ref, last_ref, mast_ref, mom_ref, var_ref, mask_ref,
    master_ref, first_ref, second_ref, copy_ref, scratch,
):
    grad = own_ref[...] + got_ref[...].astype(F32)
    grad = grad + near_ref[...].astype(F32) + last_ref[...].astype(F32)
    master = mast_ref[...]
    kept = mask_ref[...] > 0.5
    new_first = beta_one * mom_ref[...] + (1.0 - beta_one) * grad
    new_second = beta_two * var_ref[...] + (1.0 - beta_two) * grad * grad
    first_hat = new_first / (1.0 - beta_one**STEP)
    second_hat = new_second / (1.0 - beta_two**STEP)
    denominator = jnp.where(kept, jnp.sqrt(second_hat) + adam_eps, 1.0)
    master_ref[...] = jnp.where(
        kept, master - learn_rate * (first_hat / denominator + weight_decay * master), 0.0
    )
    first_ref[...] = new_first
    second_ref[...] = new_second

    def pick(i, carry):
        at = pl.ds(pl.multiple_of(table_ref[LIST, i] * ROWS, ROWS), ROWS)
        scratch[pl.ds(pl.multiple_of(i * ROWS, ROWS), ROWS), :] = master_ref[at, :]
        return carry

    lax.fori_loop(0, KEPT, pick, 0, unroll=6)
    copy_ref[...] = scratch[...].astype(BF16)


def final_kernel(*refs):
    table_ref, where_ref = refs[:2]
    pieces = refs[2:18]
    out_ref, weights = refs[18:]
    assemble(pieces, where_ref[0], where_ref[1], weights)

    def step(s, carry):
        entry = table_ref[RANK, s]
        some = (jnp.zeros((B, B), jnp.int32) + entry) < KEPT
        out_ref[s] = jnp.where(some, weights[jnp.minimum(entry, KEPT - 1)], 0.0).astype(BF16)
        return carry

    lax.fori_loop(0, SLOTS, step, 0, unroll=2)


AXES = ("dp", "tensor")
SWAP = [(i, i ^ 1) for i in range(16)]
UP = [(i, (i + 2) % 16) for i in range(16)]
DOWN = [(i, (i - 2) % 16) for i in range(16)]


def direction(z, core):
    return 1 - 2 * ((z + core) % 2)


def exchange(side):
    out = []
    for z, xh, t in itertools.product(range(ZN), range(2), range(16)):
        other = (z + side * direction(z, t % 2)) % ZN
        out.append(((z * 2 + xh) * 16 + t, (other * 2 + xh) * 16 + t))
    return out


NEAR = exchange(1)
FAR = exchange(-1)


def gather_pieces(shard):
    pieces = [[None, None] for _ in range(ZN)]
    swapped = lax.ppermute(shard, "dp", SWAP)
    up = [shard, swapped]
    down = [shard, swapped]
    pieces[0] = [shard, swapped]
    for step in range(1, 4):
        for j in range(2):
            up[j] = lax.ppermute(up[j], "dp", UP)
            down[j] = lax.ppermute(down[j], "dp", DOWN)
            pieces[ZN - step][j] = up[j]
            pieces[step][j] = down[j]
    pieces[4][0] = lax.ppermute(up[0], "dp", UP)
    pieces[4][1] = lax.ppermute(down[1], "dp", DOWN)
    return [piece for pair in pieces for piece in pair]


def reduce_chunks(keep, send):
    joined = {}
    for group in ((4, 5), (2, 3), (6, 7), (0, 1)):
        got = lax.ppermute(send[group[0] : group[1] + 1], "dp", SWAP)
        for i, rel in enumerate(group):
            joined[rel] = (keep[rel], got[i])

    def total(rel, more=None):
        value = joined[rel][0] + joined[rel][1].astype(F32)
        return (value if more is None else value + more.astype(F32)).astype(BF16)

    a = lax.ppermute(jnp.stack([total(5), total(4)]), AXES, FAR)
    b = lax.ppermute(jnp.stack([total(2, a[0]), total(3, a[1])]), AXES, NEAR)
    c = lax.ppermute(jnp.stack([total(7, b[0]), total(6, b[1])]), AXES, FAR)
    d = lax.ppermute(total(1, c[1]), AXES, NEAR)
    return joined[0][0], joined[0][1], c[0], d


def local(tokens, upstream, master_weights, first_moment, second_moment, old_blocks, new_blocks, new_columns):
    owner = lax.axis_index("tensor")
    dp = lax.axis_index("dp")
    z = dp // 2
    me = jnp.reshape(owner, (1,)).astype(jnp.int32)
    where = jnp.stack([z, dp % 2, direction(z, owner % 2)]).astype(jnp.int32)
    states = [jnp.transpose(a, (1, 0, 2)) for a in (master_weights, first_moment, second_moment)]

    gathered = lax.all_gather(tokens, "tensor", axis=0)

    table, packed = pl.pallas_call(
        pack_kernel,
        out_shape=(sd((8, 128), jnp.int32), sd((OWNERS * KEEP, 3, ROWS, B), F32)),
        in_specs=[smem()] + [vmem()] * 6,
        out_specs=(vmem(),) * 2,
        scratch_shapes=[pltpu.SMEM((8, 128), jnp.int32), pltpu.SemaphoreType.DMA],
        compiler_params=PARAMS,
    )(me, old_blocks, new_blocks, new_columns, *states)
    arrived = lax.all_to_all(packed, "tensor", split_axis=0, concat_axis=0, tiled=True)

    flat = sd((SLOTS * ROWS, B), F32)
    flat16 = sd((KEPT * ROWS, B), BF16)
    copy_in, kept_master, kept_first, kept_second, mask = pl.pallas_call(
        place_kernel,
        out_shape=(flat16, flat, flat, flat, flat),
        in_specs=[smem()] + [vmem()] * 4,
        out_specs=(vmem(),) * 5,
        scratch_shapes=[pltpu.VMEM((KEPT * ROWS, B), F32)],
        compiler_params=PARAMS,
    )(table, *states, arrived)

    pieces = gather_pieces(copy_in)

    tokens_here = tokens.shape[0]
    hidden_out, keep, send = pl.pallas_call(
        main_kernel,
        out_shape=(
            sd((tokens_here, COLS * B), BF16),
            sd((ZN, SLOTS * ROWS, B), F32),
            sd((ZN, SLOTS * ROWS, B), BF16),
        ),
        in_specs=[smem()] * 2 + [vmem()] * 18,
        out_specs=(vmem(),) * 3,
        scratch_shapes=[
            pltpu.VMEM((KEPT, B, B), F32),
            pltpu.VMEM((COLS, tokens_here, B), BF16),
            pltpu.VMEM((2 * B, B), F32),
        ],
        compiler_params=PARAMS,
        cost_estimate=pl.CostEstimate(flops=4 * 10**9, bytes_accessed=2 * 10**7, transcendentals=10**6),
    )(table, where, gathered, upstream, *pieces)

    grads = reduce_chunks(keep, send)

    new_master, new_first, new_second, fresh = pl.pallas_call(
        adam_kernel,
        out_shape=(flat, flat, flat, flat16),
        in_specs=[smem()] + [vmem()] * 8,
        out_specs=(vmem(),) * 4,
        scratch_shapes=[pltpu.VMEM((KEPT * ROWS, B), F32)],
        compiler_params=PARAMS,
    )(table, *grads, kept_master, kept_first, kept_second, mask)

    final = gather_pieces(fresh)
    weight_copy = pl.pallas_call(
        final_kernel,
        out_shape=sd((SLOTS, B, B), BF16),
        in_specs=[smem()] * 2 + [vmem()] * 16,
        out_specs=vmem(),
        scratch_shapes=[pltpu.VMEM((KEPT, B, B), F32)],
        compiler_params=PARAMS,
    )(table, where, *final)

    def back(a):
        return jnp.transpose(a.reshape(SLOTS, -1, B), (1, 0, 2))

    return (hidden_out, back(new_master), back(new_first), back(new_second), back(weight_copy))


def solution(mesh):
    split = P("dp", "tensor", None)
    return jax.shard_map(
        local,
        mesh=mesh,
        in_specs=(P("dp", "tensor"), P("dp", "tensor"), split, split, split, P(), P(), P()),
        out_specs=(P("dp", "tensor"), split, split, split, P(None, "tensor", None)),
        check_vma=False,
    )
```

profile of v0, /device:TPU:6, one launch (start us, length us, event | category | flops | bytes accessed | tf_op | source)
XLA Modules:
  0.0 167.6 jit_solution(9563260869046245572)
XLA Ops:
  7.2 0.7 all-gather.3.cloned.1.call-update
  7.9 3.2 %shard_map.119 = (s32[8,128]{1,0:T(8,128)}, f32[48,3,8,128]{3,2,1,0:T(8,128)}) custom-call(s32[1]{0:T(128)} %bitcast.me_ref, s32[16,60]{1,0:T(8,128)} %old_ref.1, s32[16,60]{1,0:T(8,128)} %new_ref.1, s32[16,12]{1,0:T(8,128)} %cols_ref.1, f32[60,8,128]{2,1,0:T(8,128)} %bitcast.27, f32[60,8,128]{2,1,0:T(8,128)} %bitcast.29, f32[60,8,128]{2,1,0:T(8,128)} %bitcast.31), custom_call_target="tpu_custom_call" | custom-call | tf_op jit(solution)/shard_map/pallas_call | solution.py:338
  11.1 16.5 %all_to_all.5.arrived_ref = f32[48,3,8,128]{3,2,1,0:T(8,128)} all-to-all(f32[48,3,8,128]{3,2,1,0:T(8,128)} %get-tuple-element.20), channel_id=1, replica_groups=mesh['dp'=16,'tensor'=16] {'tensor'}, dimensions={0} | all-to-all | bytes 1179648 | tf_op jit(solution)/shard_map/all_to_all | solution.py:346
  27.6 3.0 %shard_map.120 = (bf16[288,128]{1,0:T(8,128)(2,1)}, f32[480,128]{1,0:T(8,128)}, f32[480,128]{1,0:T(8,128)}, f32[480,128]{1,0:T(8,128)}, f32[480,128]{1,0:T(8,128)}) custom-call(s32[8,128]{1,0:T(8,128)} %get-tuple-element.19.table_ref.refs_0_, f32[60,8,128]{2,1,0:T(8,128)} %bitcast.28, f32[60,8,128]{2,1,0:T(8,128)} %bitcast.30, f32[60,8,128]{2,1,0:T(8,128)} %bitcast.32, ...), custom_call_target="tpu_custom_call" | custom-call | tf_op jit(solution)/shard_map/pallas_call | solution.py:350
  30.6 1.7 %collective-permute-start = (bf16[288,128]{1,0:T(8,128)(2,1)}, bf16[288,128]{1,0:T(8,128)(2,1)S(1)}, u32[]{:S(2)}, u32[]{:S(2)}) collective-permute-start(bf16[288,128]{1,0:T(8,128)(2,1)} %get-tuple-element.21.refs_4_), channel_id=1, source_target_pairs={{0,16},{16,0},{32,48},{48,32},{64,80},{80,64},{96,112},{112,96},{1... | collective-permute-start | bytes 221192 | tf_op jit(solution)/shard_map/ppermute | solution.py:295
  32.4 1.6 collective-permute-start.7
  34.0 4.4 %collective-permute-done.refs_5_ = bf16[288,128]{1,0:T(8,128)(2,1)S(1)} collective-permute-done((bf16[288,128]{1,0:T(8,128)(2,1)}, bf16[288,128]{1,0:T(8,128)(2,1)S(1)}, u32[]{:S(2)}, u32[]{:S(2)}) %collective-permute-start) | collective-permute-done | bytes 73760 | tf_op jit(solution)/shard_map/ppermute | solution.py:295
  38.4 7.4 %collective-permute-start.2 = (bf16[288,128]{1,0:T(8,128)(2,1)S(1)}, bf16[288,128]{1,0:T(8,128)(2,1)S(1)}, u32[]{:S(2)}, u32[]{:S(2)}) collective-permute-start(bf16[288,128]{1,0:T(8,128)(2,1)S(1)} %collective-permute-done.refs_5_), channel_id=1, source_target_pairs={{0,224},{16,240},{32,0},{48,16},{64,32},{80,48},{96,64},{112,80},{... | collective-permute-start | bytes 221192 | tf_op jit(solution)/shard_map/ppermute | solution.py:302
  45.8 0.8 collective-permute-start.1
  46.6 1.3 collective-permute-start.8
  48.0 3.4 %collective-permute-start.4 = (bf16[288,128]{1,0:T(8,128)(2,1)S(1)}, bf16[288,128]{1,0:T(8,128)(2,1)S(1)}, u32[]{:S(2)}, u32[]{:S(2)}) collective-permute-start(bf16[288,128]{1,0:T(8,128)(2,1)S(1)} %collective-permute-done.2.refs_7_), channel_id=1, source_target_pairs={{0,224},{16,240},{32,0},{48,16},{64,32},{80,48},{96,64},{112,80},{... | collective-permute-start | bytes 221192 | tf_op jit(solution)/shard_map/ppermute | solution.py:302
  51.4 1.0 collective-permute-start.3
  52.4 1.1 collective-permute-start.9
  53.4 0.1 collective-permute-start.13
  53.5 3.4 %collective-permute-start.6 = (bf16[288,128]{1,0:T(8,128)(2,1)S(1)}, bf16[288,128]{1,0:T(8,128)(2,1)S(1)}, u32[]{:S(2)}, u32[]{:S(2)}) collective-permute-start(bf16[288,128]{1,0:T(8,128)(2,1)S(1)} %collective-permute-done.4.refs_9_), channel_id=1, source_target_pairs={{0,224},{16,240},{32,0},{48,16},{64,32},{80,48},{96,64},{112,80},{... | collective-permute-start | bytes 221192 | tf_op jit(solution)/shard_map/ppermute | solution.py:302
  57.0 1.5 collective-permute-start.5
  58.4 0.6 collective-permute-start.10
  59.0 0.8 collective-permute-done.13.refs_17_
  59.8 3.2 %collective-permute-start.11 = (bf16[288,128]{1,0:T(8,128)(2,1)S(1)}, bf16[288,128]{1,0:T(8,128)(2,1)S(1)}, u32[]{:S(2)}, u32[]{:S(2)}) collective-permute-start(bf16[288,128]{1,0:T(8,128)(2,1)S(1)} %collective-permute-done.6.refs_11_), channel_id=1, source_target_pairs={{0,224},{16,240},{32,0},{48,16},{64,32},{80,48},{96,64},{112,80},{... | collective-permute-start | bytes 221192 | tf_op jit(solution)/shard_map/ppermute | solution.py:306
  63.0 0.6 pad_add_fusion.refs_1_
  63.6 0.4 collective-permute-done.10.refs_12_
  64.0 1.4 collective-permute-done.14.refs_15_
  65.5 0.5 copy-done.30
  66.0 20.2 %shard_map.121 = (bf16[512,1536]{1,0:T(8,128)(2,1)}, f32[8,480,128]{2,1,0:T(8,128)}, bf16[8,480,128]{2,1,0:T(8,128)(2,1)}) custom-call(s32[8,128]{1,0:T(8,128)} %get-tuple-element.19.table_ref.refs_0_, s32[3]{0:T(128)} %pad_add_fusion.refs_1_, bf16[16,512,384]{2,1,0:T(8,128)(2,1)} %bitcast.33, bf16[512,1536]{1,0:T(8,128)(2,1)} %refs_3_.1, ...), custom_call_target="tpu_custom_call" | custom-call | flops 4000000000 | bytes 20000000 | tf_op jit(solution)/shard_map/pallas_call | solution.py:362
  86.2 1.5 fusion.1
  87.7 1.0 collective-permute-start.18
  88.7 2.6 %collective-permute-start.17 = (bf16[2,480,128]{2,1,0:T(8,128)(2,1)S(1)}, bf16[2,480,128]{2,1,0:T(8,128)(2,1)S(1)}, u32[]{:S(2)}, u32[]{:S(2)}) collective-permute-start(bf16[2,480,128]{2,1,0:T(8,128)(2,1)S(1)} %get-tuple-element.43), channel_id=1, source_target_pairs={{0,16},{16,0},{32,48},{48,32},{64,80},{80,64},{96,112},{112,96},{1... | collective-permute-start | bytes 737288 | tf_op jit(solution)/shard_map/ppermute | solution.py:313
  91.3 6.0 %collective-permute-done.18 = bf16[2,480,128]{2,1,0:T(8,128)(2,1)S(1)} collective-permute-done((bf16[2,480,128]{2,1,0:T(8,128)(2,1)S(1)}, bf16[2,480,128]{2,1,0:T(8,128)(2,1)S(1)}, u32[]{:S(2)}, u32[]{:S(2)}) %collective-permute-start.18) | collective-permute-done | bytes 245792 | tf_op jit(solution)/shard_map/ppermute | solution.py:313
  97.5 3.0 %collective-permute-start.19 = (bf16[2,480,128]{2,1,0:T(8,128)(2,1)S(1)}, bf16[2,480,128]{2,1,0:T(8,128)(2,1)S(1)}, u32[]{:S(2)}, u32[]{:S(2)}) collective-permute-start(bf16[2,480,128]{2,1,0:T(8,128)(2,1)S(1)} %pad_maximum_fusion), channel_id=1, source_target_pairs={{0,224},{1,33},{2,226},{3,35},{4,228},{5,37},{6,230},{7,39},{8,232... | collective-permute-start | bytes 737288 | tf_op jit(solution)/shard_map/ppermute | solution.py:321
  100.5 0.8 collective-permute-start.16
  101.3 3.6 %collective-permute-done.19 = bf16[2,480,128]{2,1,0:T(8,128)(2,1)S(1)} collective-permute-done((bf16[2,480,128]{2,1,0:T(8,128)(2,1)S(1)}, bf16[2,480,128]{2,1,0:T(8,128)(2,1)S(1)}, u32[]{:S(2)}, u32[]{:S(2)}) %collective-permute-start.19) | collective-permute-done | bytes 245792 | tf_op jit(solution)/shard_map/ppermute | solution.py:321
  105.0 0.1 add_convert_fusion.4
  105.1 0.1 collective-permute-start.20
  105.2 1.7 %collective-permute-start.15 = (bf16[2,480,128]{2,1,0:T(8,128)(2,1)S(1)}, bf16[2,480,128]{2,1,0:T(8,128)(2,1)S(1)}, u32[]{:S(2)}, u32[]{:S(2)}) collective-permute-start(bf16[2,480,128]{2,1,0:T(8,128)(2,1)S(1)} %get-tuple-element.44), channel_id=1, source_target_pairs={{0,16},{16,0},{32,48},{48,32},{64,80},{80,64},{96,112},{112,96},{1... | collective-permute-start | bytes 737288 | tf_op jit(solution)/shard_map/ppermute | solution.py:313
  106.9 1.3 collective-permute-done.16
  108.2 3.2 %collective-permute-done.20 = bf16[2,480,128]{2,1,0:T(8,128)(2,1)S(1)} collective-permute-done((bf16[2,480,128]{2,1,0:T(8,128)(2,1)S(1)}, bf16[2,480,128]{2,1,0:T(8,128)(2,1)S(1)}, u32[]{:S(2)}, u32[]{:S(2)}) %collective-permute-start.20) | collective-permute-done | bytes 245792 | tf_op jit(solution)/shard_map/ppermute | solution.py:322
  111.4 0.1 add_convert_fusion.2
  111.5 3.0 %collective-permute-start.21 = (bf16[2,480,128]{2,1,0:T(8,128)(2,1)S(1)}, bf16[2,480,128]{2,1,0:T(8,128)(2,1)S(1)}, u32[]{:S(2)}, u32[]{:S(2)}) collective-permute-start(bf16[2,480,128]{2,1,0:T(8,128)(2,1)S(1)} %pad_maximum_fusion.2), channel_id=1, source_target_pairs={{0,224},{1,33},{2,226},{3,35},{4,228},{5,37},{6,230},{7,39},{8,232... | collective-permute-start | bytes 737288 | tf_op jit(solution)/shard_map/ppermute | solution.py:323
  114.6 0.7 slice_bitcast_fusion.2.got_ref
  115.2 3.8 %collective-permute-done.21 = bf16[2,480,128]{2,1,0:T(8,128)(2,1)S(1)} collective-permute-done((bf16[2,480,128]{2,1,0:T(8,128)(2,1)S(1)}, bf16[2,480,128]{2,1,0:T(8,128)(2,1)S(1)}, u32[]{:S(2)}, u32[]{:S(2)}) %collective-permute-start.21) | collective-permute-done | bytes 245792 | tf_op jit(solution)/shard_map/ppermute | solution.py:323
  119.0 0.7 fusion
  119.8 0.2 collective-permute-start.22
  120.0 0.7 slice_bitcast_fusion.1.near_ref
  120.7 4.0 %collective-permute-done.22.last_ref = bf16[480,128]{1,0:T(8,128)(2,1)S(1)} collective-permute-done((bf16[480,128]{1,0:T(8,128)(2,1)S(1)}, bf16[480,128]{1,0:T(8,128)(2,1)S(1)}, u32[]{:S(2)}, u32[]{:S(2)}) %collective-permute-start.22) | collective-permute-done | bytes 122912 | tf_op jit(solution)/shard_map/ppermute | solution.py:324
  124.6 0.6 copy-done.1
  125.3 2.8 %shard_map.122 = (f32[480,128]{1,0:T(8,128)}, f32[480,128]{1,0:T(8,128)}, f32[480,128]{1,0:T(8,128)}, bf16[288,128]{1,0:T(8,128)(2,1)}) custom-call(s32[8,128]{1,0:T(8,128)} %get-tuple-element.19.table_ref.refs_0_, f32[480,128]{1,0:T(8,128)} %get-tuple-element.40.own_ref, bf16[480,128]{1,0:T(8,128)(2,1)} %slice_bitcast_fusion.2.got_ref, ...), custom_call_target="tpu_custom_call" | custom-call | tf_op jit(solution)/shard_map/pallas_call | solution.py:382
  128.0 1.8 %collective-permute-start.23 = (bf16[288,128]{1,0:T(8,128)(2,1)}, bf16[288,128]{1,0:T(8,128)(2,1)S(1)}, u32[]{:S(2)}, u32[]{:S(2)}) collective-permute-start(bf16[288,128]{1,0:T(8,128)(2,1)} %get-tuple-element.32.refs_2_), channel_id=1, source_target_pairs={{0,16},{16,0},{32,48},{48,32},{64,80},{80,64},{96,112},{112,96},{1... | collective-permute-start | bytes 221192 | tf_op jit(solution)/shard_map/ppermute | solution.py:295
  129.8 4.3 %collective-permute-done.23.refs_3_ = bf16[288,128]{1,0:T(8,128)(2,1)S(1)} collective-permute-done((bf16[288,128]{1,0:T(8,128)(2,1)}, bf16[288,128]{1,0:T(8,128)(2,1)S(1)}, u32[]{:S(2)}, u32[]{:S(2)}) %collective-permute-start.23) | collective-permute-done | bytes 73760 | tf_op jit(solution)/shard_map/ppermute | solution.py:295
  134.1 2.9 %collective-permute-start.25 = (bf16[288,128]{1,0:T(8,128)(2,1)S(1)}, bf16[288,128]{1,0:T(8,128)(2,1)S(1)}, u32[]{:S(2)}, u32[]{:S(2)}) collective-permute-start(bf16[288,128]{1,0:T(8,128)(2,1)S(1)} %collective-permute-done.23.refs_3_), channel_id=1, source_target_pairs={{0,224},{16,240},{32,0},{48,16},{64,32},{80,48},{96,64},{112,80},{... | collective-permute-start | bytes 221192 | tf_op jit(solution)/shard_map/ppermute | solution.py:302
  137.1 2.0 %collective-permute-start.31 = (bf16[288,128]{1,0:T(8,128)(2,1)S(1)}, bf16[288,128]{1,0:T(8,128)(2,1)S(1)}, u32[]{:S(2)}, u32[]{:S(2)}) collective-permute-start(bf16[288,128]{1,0:T(8,128)(2,1)S(1)} %collective-permute-done.30.refs_16_), channel_id=1, source_target_pairs={{0,32},{16,48},{32,64},{48,80},{64,96},{80,112},{96,128},{112,144}... | collective-permute-start | bytes 221192 | tf_op jit(solution)/shard_map/ppermute | solution.py:301
  139.2 3.6 %collective-permute-start.27 = (bf16[288,128]{1,0:T(8,128)(2,1)S(1)}, bf16[288,128]{1,0:T(8,128)(2,1)S(1)}, u32[]{:S(2)}, u32[]{:S(2)}) collective-permute-start(bf16[288,128]{1,0:T(8,128)(2,1)S(1)} %collective-permute-done.25.refs_5_), channel_id=1, source_target_pairs={{0,224},{16,240},{32,0},{48,16},{64,32},{80,48},{96,64},{112,80},{... | collective-permute-start | bytes 221192 | tf_op jit(solution)/shard_map/ppermute | solution.py:302
  142.8 0.8 collective-permute-start.26
  143.5 1.2 collective-permute-start.32
  144.8 0.1 collective-permute-start.36
  144.9 3.4 %collective-permute-start.29 = (bf16[288,128]{1,0:T(8,128)(2,1)S(1)}, bf16[288,128]{1,0:T(8,128)(2,1)S(1)}, u32[]{:S(2)}, u32[]{:S(2)}) collective-permute-start(bf16[288,128]{1,0:T(8,128)(2,1)S(1)} %collective-permute-done.27.refs_7_), channel_id=1, source_target_pairs={{0,224},{16,240},{32,0},{48,16},{64,32},{80,48},{96,64},{112,80},{... | collective-permute-start | bytes 221192 | tf_op jit(solution)/shard_map/ppermute | solution.py:302
  148.3 0.8 collective-permute-start.28
  149.1 1.2 collective-permute-start.33
  150.4 0.1 collective-permute-start.37
  150.5 3.4 %collective-permute-start.34 = (bf16[288,128]{1,0:T(8,128)(2,1)S(1)}, bf16[288,128]{1,0:T(8,128)(2,1)S(1)}, u32[]{:S(2)}, u32[]{:S(2)}) collective-permute-start(bf16[288,128]{1,0:T(8,128)(2,1)S(1)} %collective-permute-done.29.refs_9_), channel_id=1, source_target_pairs={{0,224},{16,240},{32,0},{48,16},{64,32},{80,48},{96,64},{112,80},{... | collective-permute-start | bytes 221192 | tf_op jit(solution)/shard_map/ppermute | solution.py:306
  153.9 0.8 collective-permute-done.33.refs_10_
  154.7 1.2 collective-permute-done.37.refs_13_
  156.1 0.5 copy-done.15
  156.6 0.6 copy-done.16
  157.2 3.6 %shard_map.123 = bf16[60,128,128]{2,1,0:T(8,128)(2,1)} custom-call(s32[8,128]{1,0:T(8,128)} %get-tuple-element.19.table_ref.refs_0_, s32[3]{0:T(128)} %pad_add_fusion.refs_1_, bf16[288,128]{1,0:T(8,128)(2,1)} %get-tuple-element.32.refs_2_, bf16[288,128]{1,0:T(8,128)(2,1)} %copy-done.2, bf16[288,128]{1,0:T(8,128)(2,1)} %copy-done.5, ...), custom_call_target="tpu_custom_call" | custom-call | tf_op jit(solution)/shard_map/pallas_call | solution.py:392
  (96 shorter events, 0.6 us)
Async XLA Ops:
  7.2 58.2 %all-gather.3.cloned.1.call-start = ((), (), s32[]{:S(2)}) async-start(), calls=%async_computation.1 | async-start | bytes 6684672 | tf_op jit(solution)/shard_map/all_gather | solution.py:336
  30.6 7.8 %collective-permute-start = (bf16[288,128]{1,0:T(8,128)(2,1)}, bf16[288,128]{1,0:T(8,128)(2,1)S(1)}, u32[]{:S(2)}, u32[]{:S(2)}) collective-permute-start(bf16[288,128]{1,0:T(8,128)(2,1)} %get-tuple-element.21.refs_4_), channel_id=1, source_target_pairs={{0,16},{16,0},{32,48},{48,32},{64,80},{80,64},{96,112},{112,96},{1... | collective-permute-start | bytes 221192 | tf_op jit(solution)/shard_map/ppermute | solution.py:295
  32.4 14.2 %collective-permute-start.7 = (bf16[288,128]{1,0:T(8,128)(2,1)}, bf16[288,128]{1,0:T(8,128)(2,1)S(1)}, u32[]{:S(2)}, u32[]{:S(2)}) collective-permute-start(bf16[288,128]{1,0:T(8,128)(2,1)} %get-tuple-element.21.refs_4_), channel_id=1, source_target_pairs={{0,32},{16,48},{32,64},{48,80},{64,96},{80,112},{96,128},{112,144}... | collective-permute-start | bytes 221192 | tf_op jit(solution)/shard_map/ppermute | solution.py:301
  38.4 27.0 %copy-start.17 = (bf16[288,128]{1,0:T(8,128)(2,1)}, bf16[288,128]{1,0:T(8,128)(2,1)S(1)}, u32[]{:S(2)}) copy-start(bf16[288,128]{1,0:T(8,128)(2,1)S(1)} %collective-permute-done.refs_5_) | copy-start | bytes 221188
  38.4 9.5 %collective-permute-start.2 = (bf16[288,128]{1,0:T(8,128)(2,1)S(1)}, bf16[288,128]{1,0:T(8,128)(2,1)S(1)}, u32[]{:S(2)}, u32[]{:S(2)}) collective-permute-start(bf16[288,128]{1,0:T(8,128)(2,1)S(1)} %collective-permute-done.refs_5_), channel_id=1, source_target_pairs={{0,224},{16,240},{32,0},{48,16},{64,32},{80,48},{96,64},{112,80},{... | collective-permute-start | bytes 221192 | tf_op jit(solution)/shard_map/ppermute | solution.py:302
  45.8 5.6 %collective-permute-start.1 = (bf16[288,128]{1,0:T(8,128)(2,1)}, bf16[288,128]{1,0:T(8,128)(2,1)S(1)}, u32[]{:S(2)}, u32[]{:S(2)}) collective-permute-start(bf16[288,128]{1,0:T(8,128)(2,1)} %get-tuple-element.21.refs_4_), channel_id=1, source_target_pairs={{0,224},{16,240},{32,0},{48,16},{64,32},{80,48},{96,64},{112,80},{... | collective-permute-start | bytes 221192 | tf_op jit(solution)/shard_map/ppermute | solution.py:302
  46.6 18.8 %copy-start.18 = (bf16[288,128]{1,0:T(8,128)(2,1)}, bf16[288,128]{1,0:T(8,128)(2,1)S(1)}, u32[]{:S(2)}) copy-start(bf16[288,128]{1,0:T(8,128)(2,1)S(1)} %collective-permute-done.7.refs_18_) | copy-start | bytes 221188
  46.6 5.8 %collective-permute-start.8 = (bf16[288,128]{1,0:T(8,128)(2,1)S(1)}, bf16[288,128]{1,0:T(8,128)(2,1)S(1)}, u32[]{:S(2)}, u32[]{:S(2)}) collective-permute-start(bf16[288,128]{1,0:T(8,128)(2,1)S(1)} %collective-permute-done.7.refs_18_), channel_id=1, source_target_pairs={{0,32},{16,48},{32,64},{48,80},{64,96},{80,112},{96,128},{112,144}... | collective-permute-start | bytes 221192 | tf_op jit(solution)/shard_map/ppermute | solution.py:301
  47.9 5.6 %collective-permute-start.12 = (bf16[288,128]{1,0:T(8,128)(2,1)S(1)}, bf16[288,128]{1,0:T(8,128)(2,1)S(1)}, u32[]{:S(2)}, u32[]{:S(2)}) collective-permute-start(bf16[288,128]{1,0:T(8,128)(2,1)S(1)} %collective-permute-done.refs_5_), channel_id=1, source_target_pairs={{0,32},{16,48},{32,64},{48,80},{64,96},{80,112},{96,128},{112,144}... | collective-permute-start | bytes 221192 | tf_op jit(solution)/shard_map/ppermute | solution.py:301
  47.9 17.5 %copy-start.19 = (bf16[288,128]{1,0:T(8,128)(2,1)}, bf16[288,128]{1,0:T(8,128)(2,1)S(1)}, u32[]{:S(2)}) copy-start(bf16[288,128]{1,0:T(8,128)(2,1)S(1)} %collective-permute-done.2.refs_7_) | copy-start | bytes 221188
  48.0 5.6 %collective-permute-start.4 = (bf16[288,128]{1,0:T(8,128)(2,1)S(1)}, bf16[288,128]{1,0:T(8,128)(2,1)S(1)}, u32[]{:S(2)}, u32[]{:S(2)}) collective-permute-start(bf16[288,128]{1,0:T(8,128)(2,1)S(1)} %collective-permute-done.2.refs_7_), channel_id=1, source_target_pairs={{0,224},{16,240},{32,0},{48,16},{64,32},{80,48},{96,64},{112,80},{... | collective-permute-start | bytes 221192 | tf_op jit(solution)/shard_map/ppermute | solution.py:302
  51.4 14.0 %copy-start.20 = (bf16[288,128]{1,0:T(8,128)(2,1)}, bf16[288,128]{1,0:T(8,128)(2,1)S(1)}, u32[]{:S(2)}) copy-start(bf16[288,128]{1,0:T(8,128)(2,1)S(1)} %collective-permute-done.1.refs_6_) | copy-start | bytes 221188
  51.4 5.6 %collective-permute-start.3 = (bf16[288,128]{1,0:T(8,128)(2,1)S(1)}, bf16[288,128]{1,0:T(8,128)(2,1)S(1)}, u32[]{:S(2)}, u32[]{:S(2)}) collective-permute-start(bf16[288,128]{1,0:T(8,128)(2,1)S(1)} %collective-permute-done.1.refs_6_), channel_id=1, source_target_pairs={{0,224},{16,240},{32,0},{48,16},{64,32},{80,48},{96,64},{112,80},{... | collective-permute-start | bytes 221192 | tf_op jit(solution)/shard_map/ppermute | solution.py:302
  52.4 13.1 %copy-start.21 = (bf16[288,128]{1,0:T(8,128)(2,1)}, bf16[288,128]{1,0:T(8,128)(2,1)S(1)}, u32[]{:S(2)}) copy-start(bf16[288,128]{1,0:T(8,128)(2,1)S(1)} %collective-permute-done.8.refs_16_) | copy-start | bytes 221188
  52.4 6.1 %collective-permute-start.9 = (bf16[288,128]{1,0:T(8,128)(2,1)S(1)}, bf16[288,128]{1,0:T(8,128)(2,1)S(1)}, u32[]{:S(2)}, u32[]{:S(2)}) collective-permute-start(bf16[288,128]{1,0:T(8,128)(2,1)S(1)} %collective-permute-done.8.refs_16_), channel_id=1, source_target_pairs={{0,32},{16,48},{32,64},{48,80},{64,96},{80,112},{96,128},{112,144}... | collective-permute-start | bytes 221192 | tf_op jit(solution)/shard_map/ppermute | solution.py:301
  53.4 12.0 %copy-start.22 = (bf16[288,128]{1,0:T(8,128)(2,1)}, bf16[288,128]{1,0:T(8,128)(2,1)S(1)}, u32[]{:S(2)}) copy-start(bf16[288,128]{1,0:T(8,128)(2,1)S(1)} %collective-permute-done.12.refs_19_) | copy-start | bytes 221188
  53.4 6.4 %collective-permute-start.13 = (bf16[288,128]{1,0:T(8,128)(2,1)S(1)}, bf16[288,128]{1,0:T(8,128)(2,1)S(1)}, u32[]{:S(2)}, u32[]{:S(2)}) collective-permute-start(bf16[288,128]{1,0:T(8,128)(2,1)S(1)} %collective-permute-done.12.refs_19_), channel_id=1, source_target_pairs={{0,32},{16,48},{32,64},{48,80},{64,96},{80,112},{96,128},{112,144}... | collective-permute-start | bytes 221192 | tf_op jit(solution)/shard_map/ppermute | solution.py:301
  53.5 11.9 %copy-start.23 = (bf16[288,128]{1,0:T(8,128)(2,1)}, bf16[288,128]{1,0:T(8,128)(2,1)S(1)}, u32[]{:S(2)}) copy-start(bf16[288,128]{1,0:T(8,128)(2,1)S(1)} %collective-permute-done.4.refs_9_) | copy-start | bytes 221188
  53.5 6.3 %collective-permute-start.6 = (bf16[288,128]{1,0:T(8,128)(2,1)S(1)}, bf16[288,128]{1,0:T(8,128)(2,1)S(1)}, u32[]{:S(2)}, u32[]{:S(2)}) collective-permute-start(bf16[288,128]{1,0:T(8,128)(2,1)S(1)} %collective-permute-done.4.refs_9_), channel_id=1, source_target_pairs={{0,224},{16,240},{32,0},{48,16},{64,32},{80,48},{96,64},{112,80},{... | collective-permute-start | bytes 221192 | tf_op jit(solution)/shard_map/ppermute | solution.py:302
  57.0 8.5 %copy-start.24 = (bf16[288,128]{1,0:T(8,128)(2,1)}, bf16[288,128]{1,0:T(8,128)(2,1)S(1)}, u32[]{:S(2)}) copy-start(bf16[288,128]{1,0:T(8,128)(2,1)S(1)} %collective-permute-done.3.refs_8_) | copy-start | bytes 221188
  57.0 6.6 %collective-permute-start.5 = (bf16[288,128]{1,0:T(8,128)(2,1)S(1)}, bf16[288,128]{1,0:T(8,128)(2,1)S(1)}, u32[]{:S(2)}, u32[]{:S(2)}) collective-permute-start(bf16[288,128]{1,0:T(8,128)(2,1)S(1)} %collective-permute-done.3.refs_8_), channel_id=1, source_target_pairs={{0,224},{16,240},{32,0},{48,16},{64,32},{80,48},{96,64},{112,80},{... | collective-permute-start | bytes 221192 | tf_op jit(solution)/shard_map/ppermute | solution.py:302
  58.4 7.0 %copy-start.25 = (bf16[288,128]{1,0:T(8,128)(2,1)}, bf16[288,128]{1,0:T(8,128)(2,1)S(1)}, u32[]{:S(2)}) copy-start(bf16[288,128]{1,0:T(8,128)(2,1)S(1)} %collective-permute-done.9.refs_14_) | copy-start | bytes 221188
  58.4 5.6 %collective-permute-start.10 = (bf16[288,128]{1,0:T(8,128)(2,1)S(1)}, bf16[288,128]{1,0:T(8,128)(2,1)S(1)}, u32[]{:S(2)}, u32[]{:S(2)}) collective-permute-start(bf16[288,128]{1,0:T(8,128)(2,1)S(1)} %collective-permute-done.9.refs_14_), channel_id=1, source_target_pairs={{0,32},{16,48},{32,64},{48,80},{64,96},{80,112},{96,128},{112,144}... | collective-permute-start | bytes 221192 | tf_op jit(solution)/shard_map/ppermute | solution.py:305
  59.8 5.7 %copy-start.26 = (bf16[288,128]{1,0:T(8,128)(2,1)}, bf16[288,128]{1,0:T(8,128)(2,1)S(1)}, u32[]{:S(2)}) copy-start(bf16[288,128]{1,0:T(8,128)(2,1)S(1)} %collective-permute-done.13.refs_17_) | copy-start | bytes 221188
  59.8 5.6 %collective-permute-start.14 = (bf16[288,128]{1,0:T(8,128)(2,1)S(1)}, bf16[288,128]{1,0:T(8,128)(2,1)S(1)}, u32[]{:S(2)}, u32[]{:S(2)}) collective-permute-start(bf16[288,128]{1,0:T(8,128)(2,1)S(1)} %collective-permute-done.13.refs_17_), channel_id=1, source_target_pairs={{0,32},{16,48},{32,64},{48,80},{64,96},{80,112},{96,128},{112,144}... | collective-permute-start | bytes 221192 | tf_op jit(solution)/shard_map/ppermute | solution.py:301
  59.8 5.7 %copy-start.27 = (bf16[288,128]{1,0:T(8,128)(2,1)}, bf16[288,128]{1,0:T(8,128)(2,1)S(1)}, u32[]{:S(2)}) copy-start(bf16[288,128]{1,0:T(8,128)(2,1)S(1)} %collective-permute-done.6.refs_11_) | copy-start | bytes 221188
  59.8 5.5 %collective-permute-start.11 = (bf16[288,128]{1,0:T(8,128)(2,1)S(1)}, bf16[288,128]{1,0:T(8,128)(2,1)S(1)}, u32[]{:S(2)}, u32[]{:S(2)}) collective-permute-start(bf16[288,128]{1,0:T(8,128)(2,1)S(1)} %collective-permute-done.6.refs_11_), channel_id=1, source_target_pairs={{0,224},{16,240},{32,0},{48,16},{64,32},{80,48},{96,64},{112,80},{... | collective-permute-start | bytes 221192 | tf_op jit(solution)/shard_map/ppermute | solution.py:306
  63.6 1.9 %copy-start.28 = (bf16[288,128]{1,0:T(8,128)(2,1)}, bf16[288,128]{1,0:T(8,128)(2,1)S(1)}, u32[]{:S(2)}) copy-start(bf16[288,128]{1,0:T(8,128)(2,1)S(1)} %collective-permute-done.5.refs_10_) | copy-start | bytes 221188
  86.2 11.2 %copy-start = (f32[8,480,128]{2,1,0:T(8,128)S(1)}, f32[8,480,128]{2,1,0:T(8,128)}, u32[]{:S(2)}) copy-start(f32[8,480,128]{2,1,0:T(8,128)} %get-tuple-element.23) | copy-start | bytes 5898244
  87.7 9.7 %collective-permute-start.18 = (bf16[2,480,128]{2,1,0:T(8,128)(2,1)S(1)}, bf16[2,480,128]{2,1,0:T(8,128)(2,1)S(1)}, u32[]{:S(2)}, u32[]{:S(2)}) collective-permute-start(bf16[2,480,128]{2,1,0:T(8,128)(2,1)S(1)} %get-tuple-element.42), channel_id=1, source_target_pairs={{0,16},{16,0},{32,48},{48,32},{64,80},{80,64},{96,112},{112,96},{1... | collective-permute-start | bytes 737288 | tf_op jit(solution)/shard_map/ppermute | solution.py:313
  88.7 12.6 %collective-permute-start.17 = (bf16[2,480,128]{2,1,0:T(8,128)(2,1)S(1)}, bf16[2,480,128]{2,1,0:T(8,128)(2,1)S(1)}, u32[]{:S(2)}, u32[]{:S(2)}) collective-permute-start(bf16[2,480,128]{2,1,0:T(8,128)(2,1)S(1)} %get-tuple-element.43), channel_id=1, source_target_pairs={{0,16},{16,0},{32,48},{48,32},{64,80},{80,64},{96,112},{112,96},{1... | collective-permute-start | bytes 737288 | tf_op jit(solution)/shard_map/ppermute | solution.py:313
  97.5 7.5 %collective-permute-start.19 = (bf16[2,480,128]{2,1,0:T(8,128)(2,1)S(1)}, bf16[2,480,128]{2,1,0:T(8,128)(2,1)S(1)}, u32[]{:S(2)}, u32[]{:S(2)}) collective-permute-start(bf16[2,480,128]{2,1,0:T(8,128)(2,1)S(1)} %pad_maximum_fusion), channel_id=1, source_target_pairs={{0,224},{1,33},{2,226},{3,35},{4,228},{5,37},{6,230},{7,39},{8,232... | collective-permute-start | bytes 737288 | tf_op jit(solution)/shard_map/ppermute | solution.py:321
  100.5 7.7 %collective-permute-start.16 = (bf16[2,480,128]{2,1,0:T(8,128)(2,1)S(1)}, bf16[2,480,128]{2,1,0:T(8,128)(2,1)S(1)}, u32[]{:S(2)}, u32[]{:S(2)}) collective-permute-start(bf16[2,480,128]{2,1,0:T(8,128)(2,1)S(1)} %get-tuple-element.41), channel_id=1, source_target_pairs={{0,16},{16,0},{32,48},{48,32},{64,80},{80,64},{96,112},{112,96},{1... | collective-permute-start | bytes 737288 | tf_op jit(solution)/shard_map/ppermute | solution.py:313
  105.1 6.3 %collective-permute-start.20 = (bf16[2,480,128]{2,1,0:T(8,128)(2,1)S(1)}, bf16[2,480,128]{2,1,0:T(8,128)(2,1)S(1)}, u32[]{:S(2)}, u32[]{:S(2)}) collective-permute-start(bf16[2,480,128]{2,1,0:T(8,128)(2,1)S(1)} %pad_maximum_fusion.1), channel_id=1, source_target_pairs={{0,32},{1,225},{2,34},{3,227},{4,36},{5,229},{6,38},{7,231},{8,40}... | collective-permute-start | bytes 737288 | tf_op jit(solution)/shard_map/ppermute | solution.py:322
  105.2 9.4 %collective-permute-start.15 = (bf16[2,480,128]{2,1,0:T(8,128)(2,1)S(1)}, bf16[2,480,128]{2,1,0:T(8,128)(2,1)S(1)}, u32[]{:S(2)}, u32[]{:S(2)}) collective-permute-start(bf16[2,480,128]{2,1,0:T(8,128)(2,1)S(1)} %get-tuple-element.44), channel_id=1, source_target_pairs={{0,16},{16,0},{32,48},{48,32},{64,80},{80,64},{96,112},{112,96},{1... | collective-permute-start | bytes 737288 | tf_op jit(solution)/shard_map/ppermute | solution.py:313
  111.5 7.5 %collective-permute-start.21 = (bf16[2,480,128]{2,1,0:T(8,128)(2,1)S(1)}, bf16[2,480,128]{2,1,0:T(8,128)(2,1)S(1)}, u32[]{:S(2)}, u32[]{:S(2)}) collective-permute-start(bf16[2,480,128]{2,1,0:T(8,128)(2,1)S(1)} %pad_maximum_fusion.2), channel_id=1, source_target_pairs={{0,224},{1,33},{2,226},{3,35},{4,228},{5,37},{6,230},{7,39},{8,232... | collective-permute-start | bytes 737288 | tf_op jit(solution)/shard_map/ppermute | solution.py:323
  119.8 4.9 %collective-permute-start.22 = (bf16[480,128]{1,0:T(8,128)(2,1)S(1)}, bf16[480,128]{1,0:T(8,128)(2,1)S(1)}, u32[]{:S(2)}, u32[]{:S(2)}) collective-permute-start(bf16[480,128]{1,0:T(8,128)(2,1)S(1)} %get-tuple-element.39), channel_id=1, source_target_pairs={{0,32},{1,225},{2,34},{3,227},{4,36},{5,229},{6,38},{7,231},{8,40}... | collective-permute-start | bytes 368648 | tf_op jit(solution)/shard_map/ppermute | solution.py:324
  128.0 6.1 %collective-permute-start.23 = (bf16[288,128]{1,0:T(8,128)(2,1)}, bf16[288,128]{1,0:T(8,128)(2,1)S(1)}, u32[]{:S(2)}, u32[]{:S(2)}) collective-permute-start(bf16[288,128]{1,0:T(8,128)(2,1)} %get-tuple-element.32.refs_2_), channel_id=1, source_target_pairs={{0,16},{16,0},{32,48},{48,32},{64,80},{80,64},{96,112},{112,96},{1... | collective-permute-start | bytes 221192 | tf_op jit(solution)/shard_map/ppermute | solution.py:295
  129.8 7.3 %collective-permute-start.30 = (bf16[288,128]{1,0:T(8,128)(2,1)}, bf16[288,128]{1,0:T(8,128)(2,1)S(1)}, u32[]{:S(2)}, u32[]{:S(2)}) collective-permute-start(bf16[288,128]{1,0:T(8,128)(2,1)} %get-tuple-element.32.refs_2_), channel_id=1, source_target_pairs={{0,32},{16,48},{32,64},{48,80},{64,96},{80,112},{96,128},{112,144}... | collective-permute-start | bytes 221192 | tf_op jit(solution)/shard_map/ppermute | solution.py:301
  134.1 21.8 %copy-start.2 = (bf16[288,128]{1,0:T(8,128)(2,1)}, bf16[288,128]{1,0:T(8,128)(2,1)S(1)}, u32[]{:S(2)}) copy-start(bf16[288,128]{1,0:T(8,128)(2,1)S(1)} %collective-permute-done.23.refs_3_) | copy-start | bytes 221188
  134.1 5.1 %collective-permute-start.25 = (bf16[288,128]{1,0:T(8,128)(2,1)S(1)}, bf16[288,128]{1,0:T(8,128)(2,1)S(1)}, u32[]{:S(2)}, u32[]{:S(2)}) collective-permute-start(bf16[288,128]{1,0:T(8,128)(2,1)S(1)} %collective-permute-done.23.refs_3_), channel_id=1, source_target_pairs={{0,224},{16,240},{32,0},{48,16},{64,32},{80,48},{96,64},{112,80},{... | collective-permute-start | bytes 221192 | tf_op jit(solution)/shard_map/ppermute | solution.py:302
  137.1 5.7 %collective-permute-start.24 = (bf16[288,128]{1,0:T(8,128)(2,1)}, bf16[288,128]{1,0:T(8,128)(2,1)S(1)}, u32[]{:S(2)}, u32[]{:S(2)}) collective-permute-start(bf16[288,128]{1,0:T(8,128)(2,1)} %get-tuple-element.32.refs_2_), channel_id=1, source_target_pairs={{0,224},{16,240},{32,0},{48,16},{64,32},{80,48},{96,64},{112,80},{... | collective-permute-start | bytes 221192 | tf_op jit(solution)/shard_map/ppermute | solution.py:302
  137.1 18.8 %copy-start.3 = (bf16[288,128]{1,0:T(8,128)(2,1)}, bf16[288,128]{1,0:T(8,128)(2,1)S(1)}, u32[]{:S(2)}) copy-start(bf16[288,128]{1,0:T(8,128)(2,1)S(1)} %collective-permute-done.30.refs_16_) | copy-start | bytes 221188
  137.1 6.4 %collective-permute-start.31 = (bf16[288,128]{1,0:T(8,128)(2,1)S(1)}, bf16[288,128]{1,0:T(8,128)(2,1)S(1)}, u32[]{:S(2)}, u32[]{:S(2)}) collective-permute-start(bf16[288,128]{1,0:T(8,128)(2,1)S(1)} %collective-permute-done.30.refs_16_), channel_id=1, source_target_pairs={{0,32},{16,48},{32,64},{48,80},{64,96},{80,112},{96,128},{112,144}... | collective-permute-start | bytes 221192 | tf_op jit(solution)/shard_map/ppermute | solution.py:301
  139.1 5.7 %collective-permute-start.35 = (bf16[288,128]{1,0:T(8,128)(2,1)S(1)}, bf16[288,128]{1,0:T(8,128)(2,1)S(1)}, u32[]{:S(2)}, u32[]{:S(2)}) collective-permute-start(bf16[288,128]{1,0:T(8,128)(2,1)S(1)} %collective-permute-done.23.refs_3_), channel_id=1, source_target_pairs={{0,32},{16,48},{32,64},{48,80},{64,96},{80,112},{96,128},{112,144}... | collective-permute-start | bytes 221192 | tf_op jit(solution)/shard_map/ppermute | solution.py:301
  139.2 16.8 %copy-start.4 = (bf16[288,128]{1,0:T(8,128)(2,1)}, bf16[288,128]{1,0:T(8,128)(2,1)S(1)}, u32[]{:S(2)}) copy-start(bf16[288,128]{1,0:T(8,128)(2,1)S(1)} %collective-permute-done.25.refs_5_) | copy-start | bytes 221188
  139.2 5.7 %collective-permute-start.27 = (bf16[288,128]{1,0:T(8,128)(2,1)S(1)}, bf16[288,128]{1,0:T(8,128)(2,1)S(1)}, u32[]{:S(2)}, u32[]{:S(2)}) collective-permute-start(bf16[288,128]{1,0:T(8,128)(2,1)S(1)} %collective-permute-done.25.refs_5_), channel_id=1, source_target_pairs={{0,224},{16,240},{32,0},{48,16},{64,32},{80,48},{96,64},{112,80},{... | collective-permute-start | bytes 221192 | tf_op jit(solution)/shard_map/ppermute | solution.py:302
  142.8 13.2 %copy-start.5 = (bf16[288,128]{1,0:T(8,128)(2,1)}, bf16[288,128]{1,0:T(8,128)(2,1)S(1)}, u32[]{:S(2)}) copy-start(bf16[288,128]{1,0:T(8,128)(2,1)S(1)} %collective-permute-done.24.refs_4_) | copy-start | bytes 221188
  142.8 5.6 %collective-permute-start.26 = (bf16[288,128]{1,0:T(8,128)(2,1)S(1)}, bf16[288,128]{1,0:T(8,128)(2,1)S(1)}, u32[]{:S(2)}, u32[]{:S(2)}) collective-permute-start(bf16[288,128]{1,0:T(8,128)(2,1)S(1)} %collective-permute-done.24.refs_4_), channel_id=1, source_target_pairs={{0,224},{16,240},{32,0},{48,16},{64,32},{80,48},{96,64},{112,80},{... | collective-permute-start | bytes 221192 | tf_op jit(solution)/shard_map/ppermute | solution.py:302
  143.5 12.4 %copy-start.6 = (bf16[288,128]{1,0:T(8,128)(2,1)}, bf16[288,128]{1,0:T(8,128)(2,1)S(1)}, u32[]{:S(2)}) copy-start(bf16[288,128]{1,0:T(8,128)(2,1)S(1)} %collective-permute-done.31.refs_14_) | copy-start | bytes 221188
  143.5 5.6 %collective-permute-start.32 = (bf16[288,128]{1,0:T(8,128)(2,1)S(1)}, bf16[288,128]{1,0:T(8,128)(2,1)S(1)}, u32[]{:S(2)}, u32[]{:S(2)}) collective-permute-start(bf16[288,128]{1,0:T(8,128)(2,1)S(1)} %collective-permute-done.31.refs_14_), channel_id=1, source_target_pairs={{0,32},{16,48},{32,64},{48,80},{64,96},{80,112},{96,128},{112,144}... | collective-permute-start | bytes 221192 | tf_op jit(solution)/shard_map/ppermute | solution.py:301
  144.8 11.2 %copy-start.7 = (bf16[288,128]{1,0:T(8,128)(2,1)}, bf16[288,128]{1,0:T(8,128)(2,1)S(1)}, u32[]{:S(2)}) copy-start(bf16[288,128]{1,0:T(8,128)(2,1)S(1)} %collective-permute-done.35.refs_17_) | copy-start | bytes 221188
  144.8 5.6 %collective-permute-start.36 = (bf16[288,128]{1,0:T(8,128)(2,1)S(1)}, bf16[288,128]{1,0:T(8,128)(2,1)S(1)}, u32[]{:S(2)}, u32[]{:S(2)}) collective-permute-start(bf16[288,128]{1,0:T(8,128)(2,1)S(1)} %collective-permute-done.35.refs_17_), channel_id=1, source_target_pairs={{0,32},{16,48},{32,64},{48,80},{64,96},{80,112},{96,128},{112,144}... | collective-permute-start | bytes 221192 | tf_op jit(solution)/shard_map/ppermute | solution.py:301
  144.9 11.1 %copy-start.8 = (bf16[288,128]{1,0:T(8,128)(2,1)}, bf16[288,128]{1,0:T(8,128)(2,1)S(1)}, u32[]{:S(2)}) copy-start(bf16[288,128]{1,0:T(8,128)(2,1)S(1)} %collective-permute-done.27.refs_7_) | copy-start | bytes 221188
  144.9 5.6 %collective-permute-start.29 = (bf16[288,128]{1,0:T(8,128)(2,1)S(1)}, bf16[288,128]{1,0:T(8,128)(2,1)S(1)}, u32[]{:S(2)}, u32[]{:S(2)}) collective-permute-start(bf16[288,128]{1,0:T(8,128)(2,1)S(1)} %collective-permute-done.27.refs_7_), channel_id=1, source_target_pairs={{0,224},{16,240},{32,0},{48,16},{64,32},{80,48},{96,64},{112,80},{... | collective-permute-start | bytes 221192 | tf_op jit(solution)/shard_map/ppermute | solution.py:302
  148.3 7.7 %copy-start.9 = (bf16[288,128]{1,0:T(8,128)(2,1)}, bf16[288,128]{1,0:T(8,128)(2,1)S(1)}, u32[]{:S(2)}) copy-start(bf16[288,128]{1,0:T(8,128)(2,1)S(1)} %collective-permute-done.26.refs_6_) | copy-start | bytes 221188
  148.3 5.6 %collective-permute-start.28 = (bf16[288,128]{1,0:T(8,128)(2,1)S(1)}, bf16[288,128]{1,0:T(8,128)(2,1)S(1)}, u32[]{:S(2)}, u32[]{:S(2)}) collective-permute-start(bf16[288,128]{1,0:T(8,128)(2,1)S(1)} %collective-permute-done.26.refs_6_), channel_id=1, source_target_pairs={{0,224},{16,240},{32,0},{48,16},{64,32},{80,48},{96,64},{112,80},{... | collective-permute-start | bytes 221192 | tf_op jit(solution)/shard_map/ppermute | solution.py:302
  149.1 6.9 %copy-start.10 = (bf16[288,128]{1,0:T(8,128)(2,1)}, bf16[288,128]{1,0:T(8,128)(2,1)S(1)}, u32[]{:S(2)}) copy-start(bf16[288,128]{1,0:T(8,128)(2,1)S(1)} %collective-permute-done.32.refs_12_) | copy-start | bytes 221188
  149.1 5.6 %collective-permute-start.33 = (bf16[288,128]{1,0:T(8,128)(2,1)S(1)}, bf16[288,128]{1,0:T(8,128)(2,1)S(1)}, u32[]{:S(2)}, u32[]{:S(2)}) collective-permute-start(bf16[288,128]{1,0:T(8,128)(2,1)S(1)} %collective-permute-done.32.refs_12_), channel_id=1, source_target_pairs={{0,32},{16,48},{32,64},{48,80},{64,96},{80,112},{96,128},{112,144}... | collective-permute-start | bytes 221192 | tf_op jit(solution)/shard_map/ppermute | solution.py:305
  150.4 5.7 %copy-start.11 = (bf16[288,128]{1,0:T(8,128)(2,1)}, bf16[288,128]{1,0:T(8,128)(2,1)S(1)}, u32[]{:S(2)}) copy-start(bf16[288,128]{1,0:T(8,128)(2,1)S(1)} %collective-permute-done.36.refs_15_) | copy-start | bytes 221188
  150.4 5.6 %collective-permute-start.37 = (bf16[288,128]{1,0:T(8,128)(2,1)S(1)}, bf16[288,128]{1,0:T(8,128)(2,1)S(1)}, u32[]{:S(2)}, u32[]{:S(2)}) collective-permute-start(bf16[288,128]{1,0:T(8,128)(2,1)S(1)} %collective-permute-done.36.refs_15_), channel_id=1, source_target_pairs={{0,32},{16,48},{32,64},{48,80},{64,96},{80,112},{96,128},{112,144}... | collective-permute-start | bytes 221192 | tf_op jit(solution)/shard_map/ppermute | solution.py:301
  150.5 5.6 %copy-start.12 = (bf16[288,128]{1,0:T(8,128)(2,1)}, bf16[288,128]{1,0:T(8,128)(2,1)S(1)}, u32[]{:S(2)}) copy-start(bf16[288,128]{1,0:T(8,128)(2,1)S(1)} %collective-permute-done.29.refs_9_) | copy-start | bytes 221188
  150.5 5.5 %collective-permute-start.34 = (bf16[288,128]{1,0:T(8,128)(2,1)S(1)}, bf16[288,128]{1,0:T(8,128)(2,1)S(1)}, u32[]{:S(2)}, u32[]{:S(2)}) collective-permute-start(bf16[288,128]{1,0:T(8,128)(2,1)S(1)} %collective-permute-done.29.refs_9_), channel_id=1, source_target_pairs={{0,224},{16,240},{32,0},{48,16},{64,32},{80,48},{96,64},{112,80},{... | collective-permute-start | bytes 221192 | tf_op jit(solution)/shard_map/ppermute | solution.py:306
  153.9 2.2 %copy-start.13 = (bf16[288,128]{1,0:T(8,128)(2,1)}, bf16[288,128]{1,0:T(8,128)(2,1)S(1)}, u32[]{:S(2)}) copy-start(bf16[288,128]{1,0:T(8,128)(2,1)S(1)} %collective-permute-done.28.refs_8_) | copy-start | bytes 221188
  (7 other events, 6.1 us)
Sparse Core Ops, SparseCore 0:
  9.8 48.6 all-gather.2
where the time goes:
time: 171 us; the launch traced here: 168 us
  starting transfers between devices  61.2 us (36%)
  waiting for transfers between devices  36 us (21%)
  Pallas kernels  32.7 us (19%)
  blocking collectives  16.5 us (10%)
  between operations  14.4 us (8%)
  local copies, waits for them, and re-layouts  5.2 us (3%)
    ppermute x12, starting transfers between devices, gather_pieces(): down[j] = lax.ppermute(down[j], 'dp', DOWN)  29 us
    pallas_call x1, Pallas kernels, local(): pl.pallas_call(main_kernel, out_shape=(sd((tokens_here, COLS * B), BF16),...  20.2 us
    all_to_all x1, blocking collectives, local(): lax.all_to_all(packed, 'tensor', split_axis=0, concat_axis=0, tiled=True)  16.5 us
    ppermute x2, waiting for transfers between devices, gather_pieces(): swapped = lax.ppermute(shard, 'dp', SWAP)  8.71 us
    ppermute x12, starting transfers between devices, gather_pieces(): up[j] = lax.ppermute(up[j], 'dp', UP)  7.63 us
    ppermute x4, waiting for transfers between devices, reduce_chunks(): got = lax.ppermute(send[group[0]:group[1] + 1], 'dp', SWAP)  7.32 us
    ppermute x2, starting transfers between devices, gather_pieces(): pieces[4][1] = lax.ppermute(down[1], 'dp', DOWN)  6.64 us
    ppermute x4, starting transfers between devices, reduce_chunks(): got = lax.ppermute(send[group[0]:group[1] + 1], 'dp', SWAP)  6.16 us
  transfers between devices with their start and end apart: 39, of which 13 were waited for; matrix products, arithmetic and copies ran while one was open for 1% of the time, Pallas kernels for 4%

commit v1 on v0

--- a/solution.py
+++ b/solution.py
@@ -27,13 +27,24 @@
 ZN = 8
 F32 = jnp.float32
 BF16 = jnp.bfloat16
-PARAMS = pltpu.CompilerParams(vmem_limit_bytes=56 * 1024 * 1024)
+
+
+def params(mib):
+    return pltpu.CompilerParams(vmem_limit_bytes=mib * 1024 * 1024)
+
+Y_ORDER = ((0,), (1,), (-1, -2))
+
+ORDER = (5, 4, 2, 3, 7, 6, 0, 1)
 
 SEND, PLACE, BROW, BCOL, LIST, RANK = range(6)
 
 
 def vmem():
     return pl.BlockSpec(memory_space=pltpu.VMEM)
+
+
+def hbm():
+    return pl.BlockSpec(memory_space=pltpu.HBM)
 
 
 def smem():
@@ -111,7 +122,7 @@
 
 
 def pack_kernel(
-    me_ref, old_ref, new_ref, cols_ref, master_ref, first_ref, second_ref, table_ref, out_ref, scalars, sem
+    me_ref, old_ref, new_ref, cols_ref, master_ref, first_ref, second_ref, table_ref, out_ref, moments_ref, scalars, sem
 ):
     rows = routing_table(me_ref[0], old_ref, new_ref, cols_ref)
     for i, row in enumerate(rows):
@@ -125,41 +136,50 @@
         slot = scalars[SEND, q]
         at = jnp.minimum(slot, SLOTS - 1)
         some = (jnp.zeros((ROWS, B), jnp.int32) + slot) < SLOTS
-        for state, ref in enumerate((master_ref, first_ref, second_ref)):
-            out_ref[q, state] = jnp.where(some, ref[at], 0.0)
+        out_ref[q] = jnp.where(some, master_ref[at], 0.0)
+        for state, ref in enumerate((first_ref, second_ref)):
+            moments_ref[q, state] = jnp.where(some, ref[at], 0.0)
         return carry
 
     lax.fori_loop(0, OWNERS * KEEP, step, 0, unroll=8)
 
 
+def place_tile(table_ref, slot, ref, arrived):
+    index = table_ref[PLACE, slot]
+    tag = jnp.zeros((ROWS, B), jnp.int32) + index
+    here = ref[jnp.minimum(index, SLOTS - 1)]
+    there = arrived(jnp.maximum(index - SLOTS - 1, 0))
+    return jnp.where(tag < SLOTS, here, there), tag != SLOTS
+
+
+def copy_in_kernel(table_ref, master_in, arrived_ref, copy_ref, scratch):
+    def step(i, carry):
+        tile, _ = place_tile(table_ref, table_ref[LIST, i], master_in, lambda at: arrived_ref[at])
+        scratch[pl.ds(pl.multiple_of(i * ROWS, ROWS), ROWS), :] = tile
+        return carry
+
+    lax.fori_loop(0, KEPT, step, 0, unroll=12)
+    for i in range(2 * ZN):
+        copy_ref[i] = scratch[...].astype(BF16)
+
+
 def place_kernel(
-    table_ref, master_in, first_in, second_in, arrived_ref,
-    copy_ref, master_ref, first_ref, second_ref, mask_ref, scratch,
+    table_ref, master_in, first_in, second_in, arrived_ref, moments_ref,
+    master_ref, first_ref, second_ref, mask_ref,
 ):
     def step(s, carry):
-        index = table_ref[PLACE, s]
-        here = jnp.minimum(index, SLOTS - 1)
-        there = jnp.maximum(index - SLOTS - 1, 0)
-        tag = jnp.zeros((ROWS, B), jnp.int32) + index
-        kept = tag != SLOTS
         at = pl.ds(pl.multiple_of(s * ROWS, ROWS), ROWS)
-        for state, (ref, out) in enumerate(
-            ((master_in, master_ref), (first_in, first_ref), (second_in, second_ref))
+        for ref, out, arrived in (
+            (master_in, master_ref, lambda q: arrived_ref[q]),
+            (first_in, first_ref, lambda q: moments_ref[q, 0]),
+            (second_in, second_ref, lambda q: moments_ref[q, 1]),
         ):
-            tile = jnp.where(tag < SLOTS, ref[here], arrived_ref[there, state])
+            tile, kept = place_tile(table_ref, s, ref, arrived)
             out[at, :] = jnp.where(kept, tile, 0.0)
         mask_ref[at, :] = jnp.where(kept, 1.0, 0.0)
         return carry
 
-    lax.fori_loop(0, SLOTS, step, 0, unroll=6)
-
-    def pick(i, carry):
-        at = pl.ds(pl.multiple_of(table_ref[LIST, i] * ROWS, ROWS), ROWS)
-        scratch[pl.ds(pl.multiple_of(i * ROWS, ROWS), ROWS), :] = master_ref[at, :]
-        return carry
-
-    lax.fori_loop(0, KEPT, pick, 0, unroll=6)
-    copy_ref[...] = scratch[...].astype(BF16)
+    lax.fori_loop(0, SLOTS, step, 0, unroll=10)
 
 
 def assemble(pieces, z, xh, weights):
@@ -170,15 +190,42 @@
         weights[:, at, :] = piece[...].astype(F32).reshape(KEPT, ROWS, B)
 
 
+def assemble_kernel(shards_ref, out_ref, weights):
+    for i in range(2 * ZN):
+        weights[:, i * ROWS : (i + 1) * ROWS, :] = shards_ref[i].astype(F32).reshape(KEPT, ROWS, B)
+    out_ref[...] = weights[...].astype(BF16)
+
+
 def main_kernel(*refs):
-    table_ref, where_ref, tokens_ref, upstream_ref = refs[:4]
-    pieces = refs[4:20]
-    hidden_ref, keep_ref, send_ref = refs[20:23]
-    weights, local_grad, grads = refs[23:]
-    z = where_ref[0]
-    xh = where_ref[1]
-    sign = where_ref[2]
-    assemble(pieces, z, xh, weights)
+    table_ref, where_ref, upstream_in, weights_in = refs[:4]
+    token_pieces = refs[4:10]
+    hidden_out = refs[10]
+    keep_out = refs[11:15]
+    send_out = refs[15:18]
+    (
+        tokens_ref, upstream_ref, weights, hidden_ref, local_grad, grads, keep_ref, send_ref,
+        token_sems, side_sems, out_sems,
+    ) = refs[18:]
+    z, xh, sign = where_ref[0], where_ref[1], where_ref[2]
+    y, xl, core, y_sign = where_ref[3], where_ref[4], where_ref[5], where_ref[6]
+    copies = []
+    for index, ref in enumerate(token_pieces):
+        other_core, step = divmod(index, 3)
+        for i, rel in enumerate(Y_ORDER[step]):
+            y_from = lax.rem(y + (1 - 2 * other_core) * y_sign * rel + 4, 4)
+            for other_x in range(2):
+                owner = (y_from * 2 + lax.rem(xl + other_x, 2)) * 2 + lax.rem(core + other_core, 2)
+                copies.append(
+                    pltpu.make_async_copy(
+                        ref.at[2 * i + other_x], tokens_ref.at[owner], token_sems.at[len(copies)]
+                    )
+                )
+    copies.append(pltpu.make_async_copy(weights_in, weights, side_sems.at[0]))
+    copies.append(pltpu.make_async_copy(upstream_in, upstream_ref, side_sems.at[1]))
+    for copy in copies:
+        copy.start()
+    for copy in copies:
+        copy.wait()
 
     def block(row):
         lanes = pl.ds(pl.multiple_of(lax.rem(row, 3) * B, B), B)
@@ -186,7 +233,7 @@
 
     def forward(k, carry):
         xs = [block(table_ref[BROW, table_ref[LIST, k * KEEP + j]]) for j in range(KEEP)]
-        w = jnp.concatenate([weights[k * KEEP + j] for j in range(KEEP)], axis=0).astype(BF16)
+        w = jnp.concatenate([weights[k * KEEP + j] for j in range(KEEP)], axis=0)
         total = jnp.dot(jnp.concatenate(xs, axis=1), w, preferred_element_type=F32)
         lanes = pl.ds(pl.multiple_of(k * B, B), B)
         square = total * total
@@ -199,7 +246,9 @@
         local_grad[k] = (upstream_ref[:, lanes].astype(F32) * slope).astype(BF16)
         return carry
 
-    lax.fori_loop(0, COLS, forward, 0)
+    lax.fori_loop(0, COLS, forward, 0, unroll=4)
+    hidden_copy = pltpu.make_async_copy(hidden_ref, hidden_out, side_sems.at[2])
+    hidden_copy.start()
 
     def backward(p, carry):
         for half in range(2):
@@ -218,19 +267,48 @@
                 b = grads[pl.ds(pl.multiple_of(start + B, ROWS), ROWS), :]
                 return jnp.concatenate([a, b], axis=0)
 
-            keep_ref[rel, at, :] = pair(base + xh * ROWS)
-            send_ref[rel, at, :] = pair(base + (1 - xh) * ROWS).astype(BF16)
-        return carry
-
-    lax.fori_loop(0, SLOTS // 2, backward, 0)
+            spot = ORDER.index(rel)
+            keep_ref[spot, at, :] = pair(base + xh * ROWS)
+            send_ref[spot, at, :] = pair(base + (1 - xh) * ROWS).astype(BF16)
+        return carry
+
+    third = SLOTS // 2 // 3
+
+    def results(part):
+        at = pl.ds(pl.multiple_of(part * third * 16, 16), third * 16)
+        out = []
+        for group in range(4):
+            pair = pl.ds(2 * group, 2)
+            out.append((keep_ref.at[pair, at, :], keep_out[group].at[:, at, :]))
+            spot = pl.ds(2 if group == 3 else 0, 2)
+            out.append((send_ref.at[pair, at, :], send_out[min(group, 2)].at[spot, at, :]))
+        return [
+            pltpu.make_async_copy(a, b, out_sems.at[part, i]) for i, (a, b) in enumerate(out)
+        ]
+
+    def chunk(part, carry):
+        lax.fori_loop(0, third, lambda p, c: backward(part * third + p, c), 0, unroll=10)
+        for copy in results(part):
+            copy.start()
+        return carry
+
+    lax.fori_loop(0, 3, chunk, 0)
+    hidden_copy.wait()
+
+    def finish(part, carry):
+        for copy in results(part):
+            copy.wait()
+        return carry
+
+    lax.fori_loop(0, 3, finish, 0)
 
 
 def adam_kernel(
     table_ref, own_ref, got_ref, near_ref, last_ref, mast_ref, mom_ref, var_ref, mask_ref,
     master_ref, first_ref, second_ref, copy_ref, scratch,
 ):
-    grad = own_ref[...] + got_ref[...].astype(F32)
-    grad = grad + near_ref[...].astype(F32) + last_ref[...].astype(F32)
+    grad = own_ref[0] + got_ref[0].astype(F32)
+    grad = grad + near_ref[0].astype(F32) + last_ref[...].astype(F32)
     master = mast_ref[...]
     kept = mask_ref[...] > 0.5
     new_first = beta_one * mom_ref[...] + (1.0 - beta_one) * grad
@@ -300,6 +378,7 @@
         for j in range(2):
             up[j] = lax.ppermute(up[j], "dp", UP)
             down[j] = lax.ppermute(down[j], "dp", DOWN)
+        for j in range(2):
             pieces[ZN - step][j] = up[j]
             pieces[step][j] = down[j]
     pieces[4][0] = lax.ppermute(up[0], "dp", UP)
@@ -307,22 +386,37 @@
     return [piece for pair in pieces for piece in pair]
 
 
+def y_exchange(side):
+    out = []
+    for y, xl, core in itertools.product(range(4), range(2), range(2)):
+        other = (y + side * direction(y, core)) % 4
+        out.append(((y * 2 + xl) * 2 + core, (other * 2 + xl) * 2 + core))
+    return out
+
+
+Y_NEAR = y_exchange(1)
+Y_FAR = y_exchange(-1)
+X_SWAP = [(i, i ^ 2) for i in range(16)]
+CORE_SWAP = [(i, i ^ 1) for i in range(16)]
+
+
+def hop(value, pairs):
+    return lax.ppermute(value, "tensor", pairs)
+
+
 def reduce_chunks(keep, send):
-    joined = {}
-    for group in ((4, 5), (2, 3), (6, 7), (0, 1)):
-        got = lax.ppermute(send[group[0] : group[1] + 1], "dp", SWAP)
-        for i, rel in enumerate(group):
-            joined[rel] = (keep[rel], got[i])
-
-    def total(rel, more=None):
-        value = joined[rel][0] + joined[rel][1].astype(F32)
+    got = [lax.ppermute(a, "dp", SWAP) for a in send]
+    got = got[:2] + [got[2][:2], got[2][2:]]
+
+    def total(pair, more=None):
+        value = keep[pair] + got[pair].astype(F32)
         return (value if more is None else value + more.astype(F32)).astype(BF16)
 
-    a = lax.ppermute(jnp.stack([total(5), total(4)]), AXES, FAR)
-    b = lax.ppermute(jnp.stack([total(2, a[0]), total(3, a[1])]), AXES, NEAR)
-    c = lax.ppermute(jnp.stack([total(7, b[0]), total(6, b[1])]), AXES, FAR)
-    d = lax.ppermute(total(1, c[1]), AXES, NEAR)
-    return joined[0][0], joined[0][1], c[0], d
+    a = lax.ppermute(total(0), AXES, FAR)
+    b = lax.ppermute(total(1, a), AXES, NEAR)
+    c = lax.ppermute(total(2, b), AXES, FAR)
+    d = lax.ppermute(total(3, c)[1], AXES, NEAR)
+    return keep[3], got[3], c, d
 
 
 def local(tokens, upstream, master_weights, first_moment, second_moment, old_blocks, new_blocks, new_columns):
@@ -330,52 +424,94 @@
     dp = lax.axis_index("dp")
     z = dp // 2
     me = jnp.reshape(owner, (1,)).astype(jnp.int32)
-    where = jnp.stack([z, dp % 2, direction(z, owner % 2)]).astype(jnp.int32)
+    core = owner % 2
+    y = owner // 4
+    spots = [z, dp % 2, direction(z, core), y, owner // 2 % 2, core, direction(y, core)]
+    where = jnp.stack(spots).astype(jnp.int32)
     states = [jnp.transpose(a, (1, 0, 2)) for a in (master_weights, first_moment, second_moment)]
 
-    gathered = lax.all_gather(tokens, "tensor", axis=0)
-
-    table, packed = pl.pallas_call(
+    swapped = hop(tokens, X_SWAP)
+
+    table, packed, packed_moments = pl.pallas_call(
         pack_kernel,
-        out_shape=(sd((8, 128), jnp.int32), sd((OWNERS * KEEP, 3, ROWS, B), F32)),
+        out_shape=(
+            sd((8, 128), jnp.int32),
+            sd((OWNERS * KEEP, ROWS, B), F32),
+            sd((OWNERS * KEEP, 2, ROWS, B), F32),
+        ),
         in_specs=[smem()] + [vmem()] * 6,
-        out_specs=(vmem(),) * 2,
+        out_specs=(vmem(),) * 3,
         scratch_shapes=[pltpu.SMEM((8, 128), jnp.int32), pltpu.SemaphoreType.DMA],
-        compiler_params=PARAMS,
+        compiler_params=params(56),
     )(me, old_blocks, new_blocks, new_columns, *states)
     arrived = lax.all_to_all(packed, "tensor", split_axis=0, concat_axis=0, tiled=True)
 
+    arrived, swapped = lax.optimization_barrier((arrived, swapped))
+    start = jnp.stack([tokens, swapped])
+    near = hop(start, Y_NEAR)
     flat = sd((SLOTS * ROWS, B), F32)
     flat16 = sd((KEPT * ROWS, B), BF16)
-    copy_in, kept_master, kept_first, kept_second, mask = pl.pallas_call(
+    copies = pl.pallas_call(
+        copy_in_kernel,
+        out_shape=sd((2 * ZN, KEPT * ROWS, B), BF16),
+        in_specs=[smem()] + [vmem()] * 2,
+        out_specs=vmem(),
+        scratch_shapes=[pltpu.VMEM((KEPT * ROWS, B), F32)],
+        compiler_params=params(6),
+    )(table, states[0], arrived)
+    shards = lax.all_to_all(copies, "dp", split_axis=0, concat_axis=0, tiled=True)
+
+    def after(value, other):
+        return lax.optimization_barrier((value, other))[0]
+
+    far = hop(jnp.concatenate([start, near], axis=0), Y_FAR)
+    mine = [start, near, after(far, shards)]
+    token_pieces = mine + [hop(a, CORE_SWAP) for a in mine]
+
+    weights = pl.pallas_call(
+        assemble_kernel,
+        out_shape=sd((KEPT, B, B), BF16),
+        in_specs=[vmem()],
+        out_specs=vmem(),
+        scratch_shapes=[pltpu.VMEM((KEPT, B, B), F32)],
+        compiler_params=params(12),
+    )(shards)
+    moved_moments = lax.all_to_all(
+        after(packed_moments, shards), "tensor", split_axis=0, concat_axis=0, tiled=True
+    )
+    pair32 = sd((2, SLOTS * ROWS, B), F32)
+    pair16 = sd((2, SLOTS * ROWS, B), BF16)
+    hidden_out, *pairs = pl.pallas_call(
+        main_kernel,
+        out_shape=(sd(upstream.shape, BF16),) + (pair32,) * 4 + (pair16,) * 2 + (sd((4, SLOTS * ROWS, B), BF16),),
+        in_specs=[smem()] * 2 + [hbm()] * 8,
+        out_specs=(hbm(),) * 8,
+        scratch_shapes=[
+            pltpu.VMEM((OWNERS,) + tokens.shape, BF16),
+            pltpu.VMEM(upstream.shape, BF16),
+            pltpu.VMEM((KEPT, B, B), BF16),
+            pltpu.VMEM(upstream.shape, BF16),
+            pltpu.VMEM((COLS, tokens.shape[0], B), BF16),
+            pltpu.VMEM((2 * B, B), F32),
+            pltpu.VMEM((ZN, SLOTS * ROWS, B), F32),
+            pltpu.VMEM((ZN, SLOTS * ROWS, B), BF16),
+            pltpu.SemaphoreType.DMA((OWNERS,)),
+            pltpu.SemaphoreType.DMA((3,)),
+            pltpu.SemaphoreType.DMA((3, 8)),
+        ],
+        compiler_params=params(56),
+        cost_estimate=pl.CostEstimate(flops=4 * 10**9, bytes_accessed=2 * 10**7, transcendentals=10**6),
+    )(table, where, upstream, weights, *token_pieces)
+    keep, send = pairs[:4], pairs[4:]
+
+    moved_moments, keep = lax.optimization_barrier((moved_moments, keep))
+    kept_states = pl.pallas_call(
         place_kernel,
-        out_shape=(flat16, flat, flat, flat, flat),
-        in_specs=[smem()] + [vmem()] * 4,
-        out_specs=(vmem(),) * 5,
-        scratch_shapes=[pltpu.VMEM((KEPT * ROWS, B), F32)],
-        compiler_params=PARAMS,
-    )(table, *states, arrived)
-
-    pieces = gather_pieces(copy_in)
-
-    tokens_here = tokens.shape[0]
-    hidden_out, keep, send = pl.pallas_call(
-        main_kernel,
-        out_shape=(
-            sd((tokens_here, COLS * B), BF16),
-            sd((ZN, SLOTS * ROWS, B), F32),
-            sd((ZN, SLOTS * ROWS, B), BF16),
-        ),
-        in_specs=[smem()] * 2 + [vmem()] * 18,
-        out_specs=(vmem(),) * 3,
-        scratch_shapes=[
-            pltpu.VMEM((KEPT, B, B), F32),
-            pltpu.VMEM((COLS, tokens_here, B), BF16),
-            pltpu.VMEM((2 * B, B), F32),
-        ],
-        compiler_params=PARAMS,
-        cost_estimate=pl.CostEstimate(flops=4 * 10**9, bytes_accessed=2 * 10**7, transcendentals=10**6),
-    )(table, where, gathered, upstream, *pieces)
+        out_shape=(flat,) * 4,
+        in_specs=[smem()] + [vmem()] * 5,
+        out_specs=(vmem(),) * 4,
+        compiler_params=params(8),
+    )(table, *states, arrived, moved_moments)
 
     grads = reduce_chunks(keep, send)
 
@@ -385,8 +521,8 @@
         in_specs=[smem()] + [vmem()] * 8,
         out_specs=(vmem(),) * 4,
         scratch_shapes=[pltpu.VMEM((KEPT * ROWS, B), F32)],
-        compiler_params=PARAMS,
-    )(table, *grads, kept_master, kept_first, kept_second, mask)
+        compiler_params=params(8),
+    )(table, *grads, *kept_states)
 
     final = gather_pieces(fresh)
     weight_copy = pl.pallas_call(
@@ -395,7 +531,7 @@
         in_specs=[smem()] * 2 + [vmem()] * 16,
         out_specs=vmem(),
         scratch_shapes=[pltpu.VMEM((KEPT, B, B), F32)],
-        compiler_params=PARAMS,
+        compiler_params=params(12),
     )(table, where, *final)
 
     def back(a):

time: 171 us -> 157 us (0.918)
  waiting for transfers between devices: 36 us -> 62.8 us
  between operations: 14.4 us -> 0.86 us
  starting transfers between devices: 61.2 us -> 48.4 us
  Pallas kernels: 32.7 us -> 23 us
  blocking collectives: 16.5 us -> 11.8 us
  other arithmetic: 1.66 us -> 5.12 us
  local copies, waits for them, and re-layouts: 5.2 us -> 2.61 us
    all_to_all x0 -> x2, waiting for transfers between devices: none -> 27.6 us  [the longest x1 27.6 us: local(): lax.all_to_all(copies, 'dp', split_axis=0, concat_axis=0, tiled=True)]
    ppermute x12 -> x6, starting transfers between devices: 29 us -> 10.5 us  [gather_pieces(): down[j] = lax.ppermute(down[j], 'dp', DOWN)]
    all_to_all x0 -> x2, starting transfers between devices: none -> 16.3 us  [the longest x1 11.4 us: local(): lax.all_to_all(copies, 'dp', split_axis=0, concat_axis=0, tiled=True)]
    pallas_call x2 -> x4, Pallas kernels: 23.1 us -> 15.1 us  [the longest x1 11.9 us: local(): pl.pallas_call(main_kernel, out_shape=(sd(upstream.shape, BF16),) + (pair...]
    ppermute x12 -> x6, starting transfers between devices: 7.63 us -> 1.02 us  [gather_pieces(): up[j] = lax.ppermute(up[j], 'dp', UP)]
    ppermute x2 -> x1, waiting for transfers between devices: 8.71 us -> 2.14 us  [gather_pieces(): swapped = lax.ppermute(shard, 'dp', SWAP)]
    all_to_all x1, blocking collectives: 16.5 us -> 11.8 us  [local(): lax.all_to_all(packed, 'tensor', split_axis=0, concat_axis=0, tiled=True)]
    ppermute x8 -> x13, waiting for transfers between devices: 21.9 us -> 26.4 us  [the longest x3 12.4 us: reduce_chunks(): got = [lax.ppermute(a, 'dp', SWAP) for a in send]]
  transfers between devices with their start and end apart: 39 -> 30, of which waited for: 13 -> 15; matrix products, arithmetic and copies ran while one was open for 1% -> 3% of each run, Pallas kernels for 4% -> 12%
where the time goes in v1:
time: 157 us; the launch traced here: 155 us
  waiting for transfers between devices  62.8 us (40%)
  starting transfers between devices  48.4 us (31%)
  Pallas kernels  23 us (15%)
  blocking collectives  11.8 us (8%)
  other arithmetic  5.12 us (3%)
  local copies, waits for them, and re-layouts  2.61 us (2%)
    all_to_all x1, waiting for transfers between devices, local(): lax.all_to_all(copies, 'dp', split_axis=0, concat_axis=0, tiled=True)  27.6 us
    ppermute x3, waiting for transfers between devices, reduce_chunks(): got = [lax.ppermute(a, 'dp', SWAP) for a in send]  12.4 us
    pallas_call x1, Pallas kernels, local(): pl.pallas_call(main_kernel, out_shape=(sd(upstream.shape, BF16),) + (pair...  11.9 us
    all_to_all x1, blocking collectives, local(): lax.all_to_all(packed, 'tensor', split_axis=0, concat_axis=0, tiled=True)  11.8 us
    all_to_all x1, starting transfers between devices, local(): lax.all_to_all(copies, 'dp', split_axis=0, concat_axis=0, tiled=True)  11.4 us
    ppermute x6, starting transfers between devices, gather_pieces(): down[j] = lax.ppermute(down[j], 'dp', DOWN)  10.5 us
    ppermute x3, starting transfers between devices, reduce_chunks(): got = [lax.ppermute(a, 'dp', SWAP) for a in send]  7.44 us
    ppermute x1, waiting for transfers between devices, reduce_chunks(): c = lax.ppermute(total(2, b), AXES, FAR)  6.04 us
  transfers between devices with their start and end apart: 30, of which 15 were waited for; matrix products, arithmetic and copies ran while one was open for 3% of the time, Pallas kernels for 12%

profile of v1, /device:TPU:6, one launch (start us, length us, event | category | flops | bytes accessed | tf_op | source)
XLA Modules:
  0.0 154.6 jit_solution(9650271118933165070)
XLA Ops:
  0.6 0.9 collective-permute-start
  1.6 3.2 %shard_map.119 = (s32[8,128]{1,0:T(8,128)}, f32[48,8,128]{2,1,0:T(8,128)}, f32[48,2,8,128]{3,2,1,0:T(8,128)}) custom-call(s32[1]{0:T(128)} %bitcast.me_ref, s32[16,60]{1,0:T(8,128)} %old_ref.1, s32[16,60]{1,0:T(8,128)} %new_ref.1, s32[16,12]{1,0:T(8,128)} %cols_ref.1, f32[60,8,128]{2,1,0:T(8,128)} %bitcast.25, f32[60,8,128]{2,1,0:T(8,128)} %bitcast.28, ...), custom_call_target="tpu_custom_call" | custom-call | tf_op jit(solution)/shard_map/pallas_call | solution.py:435
  4.8 0.0 copy-start.5
  4.8 11.8 %all_to_all.15.arrived_ref = f32[48,8,128]{2,1,0:T(8,128)S(1)} all-to-all(f32[48,8,128]{2,1,0:T(8,128)} %get-tuple-element.34), channel_id=1, replica_groups=mesh['dp'=16,'tensor'=16] {'tensor'}, dimensions={0} | all-to-all | bytes 393216 | tf_op jit(solution)/shard_map/all_to_all | solution.py:447
  16.6 1.2 pad_maximum_fusion.1.refs_4_
  17.8 0.3 collective-permute-start.1
  18.1 1.9 %shard_map.120 = bf16[16,288,128]{2,1,0:T(8,128)(2,1)} custom-call(s32[8,128]{1,0:T(8,128)S(1)} %copy-done.5, f32[60,8,128]{2,1,0:T(8,128)S(1)} %bitcast.26, f32[48,8,128]{2,1,0:T(8,128)S(1)} %all_to_all.15.arrived_ref), custom_call_target="tpu_custom_call" | custom-call | tf_op jit(solution)/shard_map/pallas_call | solution.py:454
  20.0 11.4 %all-to-all-start.1 = ((bf16[16,288,128]{2,1,0:T(8,128)(2,1)}), bf16[16,288,128]{2,1,0:T(8,128)(2,1)S(1)}, u32[]{:S(2)}, u32[]{:S(2)}) async-start(bf16[16,288,128]{2,1,0:T(8,128)(2,1)} %shard_map.120), calls=%async_computation.1 | async-start | bytes 2359296 | tf_op jit(solution)/shard_map/all_to_all | solution.py:462
  31.5 0.0 collective-permute-done.1.refs_5_
  31.5 1.5 pad_maximum_fusion
  33.0 1.5 collective-permute-start.2
  34.6 27.6 %all-to-all-done.1.shards_ref = bf16[16,288,128]{2,1,0:T(8,128)(2,1)S(1)} async-done(((bf16[16,288,128]{2,1,0:T(8,128)(2,1)}), bf16[16,288,128]{2,1,0:T(8,128)(2,1)S(1)}, u32[]{:S(2)}, u32[]{:S(2)}) %all-to-all-start.1) | async-done | bytes 1179680 | tf_op jit(solution)/shard_map/all_to_all | solution.py:462
  62.2 0.0 collective-permute-done.2.refs_6_
  62.2 0.5 collective-permute-start.3
  62.7 0.0 collective-permute-start.4
  62.7 0.7 stack.40.refs_1_
  63.4 4.8 %all-to-all-start.2 = ((f32[48,2,8,128]{3,2,1,0:T(8,128)}), f32[48,2,8,128]{3,2,1,0:T(8,128)S(1)}, u32[]{:S(2)}, u32[]{:S(2)}) async-start(f32[48,2,8,128]{3,2,1,0:T(8,128)} %get-tuple-element.40), calls=%async_computation.2 | async-start | bytes 786432 | tf_op jit(solution)/shard_map/all_to_all | solution.py:479
  68.2 0.1 shard_map.121.refs_3_
  68.3 0.0 copy-start.1
  68.3 1.0 copy-done.1
  69.3 0.0 collective-permute-done.5.refs_9_
  69.3 0.9 copy-done.11
  70.2 11.9 %shard_map.122 = (bf16[512,1536]{1,0:T(8,128)(2,1)}, f32[2,480,128]{2,1,0:T(8,128)}, f32[2,480,128]{2,1,0:T(8,128)}, f32[2,480,128]{2,1,0:T(8,128)}, f32[2,480,1...) custom-call(s32[8,128]{1,0:T(8,128)} %get-tuple-element.33.table_ref.re, ...), custom_call_target="tpu_custom_call" | custom-call | flops 4000000000 | bytes 20000000 | tf_op jit(solution)/shard_map/pallas_call | solution.py:484
  82.1 3.7 %collective-permute-start.8 = (bf16[2,480,128]{2,1,0:T(8,128)(2,1)}, bf16[2,480,128]{2,1,0:T(8,128)(2,1)S(1)}, u32[]{:S(2)}, u32[]{:S(2)}) collective-permute-start(bf16[2,480,128]{2,1,0:T(8,128)(2,1)} %get-tuple-element.51), channel_id=1, source_target_pairs={{0,16},{16,0},{32,48},{48,32},{64,80},{80,64},{96,112},{112,96},{1... | collective-permute-start | bytes 737288 | tf_op jit(solution)/shard_map/ppermute | solution.py:408
  85.8 0.1 collective-permute-start.7
  85.9 6.8 %collective-permute-done.8 = bf16[2,480,128]{2,1,0:T(8,128)(2,1)S(1)} collective-permute-done((bf16[2,480,128]{2,1,0:T(8,128)(2,1)}, bf16[2,480,128]{2,1,0:T(8,128)(2,1)S(1)}, u32[]{:S(2)}, u32[]{:S(2)}) %collective-permute-start.8) | collective-permute-done | bytes 245792 | tf_op jit(solution)/shard_map/ppermute | solution.py:408
  92.7 1.1 add_convert_fusion.2
  93.8 0.1 collective-permute-start.9
  93.9 0.0 copy-start.3
  93.9 0.0 copy-start.4
  94.0 0.0 copy-start.6
  94.0 3.6 %collective-permute-start.6 = (bf16[4,480,128]{2,1,0:T(8,128)(2,1)}, bf16[4,480,128]{2,1,0:T(8,128)(2,1)S(1)}, u32[]{:S(2)}, u32[]{:S(2)}) collective-permute-start(bf16[4,480,128]{2,1,0:T(8,128)(2,1)} %get-tuple-element.46), channel_id=1, source_target_pairs={{0,16},{16,0},{32,48},{48,32},{64,80},{80,64},{96,112},{112,96},{1... | collective-permute-start | bytes 1474568 | tf_op jit(solution)/shard_map/ppermute | solution.py:408
  97.6 3.7 %collective-permute-done.9 = bf16[2,480,128]{2,1,0:T(8,128)(2,1)S(1)} collective-permute-done((bf16[2,480,128]{2,1,0:T(8,128)(2,1)S(1)}, bf16[2,480,128]{2,1,0:T(8,128)(2,1)S(1)}, u32[]{:S(2)}, u32[]{:S(2)}) %collective-permute-start.9) | collective-permute-done | bytes 245792 | tf_op jit(solution)/shard_map/ppermute | solution.py:415
  101.3 1.1 add_convert_fusion.1
  102.5 0.1 collective-permute-start.10
  102.6 5.5 %collective-permute-done.6 = bf16[4,480,128]{2,1,0:T(8,128)(2,1)S(1)} collective-permute-done((bf16[4,480,128]{2,1,0:T(8,128)(2,1)}, bf16[4,480,128]{2,1,0:T(8,128)(2,1)S(1)}, u32[]{:S(2)}, u32[]{:S(2)}) %collective-permute-start.6) | collective-permute-done | bytes 491552 | tf_op jit(solution)/shard_map/ppermute | solution.py:408
  108.1 0.7 collective-permute-done.10
  108.7 0.1 add_convert_fusion
  108.8 1.5 collective-permute-start.11
  110.3 6.0 %collective-permute-done.11.near_ref = bf16[2,480,128]{2,1,0:T(8,128)(2,1)S(1)} collective-permute-done((bf16[2,480,128]{2,1,0:T(8,128)(2,1)S(1)}, bf16[2,480,128]{2,1,0:T(8,128)(2,1)S(1)}, u32[]{:S(2)}, u32[]{:S(2)}) %collective-permute-start.11) | collective-permute-done | bytes 245792 | tf_op jit(solution)/shard_map/ppermute | solution.py:417
  116.4 0.1 collective-permute-start.12
  116.6 1.2 shard_map.123
  117.8 3.6 %collective-permute-done.12.last_ref = bf16[480,128]{1,0:T(8,128)(2,1)S(1)} collective-permute-done((bf16[480,128]{1,0:T(8,128)(2,1)S(1)}, bf16[480,128]{1,0:T(8,128)(2,1)S(1)}, u32[]{:S(2)}, u32[]{:S(2)}) %collective-permute-start.12) | collective-permute-done | bytes 122912 | tf_op jit(solution)/shard_map/ppermute | solution.py:418
  121.4 1.8 %shard_map.124 = (f32[480,128]{1,0:T(8,128)}, f32[480,128]{1,0:T(8,128)}, f32[480,128]{1,0:T(8,128)}, bf16[288,128]{1,0:T(8,128)(2,1)S(1)}) custom-call(s32[8,128]{1,0:T(8,128)S(1)} %copy-done.6, f32[2,480,128]{2,1,0:T(8,128)S(1)} %copy-done.2, bf16[2,480,128]{2,1,0:T(8,128)(2,1)S(1)} %slice.12.got_ref, ...), custom_call_target="tpu_custom_call" | custom-call | tf_op jit(solution)/shard_map/pallas_call | solution.py:518
  123.2 5.0 %collective-permute-start.13 = (bf16[288,128]{1,0:T(8,128)(2,1)S(1)}, bf16[288,128]{1,0:T(8,128)(2,1)S(1)}, u32[]{:S(2)}, u32[]{:S(2)}) collective-permute-start(bf16[288,128]{1,0:T(8,128)(2,1)S(1)} %get-tuple-element.60.refs_2_), channel_id=1, source_target_pairs={{0,16},{16,0},{32,48},{48,32},{64,80},{80,64},{96,112},{112,96},{1... | collective-permute-start | bytes 221192 | tf_op jit(solution)/shard_map/ppermute | solution.py:373
  128.2 0.2 collective-permute-start.20
  128.4 2.1 %collective-permute-done.13.refs_3_ = bf16[288,128]{1,0:T(8,128)(2,1)S(1)} collective-permute-done((bf16[288,128]{1,0:T(8,128)(2,1)S(1)}, bf16[288,128]{1,0:T(8,128)(2,1)S(1)}, u32[]{:S(2)}, u32[]{:S(2)}) %collective-permute-start.13) | collective-permute-done | bytes 73760 | tf_op jit(solution)/shard_map/ppermute | solution.py:373
  130.5 1.1 collective-permute-start.15
  131.6 0.0 collective-permute-start.14
  131.6 2.1 %collective-permute-done.20.refs_16_ = bf16[288,128]{1,0:T(8,128)(2,1)S(1)} collective-permute-done((bf16[288,128]{1,0:T(8,128)(2,1)S(1)}, bf16[288,128]{1,0:T(8,128)(2,1)S(1)}, u32[]{:S(2)}, u32[]{:S(2)}) %collective-permute-start.20) | collective-permute-done | bytes 73760 | tf_op jit(solution)/shard_map/ppermute | solution.py:379
  133.8 0.8 collective-permute-start.25
  134.6 0.3 collective-permute-done.15.refs_5_
  134.9 2.4 %collective-permute-start.17 = (bf16[288,128]{1,0:T(8,128)(2,1)S(1)}, bf16[288,128]{1,0:T(8,128)(2,1)S(1)}, u32[]{:S(2)}, u32[]{:S(2)}) collective-permute-start(bf16[288,128]{1,0:T(8,128)(2,1)S(1)} %collective-permute-done.15.refs_5_), channel_id=1, source_target_pairs={{0,224},{16,240},{32,0},{48,16},{64,32},{80,48},{96,64},{112,80},{... | collective-permute-start | bytes 221192 | tf_op jit(solution)/shard_map/ppermute | solution.py:380
  137.3 1.8 %collective-permute-start.16 = (bf16[288,128]{1,0:T(8,128)(2,1)S(1)}, bf16[288,128]{1,0:T(8,128)(2,1)S(1)}, u32[]{:S(2)}, u32[]{:S(2)}) collective-permute-start(bf16[288,128]{1,0:T(8,128)(2,1)S(1)} %collective-permute-done.14.refs_4_), channel_id=1, source_target_pairs={{0,224},{16,240},{32,0},{48,16},{64,32},{80,48},{96,64},{112,80},{... | collective-permute-start | bytes 221192 | tf_op jit(solution)/shard_map/ppermute | solution.py:380
  139.1 0.3 collective-permute-done.21.refs_14_
  139.4 0.8 collective-permute-done.25.refs_17_
  140.1 3.2 %collective-permute-start.19 = (bf16[288,128]{1,0:T(8,128)(2,1)S(1)}, bf16[288,128]{1,0:T(8,128)(2,1)S(1)}, u32[]{:S(2)}, u32[]{:S(2)}) collective-permute-start(bf16[288,128]{1,0:T(8,128)(2,1)S(1)} %collective-permute-done.17.refs_7_), channel_id=1, source_target_pairs={{0,224},{16,240},{32,0},{48,16},{64,32},{80,48},{96,64},{112,80},{... | collective-permute-start | bytes 221192 | tf_op jit(solution)/shard_map/ppermute | solution.py:380
  143.4 2.0 %collective-permute-start.18 = (bf16[288,128]{1,0:T(8,128)(2,1)S(1)}, bf16[288,128]{1,0:T(8,128)(2,1)S(1)}, u32[]{:S(2)}, u32[]{:S(2)}) collective-permute-start(bf16[288,128]{1,0:T(8,128)(2,1)S(1)} %collective-permute-done.16.refs_6_), channel_id=1, source_target_pairs={{0,224},{16,240},{32,0},{48,16},{64,32},{80,48},{96,64},{112,80},{... | collective-permute-start | bytes 221192 | tf_op jit(solution)/shard_map/ppermute | solution.py:380
  145.4 0.0 collective-permute-start.23
  145.4 0.3 collective-permute-done.26.refs_15_
  145.7 3.2 %collective-permute-start.24 = (bf16[288,128]{1,0:T(8,128)(2,1)S(1)}, bf16[288,128]{1,0:T(8,128)(2,1)S(1)}, u32[]{:S(2)}, u32[]{:S(2)}) collective-permute-start(bf16[288,128]{1,0:T(8,128)(2,1)S(1)} %collective-permute-done.19.refs_9_), channel_id=1, source_target_pairs={{0,224},{16,240},{32,0},{48,16},{64,32},{80,48},{96,64},{112,80},{... | collective-permute-start | bytes 221192 | tf_op jit(solution)/shard_map/ppermute | solution.py:385
  148.9 2.0 %collective-permute-done.23.refs_10_ = bf16[288,128]{1,0:T(8,128)(2,1)S(1)} collective-permute-done((bf16[288,128]{1,0:T(8,128)(2,1)S(1)}, bf16[288,128]{1,0:T(8,128)(2,1)S(1)}, u32[]{:S(2)}, u32[]{:S(2)}) %collective-permute-start.23) | collective-permute-done | bytes 73760 | tf_op jit(solution)/shard_map/ppermute | solution.py:384
  151.0 0.8 collective-permute-done.27.refs_13_
  151.8 2.8 %shard_map.125 = bf16[60,128,128]{2,1,0:T(8,128)(2,1)} custom-call(s32[8,128]{1,0:T(8,128)S(1)} %copy-done.6, s32[7]{0:T(128)S(1)} %copy-done.7, bf16[288,128]{1,0:T(8,128)(2,1)S(1)} %get-tuple-element.60.refs_2_, bf16[288,128]{1,0:T(8,128)(2,1)S(1)} %collective-permute-done.13.refs_3_, bf16[288,128]{1,0:T(8,128)(2,1)S(1)} %collective-permute-done.14.refs_4_, ...), custom_call_target="tpu_custom_call" | custom-call | tf_op jit(solution)/shard_map/pallas_call | solution.py:528
  (36 shorter events, 0.1 us)
Async XLA Ops:
  0.6 17.5 %copy-start = (f32[8,60,128]{2,0,1:T(8,128)S(1)}, f32[8,60,128]{2,0,1:T(8,128)}, u32[]{:S(2)}) copy-start(f32[8,60,128]{2,0,1:T(8,128)} %param.10) | copy-start | bytes 737284
  0.6 15.9 %collective-permute-start = (bf16[512,384]{1,0:T(8,128)(2,1)}, bf16[512,384]{1,0:T(8,128)(2,1)S(1)}, u32[]{:S(2)}, u32[]{:S(2)}) collective-permute-start(bf16[512,384]{1,0:T(8,128)(2,1)} %param.8), channel_id=1, source_target_pairs={{0,2},{1,3},{2,0},{3,1},{4,6},{5,7},{6,4},{7,5},{8,10},{9,11},{10,... | collective-permute-start | bytes 1179656 | tf_op jit(solution)/shard_map/ppermute | solution.py:404
  4.8 13.3 %copy-start.5 = (s32[8,128]{1,0:T(8,128)S(1)}, s32[8,128]{1,0:T(8,128)}, u32[]{:S(2)}) copy-start(s32[8,128]{1,0:T(8,128)} %get-tuple-element.33.table_ref.refs_0_) | copy-start | bytes 12292
  16.6 3.5 %copy-start.8 = (bf16[512,384]{1,0:T(8,128)(2,1)}, bf16[512,384]{1,0:T(8,128)(2,1)S(1)}, u32[]{:S(2)}) copy-start(bf16[512,384]{1,0:T(8,128)(2,1)S(1)} %collective-permute-done) | copy-start | bytes 1179652
  17.8 2.2 %copy-start.9 = (bf16[2,512,384]{2,1,0:T(8,128)(2,1)}, bf16[2,512,384]{2,1,0:T(8,128)(2,1)S(1)}, u32[]{:S(2)}) copy-start(bf16[2,512,384]{2,1,0:T(8,128)(2,1)S(1)} %pad_maximum_fusion.1.refs_4_) | copy-start | bytes 2359300
  17.8 13.7 %collective-permute-start.1 = (bf16[2,512,384]{2,1,0:T(8,128)(2,1)S(1)}, bf16[2,512,384]{2,1,0:T(8,128)(2,1)}, u32[]{:S(2)}, u32[]{:S(2)}) collective-permute-start(bf16[2,512,384]{2,1,0:T(8,128)(2,1)S(1)} %pad_maximum_fusion.1.refs_4_), channel_id=1, source_target_pairs={{0,4},{1,13},{2,6},{3,15},{4,0},{5,9},{6,2},{7,11},{8,12},{9,5},{1... | collective-permute-start | bytes 2359304 | tf_op jit(solution)/shard_map/ppermute | solution.py:404
  20.0 42.1 %all-to-all-start.1 = ((bf16[16,288,128]{2,1,0:T(8,128)(2,1)}), bf16[16,288,128]{2,1,0:T(8,128)(2,1)S(1)}, u32[]{:S(2)}, u32[]{:S(2)}) async-start(bf16[16,288,128]{2,1,0:T(8,128)(2,1)} %shard_map.120), calls=%async_computation.1 | async-start | bytes 2359296 | tf_op jit(solution)/shard_map/all_to_all | solution.py:462
  33.0 29.1 %collective-permute-start.2 = (bf16[4,512,384]{2,1,0:T(8,128)(2,1)S(1)}, bf16[4,512,384]{2,1,0:T(8,128)(2,1)}, u32[]{:S(2)}, u32[]{:S(2)}) collective-permute-start(bf16[4,512,384]{2,1,0:T(8,128)(2,1)S(1)} %pad_maximum_fusion), channel_id=1, source_target_pairs={{0,12},{1,5},{2,14},{3,7},{4,8},{5,1},{6,10},{7,3},{8,4},{9,13},{1... | collective-permute-start | bytes 4718600 | tf_op jit(solution)/shard_map/ppermute | solution.py:404
  62.2 7.1 %collective-permute-start.5 = (bf16[4,512,384]{2,1,0:T(8,128)(2,1)}, bf16[4,512,384]{2,1,0:T(8,128)(2,1)}, u32[]{:S(2)}, u32[]{:S(2)}) collective-permute-start(bf16[4,512,384]{2,1,0:T(8,128)(2,1)} %collective-permute-done.2.refs_6_), channel_id=1, source_target_pairs={{0,1},{1,0},{2,3},{3,2},{4,5},{5,4},{6,7},{7,6},{8,9},{9,8},{10,11... | collective-permute-start | bytes 4718600 | tf_op jit(solution)/shard_map/ppermute | solution.py:404
  62.2 7.1 %collective-permute-start.3 = (bf16[2,512,384]{2,1,0:T(8,128)(2,1)}, bf16[2,512,384]{2,1,0:T(8,128)(2,1)S(1)}, u32[]{:S(2)}, u32[]{:S(2)}) collective-permute-start(bf16[2,512,384]{2,1,0:T(8,128)(2,1)} %copy-done.9), channel_id=1, source_target_pairs={{0,1},{1,0},{2,3},{3,2},{4,5},{5,4},{6,7},{7,6},{8,9},{9,8},{10,11... | collective-permute-start | bytes 2359304 | tf_op jit(solution)/shard_map/ppermute | solution.py:404
  62.7 6.6 %collective-permute-start.4 = (bf16[2,512,384]{2,1,0:T(8,128)(2,1)}, bf16[2,512,384]{2,1,0:T(8,128)(2,1)}, u32[]{:S(2)}, u32[]{:S(2)}) collective-permute-start(bf16[2,512,384]{2,1,0:T(8,128)(2,1)} %collective-permute-done.1.refs_5_), channel_id=1, source_target_pairs={{0,1},{1,0},{2,3},{3,2},{4,5},{5,4},{6,7},{7,6},{8,9},{9,8},{10,11... | collective-permute-start | bytes 2359304 | tf_op jit(solution)/shard_map/ppermute | solution.py:404
  63.4 22.4 %all-to-all-start.2 = ((f32[48,2,8,128]{3,2,1,0:T(8,128)}), f32[48,2,8,128]{3,2,1,0:T(8,128)S(1)}, u32[]{:S(2)}, u32[]{:S(2)}) async-start(f32[48,2,8,128]{3,2,1,0:T(8,128)} %get-tuple-element.40), calls=%async_computation.2 | async-start | bytes 786432 | tf_op jit(solution)/shard_map/all_to_all | solution.py:479
  68.3 1.0 copy-start.1
  69.3 0.9 copy-start.11
  82.1 26.7 %copy-start.10 = (f32[2,480,128]{2,1,0:T(8,128)S(1)}, f32[2,480,128]{2,1,0:T(8,128)}, u32[]{:S(2)}) copy-start(f32[2,480,128]{2,1,0:T(8,128)} %get-tuple-element.47) | copy-start | bytes 1474564
  82.1 10.6 %collective-permute-start.8 = (bf16[2,480,128]{2,1,0:T(8,128)(2,1)}, bf16[2,480,128]{2,1,0:T(8,128)(2,1)S(1)}, u32[]{:S(2)}, u32[]{:S(2)}) collective-permute-start(bf16[2,480,128]{2,1,0:T(8,128)(2,1)} %get-tuple-element.51), channel_id=1, source_target_pairs={{0,16},{16,0},{32,48},{48,32},{64,80},{80,64},{96,112},{112,96},{1... | collective-permute-start | bytes 737288 | tf_op jit(solution)/shard_map/ppermute | solution.py:408
  85.8 11.8 %collective-permute-start.7 = (bf16[2,480,128]{2,1,0:T(8,128)(2,1)}, bf16[2,480,128]{2,1,0:T(8,128)(2,1)S(1)}, u32[]{:S(2)}, u32[]{:S(2)}) collective-permute-start(bf16[2,480,128]{2,1,0:T(8,128)(2,1)} %get-tuple-element.49), channel_id=1, source_target_pairs={{0,16},{16,0},{32,48},{48,32},{64,80},{80,64},{96,112},{112,96},{1... | collective-permute-start | bytes 737288 | tf_op jit(solution)/shard_map/ppermute | solution.py:408
  93.8 22.6 %copy-start.2 = (f32[2,480,128]{2,1,0:T(8,128)S(1)}, f32[2,480,128]{2,1,0:T(8,128)}, u32[]{:S(2)}) copy-start(f32[2,480,128]{2,1,0:T(8,128)} %get-tuple-element.45.own_ref) | copy-start | bytes 1474564
  93.8 7.5 %collective-permute-start.9 = (bf16[2,480,128]{2,1,0:T(8,128)(2,1)S(1)}, bf16[2,480,128]{2,1,0:T(8,128)(2,1)S(1)}, u32[]{:S(2)}, u32[]{:S(2)}) collective-permute-start(bf16[2,480,128]{2,1,0:T(8,128)(2,1)S(1)} %add_convert_fusion.2), channel_id=1, source_target_pairs={{0,224},{1,33},{2,226},{3,35},{4,228},{5,37},{6,230},{7,39},{8,232... | collective-permute-start | bytes 737288 | tf_op jit(solution)/shard_map/ppermute | solution.py:415
  93.9 22.6 %copy-start.3 = (f32[8,60,128]{2,0,1:T(8,128)S(1)}, f32[8,60,128]{2,0,1:T(8,128)}, u32[]{:S(2)}) copy-start(f32[8,60,128]{2,0,1:T(8,128)} %param.11) | copy-start | bytes 737284
  93.9 22.6 %copy-start.4 = (f32[8,60,128]{2,0,1:T(8,128)S(1)}, f32[8,60,128]{2,0,1:T(8,128)}, u32[]{:S(2)}) copy-start(f32[8,60,128]{2,0,1:T(8,128)} %param.12) | copy-start | bytes 737284
  94.0 22.6 %copy-start.6 = (s32[8,128]{1,0:T(8,128)S(1)}, s32[8,128]{1,0:T(8,128)}, u32[]{:S(2)}) copy-start(s32[8,128]{1,0:T(8,128)} %get-tuple-element.33.table_ref.refs_0_) | copy-start | bytes 12292
  94.0 14.1 %collective-permute-start.6 = (bf16[4,480,128]{2,1,0:T(8,128)(2,1)}, bf16[4,480,128]{2,1,0:T(8,128)(2,1)S(1)}, u32[]{:S(2)}, u32[]{:S(2)}) collective-permute-start(bf16[4,480,128]{2,1,0:T(8,128)(2,1)} %get-tuple-element.46), channel_id=1, source_target_pairs={{0,16},{16,0},{32,48},{48,32},{64,80},{80,64},{96,112},{112,96},{1... | collective-permute-start | bytes 1474568 | tf_op jit(solution)/shard_map/ppermute | solution.py:408
  102.5 6.3 %collective-permute-start.10 = (bf16[2,480,128]{2,1,0:T(8,128)(2,1)S(1)}, bf16[2,480,128]{2,1,0:T(8,128)(2,1)S(1)}, u32[]{:S(2)}, u32[]{:S(2)}) collective-permute-start(bf16[2,480,128]{2,1,0:T(8,128)(2,1)S(1)} %add_convert_fusion.1), channel_id=1, source_target_pairs={{0,32},{1,225},{2,34},{3,227},{4,36},{5,229},{6,38},{7,231},{8,40}... | collective-permute-start | bytes 737288 | tf_op jit(solution)/shard_map/ppermute | solution.py:416
  108.8 7.5 %collective-permute-start.11 = (bf16[2,480,128]{2,1,0:T(8,128)(2,1)S(1)}, bf16[2,480,128]{2,1,0:T(8,128)(2,1)S(1)}, u32[]{:S(2)}, u32[]{:S(2)}) collective-permute-start(bf16[2,480,128]{2,1,0:T(8,128)(2,1)S(1)} %add_convert_fusion), channel_id=1, source_target_pairs={{0,224},{1,33},{2,226},{3,35},{4,228},{5,37},{6,230},{7,39},{8,232... | collective-permute-start | bytes 737288 | tf_op jit(solution)/shard_map/ppermute | solution.py:417
  116.4 35.3 %copy-start.7 = (s32[7]{0:T(128)S(1)}, s32[7]{0:T(128)}, u32[]{:S(2)}) copy-start(s32[7]{0:T(128)} %stack.40.refs_1_) | copy-start | bytes 88
  116.4 5.0 %collective-permute-start.12 = (bf16[480,128]{1,0:T(8,128)(2,1)S(1)}, bf16[480,128]{1,0:T(8,128)(2,1)S(1)}, u32[]{:S(2)}, u32[]{:S(2)}) collective-permute-start(bf16[480,128]{1,0:T(8,128)(2,1)S(1)} %fusion.2), channel_id=1, source_target_pairs={{0,32},{1,225},{2,34},{3,227},{4,36},{5,229},{6,38},{7,231},{8,40}... | collective-permute-start | bytes 368648 | tf_op jit(solution)/shard_map/ppermute | solution.py:418
  123.2 7.3 %collective-permute-start.13 = (bf16[288,128]{1,0:T(8,128)(2,1)S(1)}, bf16[288,128]{1,0:T(8,128)(2,1)S(1)}, u32[]{:S(2)}, u32[]{:S(2)}) collective-permute-start(bf16[288,128]{1,0:T(8,128)(2,1)S(1)} %get-tuple-element.60.refs_2_), channel_id=1, source_target_pairs={{0,16},{16,0},{32,48},{48,32},{64,80},{80,64},{96,112},{112,96},{1... | collective-permute-start | bytes 221192 | tf_op jit(solution)/shard_map/ppermute | solution.py:373
  128.2 5.6 %collective-permute-start.20 = (bf16[288,128]{1,0:T(8,128)(2,1)S(1)}, bf16[288,128]{1,0:T(8,128)(2,1)S(1)}, u32[]{:S(2)}, u32[]{:S(2)}) collective-permute-start(bf16[288,128]{1,0:T(8,128)(2,1)S(1)} %get-tuple-element.60.refs_2_), channel_id=1, source_target_pairs={{0,32},{16,48},{32,64},{48,80},{64,96},{80,112},{96,128},{112,144}... | collective-permute-start | bytes 221192 | tf_op jit(solution)/shard_map/ppermute | solution.py:379
  130.5 4.4 %collective-permute-start.15 = (bf16[288,128]{1,0:T(8,128)(2,1)S(1)}, bf16[288,128]{1,0:T(8,128)(2,1)S(1)}, u32[]{:S(2)}, u32[]{:S(2)}) collective-permute-start(bf16[288,128]{1,0:T(8,128)(2,1)S(1)} %collective-permute-done.13.refs_3_), channel_id=1, source_target_pairs={{0,224},{16,240},{32,0},{48,16},{64,32},{80,48},{96,64},{112,80},{... | collective-permute-start | bytes 221192 | tf_op jit(solution)/shard_map/ppermute | solution.py:380
  131.6 5.7 %collective-permute-start.14 = (bf16[288,128]{1,0:T(8,128)(2,1)S(1)}, bf16[288,128]{1,0:T(8,128)(2,1)S(1)}, u32[]{:S(2)}, u32[]{:S(2)}) collective-permute-start(bf16[288,128]{1,0:T(8,128)(2,1)S(1)} %get-tuple-element.60.refs_2_), channel_id=1, source_target_pairs={{0,224},{16,240},{32,0},{48,16},{64,32},{80,48},{96,64},{112,80},{... | collective-permute-start | bytes 221192 | tf_op jit(solution)/shard_map/ppermute | solution.py:380
  133.8 5.6 %collective-permute-start.21 = (bf16[288,128]{1,0:T(8,128)(2,1)S(1)}, bf16[288,128]{1,0:T(8,128)(2,1)S(1)}, u32[]{:S(2)}, u32[]{:S(2)}) collective-permute-start(bf16[288,128]{1,0:T(8,128)(2,1)S(1)} %collective-permute-done.20.refs_16_), channel_id=1, source_target_pairs={{0,32},{16,48},{32,64},{48,80},{64,96},{80,112},{96,128},{112,144}... | collective-permute-start | bytes 221192 | tf_op jit(solution)/shard_map/ppermute | solution.py:379
  133.8 6.4 %collective-permute-start.25 = (bf16[288,128]{1,0:T(8,128)(2,1)S(1)}, bf16[288,128]{1,0:T(8,128)(2,1)S(1)}, u32[]{:S(2)}, u32[]{:S(2)}) collective-permute-start(bf16[288,128]{1,0:T(8,128)(2,1)S(1)} %collective-permute-done.13.refs_3_), channel_id=1, source_target_pairs={{0,32},{16,48},{32,64},{48,80},{64,96},{80,112},{96,128},{112,144}... | collective-permute-start | bytes 221192 | tf_op jit(solution)/shard_map/ppermute | solution.py:379
  134.9 5.2 %collective-permute-start.17 = (bf16[288,128]{1,0:T(8,128)(2,1)S(1)}, bf16[288,128]{1,0:T(8,128)(2,1)S(1)}, u32[]{:S(2)}, u32[]{:S(2)}) collective-permute-start(bf16[288,128]{1,0:T(8,128)(2,1)S(1)} %collective-permute-done.15.refs_5_), channel_id=1, source_target_pairs={{0,224},{16,240},{32,0},{48,16},{64,32},{80,48},{96,64},{112,80},{... | collective-permute-start | bytes 221192 | tf_op jit(solution)/shard_map/ppermute | solution.py:380
  137.3 6.1 %collective-permute-start.16 = (bf16[288,128]{1,0:T(8,128)(2,1)S(1)}, bf16[288,128]{1,0:T(8,128)(2,1)S(1)}, u32[]{:S(2)}, u32[]{:S(2)}) collective-permute-start(bf16[288,128]{1,0:T(8,128)(2,1)S(1)} %collective-permute-done.14.refs_4_), channel_id=1, source_target_pairs={{0,224},{16,240},{32,0},{48,16},{64,32},{80,48},{96,64},{112,80},{... | collective-permute-start | bytes 221192 | tf_op jit(solution)/shard_map/ppermute | solution.py:380
  139.3 6.1 %collective-permute-start.22 = (bf16[288,128]{1,0:T(8,128)(2,1)S(1)}, bf16[288,128]{1,0:T(8,128)(2,1)S(1)}, u32[]{:S(2)}, u32[]{:S(2)}) collective-permute-start(bf16[288,128]{1,0:T(8,128)(2,1)S(1)} %collective-permute-done.21.refs_14_), channel_id=1, source_target_pairs={{0,32},{16,48},{32,64},{48,80},{64,96},{80,112},{96,128},{112,144}... | collective-permute-start | bytes 221192 | tf_op jit(solution)/shard_map/ppermute | solution.py:379
  140.1 5.6 %collective-permute-start.26 = (bf16[288,128]{1,0:T(8,128)(2,1)S(1)}, bf16[288,128]{1,0:T(8,128)(2,1)S(1)}, u32[]{:S(2)}, u32[]{:S(2)}) collective-permute-start(bf16[288,128]{1,0:T(8,128)(2,1)S(1)} %collective-permute-done.25.refs_17_), channel_id=1, source_target_pairs={{0,32},{16,48},{32,64},{48,80},{64,96},{80,112},{96,128},{112,144}... | collective-permute-start | bytes 221192 | tf_op jit(solution)/shard_map/ppermute | solution.py:379
  140.1 5.6 %collective-permute-start.19 = (bf16[288,128]{1,0:T(8,128)(2,1)S(1)}, bf16[288,128]{1,0:T(8,128)(2,1)S(1)}, u32[]{:S(2)}, u32[]{:S(2)}) collective-permute-start(bf16[288,128]{1,0:T(8,128)(2,1)S(1)} %collective-permute-done.17.refs_7_), channel_id=1, source_target_pairs={{0,224},{16,240},{32,0},{48,16},{64,32},{80,48},{96,64},{112,80},{... | collective-permute-start | bytes 221192 | tf_op jit(solution)/shard_map/ppermute | solution.py:380
  143.4 5.6 %collective-permute-start.18 = (bf16[288,128]{1,0:T(8,128)(2,1)S(1)}, bf16[288,128]{1,0:T(8,128)(2,1)S(1)}, u32[]{:S(2)}, u32[]{:S(2)}) collective-permute-start(bf16[288,128]{1,0:T(8,128)(2,1)S(1)} %collective-permute-done.16.refs_6_), channel_id=1, source_target_pairs={{0,224},{16,240},{32,0},{48,16},{64,32},{80,48},{96,64},{112,80},{... | collective-permute-start | bytes 221192 | tf_op jit(solution)/shard_map/ppermute | solution.py:380
  145.4 5.6 %collective-permute-start.23 = (bf16[288,128]{1,0:T(8,128)(2,1)S(1)}, bf16[288,128]{1,0:T(8,128)(2,1)S(1)}, u32[]{:S(2)}, u32[]{:S(2)}) collective-permute-start(bf16[288,128]{1,0:T(8,128)(2,1)S(1)} %collective-permute-done.22.refs_12_), channel_id=1, source_target_pairs={{0,32},{16,48},{32,64},{48,80},{64,96},{80,112},{96,128},{112,144}... | collective-permute-start | bytes 221192 | tf_op jit(solution)/shard_map/ppermute | solution.py:384
  145.7 6.1 %collective-permute-start.27 = (bf16[288,128]{1,0:T(8,128)(2,1)S(1)}, bf16[288,128]{1,0:T(8,128)(2,1)S(1)}, u32[]{:S(2)}, u32[]{:S(2)}) collective-permute-start(bf16[288,128]{1,0:T(8,128)(2,1)S(1)} %collective-permute-done.26.refs_15_), channel_id=1, source_target_pairs={{0,32},{16,48},{32,64},{48,80},{64,96},{80,112},{96,128},{112,144}... | collective-permute-start | bytes 221192 | tf_op jit(solution)/shard_map/ppermute | solution.py:379
  145.7 6.1 %collective-permute-start.24 = (bf16[288,128]{1,0:T(8,128)(2,1)S(1)}, bf16[288,128]{1,0:T(8,128)(2,1)S(1)}, u32[]{:S(2)}, u32[]{:S(2)}) collective-permute-start(bf16[288,128]{1,0:T(8,128)(2,1)S(1)} %collective-permute-done.19.refs_9_), channel_id=1, source_target_pairs={{0,224},{16,240},{32,0},{48,16},{64,32},{80,48},{96,64},{112,80},{... | collective-permute-start | bytes 221192 | tf_op jit(solution)/shard_map/ppermute | solution.py:385

commit v2 on v1

--- a/solution.py
+++ b/solution.py
@@ -32,6 +32,7 @@
 def params(mib):
     return pltpu.CompilerParams(vmem_limit_bytes=mib * 1024 * 1024)
 
+Z_ORDER = ((0,), (1,), (-1, -2), (2, 3), (-3, -4))
 Y_ORDER = ((0,), (1,), (-1, -2))
 
 ORDER = (5, 4, 2, 3, 7, 6, 0, 1)
@@ -45,6 +46,10 @@
 
 def hbm():
     return pl.BlockSpec(memory_space=pltpu.HBM)
+
+
+def anywhere():
+    return pl.BlockSpec(memory_space=pl.ANY)
 
 
 def smem():
@@ -122,9 +127,9 @@
 
 
 def pack_kernel(
-    me_ref, old_ref, new_ref, cols_ref, master_ref, first_ref, second_ref, table_ref, out_ref, moments_ref, scalars, sem
+    old_ref, new_ref, cols_ref, master_ref, first_ref, second_ref, table_ref, out_ref, moments_ref, scalars, sem
 ):
-    rows = routing_table(me_ref[0], old_ref, new_ref, cols_ref)
+    rows = routing_table(lax.axis_index("tensor"), old_ref, new_ref, cols_ref)
     for i, row in enumerate(rows):
         table_ref[i : i + 1, :] = row.astype(jnp.int32)
     table_ref[len(rows) : 8, :] = jnp.zeros((8 - len(rows), 128), jnp.int32)
@@ -159,8 +164,7 @@
         return carry
 
     lax.fori_loop(0, KEPT, step, 0, unroll=12)
-    for i in range(2 * ZN):
-        copy_ref[i] = scratch[...].astype(BF16)
+    copy_ref[...] = scratch[...].astype(BF16)
 
 
 def place_kernel(
@@ -182,6 +186,11 @@
     lax.fori_loop(0, SLOTS, step, 0, unroll=10)
 
 
+def place_of(axis):
+    index = lax.axis_index(axis)
+    return index // 2, index % 2
+
+
 def assemble(pieces, z, xh, weights):
     for index, piece in enumerate(pieces):
         rel, other = divmod(index, 2)
@@ -190,24 +199,34 @@
         weights[:, at, :] = piece[...].astype(F32).reshape(KEPT, ROWS, B)
 
 
-def assemble_kernel(shards_ref, out_ref, weights):
-    for i in range(2 * ZN):
-        weights[:, i * ROWS : (i + 1) * ROWS, :] = shards_ref[i].astype(F32).reshape(KEPT, ROWS, B)
+def assemble_kernel(*refs):
+    pieces = refs[:5]
+    out_ref, weights = refs[5:]
+    z, xh = place_of("dp")
+    sign = direction(z, lax.axis_index("tensor") % 2)
+    for ref, rels in zip(pieces, Z_ORDER, strict=True):
+        for i, rel in enumerate(rels):
+            for other in range(2):
+                source = lax.rem(z + sign * rel + ZN, ZN) * 2 + lax.rem(xh + other, 2)
+                at = pl.ds(pl.multiple_of(source * ROWS, ROWS), ROWS)
+                weights[:, at, :] = ref[2 * i + other].astype(F32).reshape(KEPT, ROWS, B)
     out_ref[...] = weights[...].astype(BF16)
 
 
 def main_kernel(*refs):
-    table_ref, where_ref, upstream_in, weights_in = refs[:4]
-    token_pieces = refs[4:10]
-    hidden_out = refs[10]
-    keep_out = refs[11:15]
-    send_out = refs[15:18]
+    table_ref, upstream_in, weights = refs[:3]
+    token_pieces = refs[3:9]
+    hidden_out = refs[9]
+    keep_out = refs[10:14]
+    send_out = refs[14:17]
     (
-        tokens_ref, upstream_ref, weights, hidden_ref, local_grad, grads, keep_ref, send_ref,
+        tokens_ref, upstream_ref, hidden_ref, local_grad, grads, keep_ref, send_ref,
         token_sems, side_sems, out_sems,
-    ) = refs[18:]
-    z, xh, sign = where_ref[0], where_ref[1], where_ref[2]
-    y, xl, core, y_sign = where_ref[3], where_ref[4], where_ref[5], where_ref[6]
+    ) = refs[17:]
+    z, xh = place_of("dp")
+    y, rest = lax.axis_index("tensor") // 4, lax.axis_index("tensor") % 4
+    xl, core = rest // 2, rest % 2
+    sign, y_sign = direction(z, core), direction(y, core)
     copies = []
     for index, ref in enumerate(token_pieces):
         other_core, step = divmod(index, 3)
@@ -220,8 +239,7 @@
                         ref.at[2 * i + other_x], tokens_ref.at[owner], token_sems.at[len(copies)]
                     )
                 )
-    copies.append(pltpu.make_async_copy(weights_in, weights, side_sems.at[0]))
-    copies.append(pltpu.make_async_copy(upstream_in, upstream_ref, side_sems.at[1]))
+    copies.append(pltpu.make_async_copy(upstream_in, upstream_ref, side_sems.at[0]))
     for copy in copies:
         copy.start()
     for copy in copies:
@@ -247,7 +265,7 @@
         return carry
 
     lax.fori_loop(0, COLS, forward, 0, unroll=4)
-    hidden_copy = pltpu.make_async_copy(hidden_ref, hidden_out, side_sems.at[2])
+    hidden_copy = pltpu.make_async_copy(hidden_ref, hidden_out, side_sems.at[1])
     hidden_copy.start()
 
     def backward(p, carry):
@@ -332,10 +350,10 @@
 
 
 def final_kernel(*refs):
-    table_ref, where_ref = refs[:2]
-    pieces = refs[2:18]
-    out_ref, weights = refs[18:]
-    assemble(pieces, where_ref[0], where_ref[1], weights)
+    table_ref = refs[0]
+    pieces = refs[1:17]
+    out_ref, weights = refs[17:]
+    assemble(pieces, *place_of("dp"), weights)
 
     def step(s, carry):
         entry = table_ref[RANK, s]
@@ -420,14 +438,6 @@
 
 
 def local(tokens, upstream, master_weights, first_moment, second_moment, old_blocks, new_blocks, new_columns):
-    owner = lax.axis_index("tensor")
-    dp = lax.axis_index("dp")
-    z = dp // 2
-    me = jnp.reshape(owner, (1,)).astype(jnp.int32)
-    core = owner % 2
-    y = owner // 4
-    spots = [z, dp % 2, direction(z, core), y, owner // 2 % 2, core, direction(y, core)]
-    where = jnp.stack(spots).astype(jnp.int32)
     states = [jnp.transpose(a, (1, 0, 2)) for a in (master_weights, first_moment, second_moment)]
 
     swapped = hop(tokens, X_SWAP)
@@ -439,11 +449,11 @@
             sd((OWNERS * KEEP, ROWS, B), F32),
             sd((OWNERS * KEEP, 2, ROWS, B), F32),
         ),
-        in_specs=[smem()] + [vmem()] * 6,
+        in_specs=[vmem()] * 6,
         out_specs=(vmem(),) * 3,
         scratch_shapes=[pltpu.SMEM((8, 128), jnp.int32), pltpu.SemaphoreType.DMA],
         compiler_params=params(56),
-    )(me, old_blocks, new_blocks, new_columns, *states)
+    )(old_blocks, new_blocks, new_columns, *states)
     arrived = lax.all_to_all(packed, "tensor", split_axis=0, concat_axis=0, tiled=True)
 
     arrived, swapped = lax.optimization_barrier((arrived, swapped))
@@ -451,57 +461,60 @@
     near = hop(start, Y_NEAR)
     flat = sd((SLOTS * ROWS, B), F32)
     flat16 = sd((KEPT * ROWS, B), BF16)
-    copies = pl.pallas_call(
+    copy_in = pl.pallas_call(
         copy_in_kernel,
-        out_shape=sd((2 * ZN, KEPT * ROWS, B), BF16),
+        out_shape=flat16,
         in_specs=[smem()] + [vmem()] * 2,
         out_specs=vmem(),
         scratch_shapes=[pltpu.VMEM((KEPT * ROWS, B), F32)],
         compiler_params=params(6),
     )(table, states[0], arrived)
-    shards = lax.all_to_all(copies, "dp", split_axis=0, concat_axis=0, tiled=True)
+    pair = jnp.stack([copy_in, lax.ppermute(copy_in, "dp", SWAP)])
+    shards = [pair, lax.ppermute(pair, AXES, NEAR)]
+    shards.append(lax.ppermute(jnp.concatenate(shards, axis=0), AXES, FAR))
+    shards.append(lax.ppermute(shards[2], AXES, NEAR))
+    shards.append(lax.ppermute(shards[3], AXES, FAR))
 
     def after(value, other):
         return lax.optimization_barrier((value, other))[0]
 
-    far = hop(jnp.concatenate([start, near], axis=0), Y_FAR)
-    mine = [start, near, after(far, shards)]
+    far = hop(jnp.concatenate([start, after(near, shards[1])], axis=0), Y_FAR)
+    mine = [start, near, after(far, shards[4])]
     token_pieces = mine + [hop(a, CORE_SWAP) for a in mine]
 
     weights = pl.pallas_call(
         assemble_kernel,
         out_shape=sd((KEPT, B, B), BF16),
-        in_specs=[vmem()],
+        in_specs=[vmem()] * 5,
         out_specs=vmem(),
         scratch_shapes=[pltpu.VMEM((KEPT, B, B), F32)],
         compiler_params=params(12),
-    )(shards)
+    )(*shards)
     moved_moments = lax.all_to_all(
-        after(packed_moments, shards), "tensor", split_axis=0, concat_axis=0, tiled=True
+        after(packed_moments, shards[4]), "tensor", split_axis=0, concat_axis=0, tiled=True
     )
     pair32 = sd((2, SLOTS * ROWS, B), F32)
     pair16 = sd((2, SLOTS * ROWS, B), BF16)
     hidden_out, *pairs = pl.pallas_call(
         main_kernel,
         out_shape=(sd(upstream.shape, BF16),) + (pair32,) * 4 + (pair16,) * 2 + (sd((4, SLOTS * ROWS, B), BF16),),
-        in_specs=[smem()] * 2 + [hbm()] * 8,
+        in_specs=[smem()] + [hbm(), vmem()] + [anywhere()] * 6,
         out_specs=(hbm(),) * 8,
         scratch_shapes=[
             pltpu.VMEM((OWNERS,) + tokens.shape, BF16),
             pltpu.VMEM(upstream.shape, BF16),
-            pltpu.VMEM((KEPT, B, B), BF16),
             pltpu.VMEM(upstream.shape, BF16),
             pltpu.VMEM((COLS, tokens.shape[0], B), BF16),
             pltpu.VMEM((2 * B, B), F32),
             pltpu.VMEM((ZN, SLOTS * ROWS, B), F32),
             pltpu.VMEM((ZN, SLOTS * ROWS, B), BF16),
             pltpu.SemaphoreType.DMA((OWNERS,)),
-            pltpu.SemaphoreType.DMA((3,)),
+            pltpu.SemaphoreType.DMA((2,)),
             pltpu.SemaphoreType.DMA((3, 8)),
         ],
         compiler_params=params(56),
         cost_estimate=pl.CostEstimate(flops=4 * 10**9, bytes_accessed=2 * 10**7, transcendentals=10**6),
-    )(table, where, upstream, weights, *token_pieces)
+    )(table, upstream, weights, *token_pieces)
     keep, send = pairs[:4], pairs[4:]
 
     moved_moments, keep = lax.optimization_barrier((moved_moments, keep))
@@ -528,11 +541,11 @@
     weight_copy = pl.pallas_call(
         final_kernel,
         out_shape=sd((SLOTS, B, B), BF16),
-        in_specs=[smem()] * 2 + [vmem()] * 16,
+        in_specs=[smem()] + [vmem()] * 16,
         out_specs=vmem(),
         scratch_shapes=[pltpu.VMEM((KEPT, B, B), F32)],
         compiler_params=params(12),
-    )(table, where, *final)
+    )(table, *final)
 
     def back(a):
         return jnp.transpose(a.reshape(SLOTS, -1, B), (1, 0, 2))

time: 157 us -> 151 us (0.962); the launches traced: 155 us -> 150 us
  waiting for transfers between devices: 62.8 us -> 55.5 us
  starting transfers between devices: 48.4 us -> 53.6 us
    all_to_all x2 -> x1, waiting for transfers between devices: 27.6 us -> 0.01 us  [local(): lax.all_to_all(after(packed_moments, shards[4]), 'tensor', split_axis=0,...]
    ppermute x0 -> x5, waiting for transfers between devices: none -> 24.6 us  [the longest x1 6.72 us: local(): shards.append(lax.ppermute(shards[2], AXES, NEAR))]
    ppermute x0 -> x5, starting transfers between devices: none -> 12.5 us  [the longest x1 5.94 us: local(): shards.append(lax.ppermute(jnp.concatenate(shards, axis=0), AXES, FAR))]
    all_to_all x2 -> x1, starting transfers between devices: 16.3 us -> 5.3 us  [local(): lax.all_to_all(after(packed_moments, shards[4]), 'tensor', split_axis=0,...]
    ppermute x1, starting transfers between devices: 4.98 us -> 1.11 us  [gather_pieces(): swapped = lax.ppermute(shard, 'dp', SWAP)]
    ppermute x1, starting transfers between devices: 0.09 us -> 3.37 us  [reduce_chunks(): a = lax.ppermute(total(0), AXES, FAR)]
    ppermute x6, waiting for transfers between devices: 4.31 us -> 1.26 us  [gather_pieces(): up[j] = lax.ppermute(up[j], 'dp', UP)]
    ppermute x3, starting transfers between devices: 7.44 us -> 4.72 us  [reduce_chunks(): got = [lax.ppermute(a, 'dp', SWAP) for a in send]]
  transfers between devices with their start and end apart: 30 -> 34, of which waited for: 15 -> 15; matrix products, arithmetic and copies ran while one was open for 3% -> 2% of each run, Pallas kernels for 12% -> 12%
where the time goes in v2:
time: 151 us; the launch traced here: 150 us
  waiting for transfers between devices  55.5 us (37%)
  starting transfers between devices  53.6 us (35%)
  Pallas kernels  22.5 us (15%)
  blocking collectives  11.9 us (8%)
  other arithmetic  4.78 us (3%)
    ppermute x3, waiting for transfers between devices, reduce_chunks(): got = [lax.ppermute(a, 'dp', SWAP) for a in send]  12.2 us
    pallas_call x1, Pallas kernels, local(): pl.pallas_call(main_kernel, out_shape=(sd(upstream.shape, BF16),) + (pair...  12.1 us
    ppermute x6, starting transfers between devices, gather_pieces(): down[j] = lax.ppermute(down[j], 'dp', DOWN)  12 us
    all_to_all x1, blocking collectives, local(): lax.all_to_all(packed, 'tensor', split_axis=0, concat_axis=0, tiled=True)  11.9 us
    ppermute x1, waiting for transfers between devices, local(): shards.append(lax.ppermute(shards[2], AXES, NEAR))  6.72 us
    ppermute x1, starting transfers between devices, local(): shards.append(lax.ppermute(jnp.concatenate(shards, axis=0), AXES, FAR))  5.94 us
    all_to_all x1, starting transfers between devices, local(): lax.all_to_all(after(packed_moments, shards[4]), 'tensor', split_axis=0,...  5.3 us
    ppermute x1, waiting for transfers between devices, local(): pair = jnp.stack([copy_in, lax.ppermute(copy_in, 'dp', SWAP)])  5.24 us
  transfers between devices with their start and end apart: 34, of which 15 were waited for; matrix products, arithmetic and copies ran while one was open for 2% of the time, Pallas kernels for 12%

profile of v2, /device:TPU:6, one launch (start us, length us, event | category | flops | bytes accessed | tf_op | source)
XLA Modules:
  0.0 150.2 jit_solution(761837753128939995)
XLA Ops:
  0.6 0.9 collective-permute-start
  1.6 3.2 %shard_map.119 = (s32[8,128]{1,0:T(8,128)}, f32[48,8,128]{2,1,0:T(8,128)}, f32[48,2,8,128]{3,2,1,0:T(8,128)}) custom-call(s32[16,60]{1,0:T(8,128)} %old_ref.1, s32[16,60]{1,0:T(8,128)} %new_ref.1, s32[16,12]{1,0:T(8,128)} %cols_ref.1, f32[60,8,128]{2,1,0:T(8,128)} %bitcast.19, f32[60,8,128]{2,1,0:T(8,128)} %bitcast.22, f32[60,8,128]{2,1,0:T(8,128)} %bitcast.24), custom_call_target="tpu_custom_call" | custom-call | tf_op jit(solution)/shard_map/pallas_call | solution.py:445
  4.8 0.0 copy-start.5
  4.8 0.0 copy-start.7
  4.8 11.9 %all_to_all.10.arrived_ref = f32[48,8,128]{2,1,0:T(8,128)S(1)} all-to-all(f32[48,8,128]{2,1,0:T(8,128)} %get-tuple-element.35), channel_id=1, replica_groups=mesh['dp'=16,'tensor'=16] {'tensor'}, dimensions={0} | all-to-all | bytes 393216 | tf_op jit(solution)/shard_map/all_to_all | solution.py:457
  16.7 1.1 pad_maximum_fusion.1.refs_3_
  17.8 0.3 collective-permute-start.6
  18.1 0.8 shard_map.120
  19.0 1.2 collective-permute-start.1
  20.2 5.2 %collective-permute-done.1 = bf16[288,128]{1,0:T(8,128)(2,1)S(1)} collective-permute-done((bf16[288,128]{1,0:T(8,128)(2,1)S(1)}, bf16[288,128]{1,0:T(8,128)(2,1)S(1)}, u32[]{:S(2)}, u32[]{:S(2)}) %collective-permute-start.1) | collective-permute-done | bytes 73760 | tf_op jit(solution)/shard_map/ppermute | solution.py:472
  25.5 2.0 %collective-permute-start.2 = (bf16[2,288,128]{2,1,0:T(8,128)(2,1)S(1)}, bf16[2,288,128]{2,1,0:T(8,128)(2,1)S(1)}, u32[]{:S(2)}, u32[]{:S(2)}) collective-permute-start(bf16[2,288,128]{2,1,0:T(8,128)(2,1)S(1)} %pad_maximum_fusion.3.refs_0_), channel_id=1, source_target_pairs={{0,32},{1,225},{2,34},{3,227},{4,36},{5,229},{6,38},{7,231},{8,40}... | collective-permute-start | bytes 442376 | tf_op jit(solution)/shard_map/ppermute | solution.py:473
  27.5 3.2 %collective-permute-done.2.refs_1_ = bf16[2,288,128]{2,1,0:T(8,128)(2,1)S(1)} collective-permute-done((bf16[2,288,128]{2,1,0:T(8,128)(2,1)S(1)}, bf16[2,288,128]{2,1,0:T(8,128)(2,1)S(1)}, u32[]{:S(2)}, u32[]{:S(2)}) %collective-permute-start.2) | collective-permute-done | bytes 147488 | tf_op jit(solution)/shard_map/ppermute | solution.py:473
  30.7 1.3 pad_maximum_fusion
  32.0 1.3 collective-permute-start.7
  33.3 5.9 %collective-permute-start.3 = (bf16[4,288,128]{2,1,0:T(8,128)(2,1)S(1)}, bf16[4,288,128]{2,1,0:T(8,128)(2,1)S(1)}, u32[]{:S(2)}, u32[]{:S(2)}) collective-permute-start(bf16[4,288,128]{2,1,0:T(8,128)(2,1)S(1)} %pad_maximum_fusion.2), channel_id=1, source_target_pairs={{0,224},{1,33},{2,226},{3,35},{4,228},{5,37},{6,230},{7,39},{8,232... | collective-permute-start | bytes 884744 | tf_op jit(solution)/shard_map/ppermute | solution.py:474
  39.3 4.7 %collective-permute-done.3.refs_2_ = bf16[4,288,128]{2,1,0:T(8,128)(2,1)S(1)} collective-permute-done((bf16[4,288,128]{2,1,0:T(8,128)(2,1)S(1)}, bf16[4,288,128]{2,1,0:T(8,128)(2,1)S(1)}, u32[]{:S(2)}, u32[]{:S(2)}) %collective-permute-start.3) | collective-permute-done | bytes 294944 | tf_op jit(solution)/shard_map/ppermute | solution.py:474
  44.0 6.7 %collective-permute-done.4.refs_3_ = bf16[4,288,128]{2,1,0:T(8,128)(2,1)S(1)} collective-permute-done((bf16[4,288,128]{2,1,0:T(8,128)(2,1)S(1)}, bf16[4,288,128]{2,1,0:T(8,128)(2,1)S(1)}, u32[]{:S(2)}, u32[]{:S(2)}) %collective-permute-start.4) | collective-permute-done | bytes 294944 | tf_op jit(solution)/shard_map/ppermute | solution.py:475
  50.7 3.3 %collective-permute-start.5 = (bf16[4,288,128]{2,1,0:T(8,128)(2,1)S(1)}, bf16[4,288,128]{2,1,0:T(8,128)(2,1)S(1)}, u32[]{:S(2)}, u32[]{:S(2)}) collective-permute-start(bf16[4,288,128]{2,1,0:T(8,128)(2,1)S(1)} %collective-permute-done.4.refs_3_), channel_id=1, source_target_pairs={{0,224},{1,33},{2,226},{3,35},{4,228},{5,37},{6,230},{7,39},{8,232... | collective-permute-start | bytes 884744 | tf_op jit(solution)/shard_map/ppermute | solution.py:476
  54.0 4.7 %collective-permute-done.5.refs_4_ = bf16[4,288,128]{2,1,0:T(8,128)(2,1)S(1)} collective-permute-done((bf16[4,288,128]{2,1,0:T(8,128)(2,1)S(1)}, bf16[4,288,128]{2,1,0:T(8,128)(2,1)S(1)}, u32[]{:S(2)}, u32[]{:S(2)}) %collective-permute-start.5) | collective-permute-done | bytes 294944 | tf_op jit(solution)/shard_map/ppermute | solution.py:476
  58.7 0.5 collective-permute-start.8
  59.2 0.1 collective-permute-start.9
  59.3 5.3 %all-to-all-start.1 = ((f32[48,2,8,128]{3,2,1,0:T(8,128)}), f32[48,2,8,128]{3,2,1,0:T(8,128)S(1)}, u32[]{:S(2)}, u32[]{:S(2)}) async-start(f32[48,2,8,128]{3,2,1,0:T(8,128)} %get-tuple-element.42), calls=%async_computation.1 | async-start | bytes 786432 | tf_op jit(solution)/shard_map/all_to_all | solution.py:493
  64.6 0.4 shard_map.121.refs_2_
  65.1 0.0 copy-start.1
  65.1 1.0 copy-done.1
  66.1 12.1 %shard_map.122 = (bf16[512,1536]{1,0:T(8,128)(2,1)}, f32[2,480,128]{2,1,0:T(8,128)}, f32[2,480,128]{2,1,0:T(8,128)}, f32[2,480,128]{2,1,0:T(8,128)}, f32[2,480,1...) custom-call(s32[8,128]{1,0:T(8,128)} %get-tuple-element.34.table_ref.re, ...), custom_call_target="tpu_custom_call" | custom-call | flops 4000000000 | bytes 20000000 | tf_op jit(solution)/shard_map/pallas_call | solution.py:498
  78.2 1.2 collective-permute-start.13
  79.5 2.4 %collective-permute-start.12 = (bf16[2,480,128]{2,1,0:T(8,128)(2,1)}, bf16[2,480,128]{2,1,0:T(8,128)(2,1)S(1)}, u32[]{:S(2)}, u32[]{:S(2)}) collective-permute-start(bf16[2,480,128]{2,1,0:T(8,128)(2,1)} %get-tuple-element.51), channel_id=1, source_target_pairs={{0,16},{16,0},{32,48},{48,32},{64,80},{80,64},{96,112},{112,96},{1... | collective-permute-start | bytes 737288 | tf_op jit(solution)/shard_map/ppermute | solution.py:426
  81.8 7.0 %collective-permute-done.13 = bf16[2,480,128]{2,1,0:T(8,128)(2,1)S(1)} collective-permute-done((bf16[2,480,128]{2,1,0:T(8,128)(2,1)}, bf16[2,480,128]{2,1,0:T(8,128)(2,1)S(1)}, u32[]{:S(2)}, u32[]{:S(2)}) %collective-permute-start.13) | collective-permute-done | bytes 245792 | tf_op jit(solution)/shard_map/ppermute | solution.py:426
  88.8 1.1 add_convert_fusion.2
  89.9 3.4 %collective-permute-start.14 = (bf16[2,480,128]{2,1,0:T(8,128)(2,1)S(1)}, bf16[2,480,128]{2,1,0:T(8,128)(2,1)S(1)}, u32[]{:S(2)}, u32[]{:S(2)}) collective-permute-start(bf16[2,480,128]{2,1,0:T(8,128)(2,1)S(1)} %add_convert_fusion.2), channel_id=1, source_target_pairs={{0,224},{1,33},{2,226},{3,35},{4,228},{5,37},{6,230},{7,39},{8,232... | collective-permute-start | bytes 737288 | tf_op jit(solution)/shard_map/ppermute | solution.py:433
  93.3 1.1 collective-permute-start.11
  94.4 3.1 %collective-permute-done.14 = bf16[2,480,128]{2,1,0:T(8,128)(2,1)S(1)} collective-permute-done((bf16[2,480,128]{2,1,0:T(8,128)(2,1)S(1)}, bf16[2,480,128]{2,1,0:T(8,128)(2,1)S(1)}, u32[]{:S(2)}, u32[]{:S(2)}) %collective-permute-start.14) | collective-permute-done | bytes 245792 | tf_op jit(solution)/shard_map/ppermute | solution.py:433
  97.5 1.1 add_convert_fusion.1
  98.6 0.1 collective-permute-start.15
  98.7 5.2 %collective-permute-done.11 = bf16[4,480,128]{2,1,0:T(8,128)(2,1)S(1)} collective-permute-done((bf16[4,480,128]{2,1,0:T(8,128)(2,1)}, bf16[4,480,128]{2,1,0:T(8,128)(2,1)S(1)}, u32[]{:S(2)}, u32[]{:S(2)}) %collective-permute-start.11) | collective-permute-done | bytes 491552 | tf_op jit(solution)/shard_map/ppermute | solution.py:426
  103.9 1.0 collective-permute-done.15
  104.9 0.1 add_convert_fusion
  105.0 3.3 %collective-permute-start.16 = (bf16[2,480,128]{2,1,0:T(8,128)(2,1)S(1)}, bf16[2,480,128]{2,1,0:T(8,128)(2,1)S(1)}, u32[]{:S(2)}, u32[]{:S(2)}) collective-permute-start(bf16[2,480,128]{2,1,0:T(8,128)(2,1)S(1)} %add_convert_fusion), channel_id=1, source_target_pairs={{0,224},{1,33},{2,226},{3,35},{4,228},{5,37},{6,230},{7,39},{8,232... | collective-permute-start | bytes 737288 | tf_op jit(solution)/shard_map/ppermute | solution.py:435
  108.3 4.2 %collective-permute-done.16.near_ref = bf16[2,480,128]{2,1,0:T(8,128)(2,1)S(1)} collective-permute-done((bf16[2,480,128]{2,1,0:T(8,128)(2,1)S(1)}, bf16[2,480,128]{2,1,0:T(8,128)(2,1)S(1)}, u32[]{:S(2)}, u32[]{:S(2)}) %collective-permute-start.16) | collective-permute-done | bytes 245792 | tf_op jit(solution)/shard_map/ppermute | solution.py:435
  112.5 0.1 collective-permute-start.17
  112.6 1.2 shard_map.123
  113.9 3.6 %collective-permute-done.17.last_ref = bf16[480,128]{1,0:T(8,128)(2,1)S(1)} collective-permute-done((bf16[480,128]{1,0:T(8,128)(2,1)S(1)}, bf16[480,128]{1,0:T(8,128)(2,1)S(1)}, u32[]{:S(2)}, u32[]{:S(2)}) %collective-permute-start.17) | collective-permute-done | bytes 122912 | tf_op jit(solution)/shard_map/ppermute | solution.py:436
  117.5 1.8 %shard_map.124 = (f32[480,128]{1,0:T(8,128)}, f32[480,128]{1,0:T(8,128)}, f32[480,128]{1,0:T(8,128)}, bf16[288,128]{1,0:T(8,128)(2,1)S(1)}) custom-call(s32[8,128]{1,0:T(8,128)S(1)} %copy-done.6, f32[2,480,128]{2,1,0:T(8,128)S(1)} %copy-done.2, bf16[2,480,128]{2,1,0:T(8,128)(2,1)S(1)} %slice.12.got_ref, ...), custom_call_target="tpu_custom_call" | custom-call | tf_op jit(solution)/shard_map/pallas_call | solution.py:531
  119.3 1.1 collective-permute-start.18
  120.4 0.0 collective-permute-start.25
  120.4 4.7 %collective-permute-done.18.refs_2_ = bf16[288,128]{1,0:T(8,128)(2,1)S(1)} collective-permute-done((bf16[288,128]{1,0:T(8,128)(2,1)S(1)}, bf16[288,128]{1,0:T(8,128)(2,1)S(1)}, u32[]{:S(2)}, u32[]{:S(2)}) %collective-permute-start.18) | collective-permute-done | bytes 73760 | tf_op jit(solution)/shard_map/ppermute | solution.py:391
  125.2 3.2 %collective-permute-start.20 = (bf16[288,128]{1,0:T(8,128)(2,1)S(1)}, bf16[288,128]{1,0:T(8,128)(2,1)S(1)}, u32[]{:S(2)}, u32[]{:S(2)}) collective-permute-start(bf16[288,128]{1,0:T(8,128)(2,1)S(1)} %collective-permute-done.18.refs_2_), channel_id=1, source_target_pairs={{0,224},{16,240},{32,0},{48,16},{64,32},{80,48},{96,64},{112,80},{... | collective-permute-start | bytes 221192 | tf_op jit(solution)/shard_map/ppermute | solution.py:398
  128.4 0.0 collective-permute-start.19
  128.4 2.0 %collective-permute-start.26 = (bf16[288,128]{1,0:T(8,128)(2,1)S(1)}, bf16[288,128]{1,0:T(8,128)(2,1)S(1)}, u32[]{:S(2)}, u32[]{:S(2)}) collective-permute-start(bf16[288,128]{1,0:T(8,128)(2,1)S(1)} %collective-permute-done.25.refs_15_), channel_id=1, source_target_pairs={{0,32},{16,48},{32,64},{48,80},{64,96},{80,112},{96,128},{112,144}... | collective-permute-start | bytes 221192 | tf_op jit(solution)/shard_map/ppermute | solution.py:397
  130.4 0.0 collective-permute-start.30
  130.4 0.1 collective-permute-done.20.refs_4_
  130.5 3.7 %collective-permute-start.22 = (bf16[288,128]{1,0:T(8,128)(2,1)S(1)}, bf16[288,128]{1,0:T(8,128)(2,1)S(1)}, u32[]{:S(2)}, u32[]{:S(2)}) collective-permute-start(bf16[288,128]{1,0:T(8,128)(2,1)S(1)} %collective-permute-done.20.refs_4_), channel_id=1, source_target_pairs={{0,224},{16,240},{32,0},{48,16},{64,32},{80,48},{96,64},{112,80},{... | collective-permute-start | bytes 221192 | tf_op jit(solution)/shard_map/ppermute | solution.py:398
  134.2 0.8 collective-permute-start.21
  135.0 1.2 collective-permute-start.27
  136.3 0.1 collective-permute-start.31
  136.4 3.4 %collective-permute-start.24 = (bf16[288,128]{1,0:T(8,128)(2,1)S(1)}, bf16[288,128]{1,0:T(8,128)(2,1)S(1)}, u32[]{:S(2)}, u32[]{:S(2)}) collective-permute-start(bf16[288,128]{1,0:T(8,128)(2,1)S(1)} %collective-permute-done.22.refs_6_), channel_id=1, source_target_pairs={{0,224},{16,240},{32,0},{48,16},{64,32},{80,48},{96,64},{112,80},{... | collective-permute-start | bytes 221192 | tf_op jit(solution)/shard_map/ppermute | solution.py:398
  139.8 0.8 collective-permute-start.23
  140.6 1.2 collective-permute-start.28
  141.8 0.1 collective-permute-start.32
  141.9 3.4 %collective-permute-start.29 = (bf16[288,128]{1,0:T(8,128)(2,1)S(1)}, bf16[288,128]{1,0:T(8,128)(2,1)S(1)}, u32[]{:S(2)}, u32[]{:S(2)}) collective-permute-start(bf16[288,128]{1,0:T(8,128)(2,1)S(1)} %collective-permute-done.24.refs_8_), channel_id=1, source_target_pairs={{0,224},{16,240},{32,0},{48,16},{64,32},{80,48},{96,64},{112,80},{... | collective-permute-start | bytes 221192 | tf_op jit(solution)/shard_map/ppermute | solution.py:403
  145.4 0.8 collective-permute-done.28.refs_9_
  146.2 1.2 collective-permute-done.32.refs_12_
  147.4 2.8 %shard_map.125 = bf16[60,128,128]{2,1,0:T(8,128)(2,1)} custom-call(s32[8,128]{1,0:T(8,128)S(1)} %copy-done.6, bf16[288,128]{1,0:T(8,128)(2,1)S(1)} %get-tuple-element.62.refs_1_, bf16[288,128]{1,0:T(8,128)(2,1)S(1)} %collective-permute-done.18.refs_2_, bf16[288,128]{1,0:T(8,128)(2,1)S(1)} %collective-permute-done.19.refs_3_, ...), custom_call_target="tpu_custom_call" | custom-call | tf_op jit(solution)/shard_map/pallas_call | solution.py:541
  (41 shorter events, 0.2 us)
Async XLA Ops:
  0.6 17.5 %copy-start = (f32[8,60,128]{2,0,1:T(8,128)S(1)}, f32[8,60,128]{2,0,1:T(8,128)}, u32[]{:S(2)}) copy-start(f32[8,60,128]{2,0,1:T(8,128)} %param.10) | copy-start | bytes 737284
  0.6 16.1 %collective-permute-start = (bf16[512,384]{1,0:T(8,128)(2,1)}, bf16[512,384]{1,0:T(8,128)(2,1)S(1)}, u32[]{:S(2)}, u32[]{:S(2)}) collective-permute-start(bf16[512,384]{1,0:T(8,128)(2,1)} %param.8), channel_id=1, source_target_pairs={{0,2},{1,3},{2,0},{3,1},{4,6},{5,7},{6,4},{7,5},{8,10},{9,11},{10,... | collective-permute-start | bytes 1179656 | tf_op jit(solution)/shard_map/ppermute | solution.py:422
  4.8 13.3 %copy-start.5 = (s32[8,128]{1,0:T(8,128)S(1)}, s32[8,128]{1,0:T(8,128)}, u32[]{:S(2)}) copy-start(s32[8,128]{1,0:T(8,128)} %get-tuple-element.34.table_ref.refs_0_) | copy-start | bytes 12292
  4.8 25.9 %copy-start.7 = (bf16[512,384]{1,0:T(8,128)(2,1)S(1)}, bf16[512,384]{1,0:T(8,128)(2,1)}, u32[]{:S(2)}) copy-start(bf16[512,384]{1,0:T(8,128)(2,1)} %param.8) | copy-start | bytes 1179652
  17.8 40.9 %copy-start.8 = (bf16[2,512,384]{2,1,0:T(8,128)(2,1)}, bf16[2,512,384]{2,1,0:T(8,128)(2,1)S(1)}, u32[]{:S(2)}) copy-start(bf16[2,512,384]{2,1,0:T(8,128)(2,1)S(1)} %pad_maximum_fusion.1.refs_3_) | copy-start | bytes 2359300
  17.8 12.8 %collective-permute-start.6 = (bf16[2,512,384]{2,1,0:T(8,128)(2,1)S(1)}, bf16[2,512,384]{2,1,0:T(8,128)(2,1)}, u32[]{:S(2)}, u32[]{:S(2)}) collective-permute-start(bf16[2,512,384]{2,1,0:T(8,128)(2,1)S(1)} %pad_maximum_fusion.1.refs_3_), channel_id=1, source_target_pairs={{0,4},{1,13},{2,6},{3,15},{4,0},{5,9},{6,2},{7,11},{8,12},{9,5},{1... | collective-permute-start | bytes 2359304 | tf_op jit(solution)/shard_map/ppermute | solution.py:422
  19.0 6.5 %collective-permute-start.1 = (bf16[288,128]{1,0:T(8,128)(2,1)S(1)}, bf16[288,128]{1,0:T(8,128)(2,1)S(1)}, u32[]{:S(2)}, u32[]{:S(2)}) collective-permute-start(bf16[288,128]{1,0:T(8,128)(2,1)S(1)} %shard_map.120), channel_id=1, source_target_pairs={{0,16},{16,0},{32,48},{48,32},{64,80},{80,64},{96,112},{112,96},{1... | collective-permute-start | bytes 221192 | tf_op jit(solution)/shard_map/ppermute | solution.py:472
  25.5 5.2 %collective-permute-start.2 = (bf16[2,288,128]{2,1,0:T(8,128)(2,1)S(1)}, bf16[2,288,128]{2,1,0:T(8,128)(2,1)S(1)}, u32[]{:S(2)}, u32[]{:S(2)}) collective-permute-start(bf16[2,288,128]{2,1,0:T(8,128)(2,1)S(1)} %pad_maximum_fusion.3.refs_0_), channel_id=1, source_target_pairs={{0,32},{1,225},{2,34},{3,227},{4,36},{5,229},{6,38},{7,231},{8,40}... | collective-permute-start | bytes 442376 | tf_op jit(solution)/shard_map/ppermute | solution.py:473
  32.0 26.7 %collective-permute-start.7 = (bf16[4,512,384]{2,1,0:T(8,128)(2,1)S(1)}, bf16[4,512,384]{2,1,0:T(8,128)(2,1)}, u32[]{:S(2)}, u32[]{:S(2)}) collective-permute-start(bf16[4,512,384]{2,1,0:T(8,128)(2,1)S(1)} %pad_maximum_fusion), channel_id=1, source_target_pairs={{0,12},{1,5},{2,14},{3,7},{4,8},{5,1},{6,10},{7,3},{8,4},{9,13},{1... | collective-permute-start | bytes 4718600 | tf_op jit(solution)/shard_map/ppermute | solution.py:422
  33.3 10.6 %collective-permute-start.3 = (bf16[4,288,128]{2,1,0:T(8,128)(2,1)S(1)}, bf16[4,288,128]{2,1,0:T(8,128)(2,1)S(1)}, u32[]{:S(2)}, u32[]{:S(2)}) collective-permute-start(bf16[4,288,128]{2,1,0:T(8,128)(2,1)S(1)} %pad_maximum_fusion.2), channel_id=1, source_target_pairs={{0,224},{1,33},{2,226},{3,35},{4,228},{5,37},{6,230},{7,39},{8,232... | collective-permute-start | bytes 884744 | tf_op jit(solution)/shard_map/ppermute | solution.py:474
  44.0 6.7 %collective-permute-start.4 = (bf16[4,288,128]{2,1,0:T(8,128)(2,1)S(1)}, bf16[4,288,128]{2,1,0:T(8,128)(2,1)S(1)}, u32[]{:S(2)}, u32[]{:S(2)}) collective-permute-start(bf16[4,288,128]{2,1,0:T(8,128)(2,1)S(1)} %collective-permute-done.3.refs_2_), channel_id=1, source_target_pairs={{0,32},{1,225},{2,34},{3,227},{4,36},{5,229},{6,38},{7,231},{8,40}... | collective-permute-start | bytes 884744 | tf_op jit(solution)/shard_map/ppermute | solution.py:475
  50.7 8.0 %collective-permute-start.5 = (bf16[4,288,128]{2,1,0:T(8,128)(2,1)S(1)}, bf16[4,288,128]{2,1,0:T(8,128)(2,1)S(1)}, u32[]{:S(2)}, u32[]{:S(2)}) collective-permute-start(bf16[4,288,128]{2,1,0:T(8,128)(2,1)S(1)} %collective-permute-done.4.refs_3_), channel_id=1, source_target_pairs={{0,224},{1,33},{2,226},{3,35},{4,228},{5,37},{6,230},{7,39},{8,232... | collective-permute-start | bytes 884744 | tf_op jit(solution)/shard_map/ppermute | solution.py:476
  58.7 7.4 %collective-permute-start.10 = (bf16[4,512,384]{2,1,0:T(8,128)(2,1)}, bf16[4,512,384]{2,1,0:T(8,128)(2,1)}, u32[]{:S(2)}, u32[]{:S(2)}) collective-permute-start(bf16[4,512,384]{2,1,0:T(8,128)(2,1)} %collective-permute-done.7.refs_5_), channel_id=1, source_target_pairs={{0,1},{1,0},{2,3},{3,2},{4,5},{5,4},{6,7},{7,6},{8,9},{9,8},{10,11... | collective-permute-start | bytes 4718600 | tf_op jit(solution)/shard_map/ppermute | solution.py:422
  58.7 7.3 %collective-permute-start.8 = (bf16[2,512,384]{2,1,0:T(8,128)(2,1)S(1)}, bf16[2,512,384]{2,1,0:T(8,128)(2,1)}, u32[]{:S(2)}, u32[]{:S(2)}) collective-permute-start(bf16[2,512,384]{2,1,0:T(8,128)(2,1)S(1)} %pad_maximum_fusion.1.refs_3_), channel_id=1, source_target_pairs={{0,1},{1,0},{2,3},{3,2},{4,5},{5,4},{6,7},{7,6},{8,9},{9,8},{10,11... | collective-permute-start | bytes 2359304 | tf_op jit(solution)/shard_map/ppermute | solution.py:422
  59.2 6.8 %collective-permute-start.9 = (bf16[2,512,384]{2,1,0:T(8,128)(2,1)}, bf16[2,512,384]{2,1,0:T(8,128)(2,1)}, u32[]{:S(2)}, u32[]{:S(2)}) collective-permute-start(bf16[2,512,384]{2,1,0:T(8,128)(2,1)} %collective-permute-done.6.refs_4_), channel_id=1, source_target_pairs={{0,1},{1,0},{2,3},{3,2},{4,5},{5,4},{6,7},{7,6},{8,9},{9,8},{10,11... | collective-permute-start | bytes 2359304 | tf_op jit(solution)/shard_map/ppermute | solution.py:422
  59.3 20.1 %all-to-all-start.1 = ((f32[48,2,8,128]{3,2,1,0:T(8,128)}), f32[48,2,8,128]{3,2,1,0:T(8,128)S(1)}, u32[]{:S(2)}, u32[]{:S(2)}) async-start(f32[48,2,8,128]{3,2,1,0:T(8,128)} %get-tuple-element.42), calls=%async_computation.1 | async-start | bytes 786432 | tf_op jit(solution)/shard_map/all_to_all | solution.py:493
  65.1 1.0 copy-start.1
  78.2 26.6 %copy-start.9 = (f32[2,480,128]{2,1,0:T(8,128)S(1)}, f32[2,480,128]{2,1,0:T(8,128)}, u32[]{:S(2)}) copy-start(f32[2,480,128]{2,1,0:T(8,128)} %get-tuple-element.49) | copy-start | bytes 1474564
  78.2 10.6 %collective-permute-start.13 = (bf16[2,480,128]{2,1,0:T(8,128)(2,1)}, bf16[2,480,128]{2,1,0:T(8,128)(2,1)S(1)}, u32[]{:S(2)}, u32[]{:S(2)}) collective-permute-start(bf16[2,480,128]{2,1,0:T(8,128)(2,1)} %get-tuple-element.53), channel_id=1, source_target_pairs={{0,16},{16,0},{32,48},{48,32},{64,80},{80,64},{96,112},{112,96},{1... | collective-permute-start | bytes 737288 | tf_op jit(solution)/shard_map/ppermute | solution.py:426
  79.5 14.9 %collective-permute-start.12 = (bf16[2,480,128]{2,1,0:T(8,128)(2,1)}, bf16[2,480,128]{2,1,0:T(8,128)(2,1)S(1)}, u32[]{:S(2)}, u32[]{:S(2)}) collective-permute-start(bf16[2,480,128]{2,1,0:T(8,128)(2,1)} %get-tuple-element.51), channel_id=1, source_target_pairs={{0,16},{16,0},{32,48},{48,32},{64,80},{80,64},{96,112},{112,96},{1... | collective-permute-start | bytes 737288 | tf_op jit(solution)/shard_map/ppermute | solution.py:426
  89.9 22.5 %copy-start.2 = (f32[2,480,128]{2,1,0:T(8,128)S(1)}, f32[2,480,128]{2,1,0:T(8,128)}, u32[]{:S(2)}) copy-start(f32[2,480,128]{2,1,0:T(8,128)} %get-tuple-element.47.own_ref) | copy-start | bytes 1474564
  89.9 7.5 %collective-permute-start.14 = (bf16[2,480,128]{2,1,0:T(8,128)(2,1)S(1)}, bf16[2,480,128]{2,1,0:T(8,128)(2,1)S(1)}, u32[]{:S(2)}, u32[]{:S(2)}) collective-permute-start(bf16[2,480,128]{2,1,0:T(8,128)(2,1)S(1)} %add_convert_fusion.2), channel_id=1, source_target_pairs={{0,224},{1,33},{2,226},{3,35},{4,228},{5,37},{6,230},{7,39},{8,232... | collective-permute-start | bytes 737288 | tf_op jit(solution)/shard_map/ppermute | solution.py:433
  93.3 19.3 %copy-start.3 = (f32[8,60,128]{2,0,1:T(8,128)S(1)}, f32[8,60,128]{2,0,1:T(8,128)}, u32[]{:S(2)}) copy-start(f32[8,60,128]{2,0,1:T(8,128)} %param.11) | copy-start | bytes 737284
  93.3 19.3 %copy-start.4 = (f32[8,60,128]{2,0,1:T(8,128)S(1)}, f32[8,60,128]{2,0,1:T(8,128)}, u32[]{:S(2)}) copy-start(f32[8,60,128]{2,0,1:T(8,128)} %param.12) | copy-start | bytes 737284
  93.3 19.3 %copy-start.6 = (s32[8,128]{1,0:T(8,128)S(1)}, s32[8,128]{1,0:T(8,128)}, u32[]{:S(2)}) copy-start(s32[8,128]{1,0:T(8,128)} %get-tuple-element.34.table_ref.refs_0_) | copy-start | bytes 12292
  93.3 10.6 %collective-permute-start.11 = (bf16[4,480,128]{2,1,0:T(8,128)(2,1)}, bf16[4,480,128]{2,1,0:T(8,128)(2,1)S(1)}, u32[]{:S(2)}, u32[]{:S(2)}) collective-permute-start(bf16[4,480,128]{2,1,0:T(8,128)(2,1)} %get-tuple-element.48), channel_id=1, source_target_pairs={{0,16},{16,0},{32,48},{48,32},{64,80},{80,64},{96,112},{112,96},{1... | collective-permute-start | bytes 1474568 | tf_op jit(solution)/shard_map/ppermute | solution.py:426
  98.6 6.3 %collective-permute-start.15 = (bf16[2,480,128]{2,1,0:T(8,128)(2,1)S(1)}, bf16[2,480,128]{2,1,0:T(8,128)(2,1)S(1)}, u32[]{:S(2)}, u32[]{:S(2)}) collective-permute-start(bf16[2,480,128]{2,1,0:T(8,128)(2,1)S(1)} %add_convert_fusion.1), channel_id=1, source_target_pairs={{0,32},{1,225},{2,34},{3,227},{4,36},{5,229},{6,38},{7,231},{8,40}... | collective-permute-start | bytes 737288 | tf_op jit(solution)/shard_map/ppermute | solution.py:434
  105.0 7.5 %collective-permute-start.16 = (bf16[2,480,128]{2,1,0:T(8,128)(2,1)S(1)}, bf16[2,480,128]{2,1,0:T(8,128)(2,1)S(1)}, u32[]{:S(2)}, u32[]{:S(2)}) collective-permute-start(bf16[2,480,128]{2,1,0:T(8,128)(2,1)S(1)} %add_convert_fusion), channel_id=1, source_target_pairs={{0,224},{1,33},{2,226},{3,35},{4,228},{5,37},{6,230},{7,39},{8,232... | collective-permute-start | bytes 737288 | tf_op jit(solution)/shard_map/ppermute | solution.py:435
  112.5 5.0 %collective-permute-start.17 = (bf16[480,128]{1,0:T(8,128)(2,1)S(1)}, bf16[480,128]{1,0:T(8,128)(2,1)S(1)}, u32[]{:S(2)}, u32[]{:S(2)}) collective-permute-start(bf16[480,128]{1,0:T(8,128)(2,1)S(1)} %fusion.2), channel_id=1, source_target_pairs={{0,32},{1,225},{2,34},{3,227},{4,36},{5,229},{6,38},{7,231},{8,40}... | collective-permute-start | bytes 368648 | tf_op jit(solution)/shard_map/ppermute | solution.py:436
  119.3 5.9 %collective-permute-start.18 = (bf16[288,128]{1,0:T(8,128)(2,1)S(1)}, bf16[288,128]{1,0:T(8,128)(2,1)S(1)}, u32[]{:S(2)}, u32[]{:S(2)}) collective-permute-start(bf16[288,128]{1,0:T(8,128)(2,1)S(1)} %get-tuple-element.62.refs_1_), channel_id=1, source_target_pairs={{0,16},{16,0},{32,48},{48,32},{64,80},{80,64},{96,112},{112,96},{1... | collective-permute-start | bytes 221192 | tf_op jit(solution)/shard_map/ppermute | solution.py:391
  120.4 8.0 %collective-permute-start.25 = (bf16[288,128]{1,0:T(8,128)(2,1)S(1)}, bf16[288,128]{1,0:T(8,128)(2,1)S(1)}, u32[]{:S(2)}, u32[]{:S(2)}) collective-permute-start(bf16[288,128]{1,0:T(8,128)(2,1)S(1)} %get-tuple-element.62.refs_1_), channel_id=1, source_target_pairs={{0,32},{16,48},{32,64},{48,80},{64,96},{80,112},{96,128},{112,144}... | collective-permute-start | bytes 221192 | tf_op jit(solution)/shard_map/ppermute | solution.py:397
  125.2 5.4 %collective-permute-start.20 = (bf16[288,128]{1,0:T(8,128)(2,1)S(1)}, bf16[288,128]{1,0:T(8,128)(2,1)S(1)}, u32[]{:S(2)}, u32[]{:S(2)}) collective-permute-start(bf16[288,128]{1,0:T(8,128)(2,1)S(1)} %collective-permute-done.18.refs_2_), channel_id=1, source_target_pairs={{0,224},{16,240},{32,0},{48,16},{64,32},{80,48},{96,64},{112,80},{... | collective-permute-start | bytes 221192 | tf_op jit(solution)/shard_map/ppermute | solution.py:398
  128.4 5.9 %collective-permute-start.19 = (bf16[288,128]{1,0:T(8,128)(2,1)S(1)}, bf16[288,128]{1,0:T(8,128)(2,1)S(1)}, u32[]{:S(2)}, u32[]{:S(2)}) collective-permute-start(bf16[288,128]{1,0:T(8,128)(2,1)S(1)} %get-tuple-element.62.refs_1_), channel_id=1, source_target_pairs={{0,224},{16,240},{32,0},{48,16},{64,32},{80,48},{96,64},{112,80},{... | collective-permute-start | bytes 221192 | tf_op jit(solution)/shard_map/ppermute | solution.py:398
  128.4 6.6 %collective-permute-start.26 = (bf16[288,128]{1,0:T(8,128)(2,1)S(1)}, bf16[288,128]{1,0:T(8,128)(2,1)S(1)}, u32[]{:S(2)}, u32[]{:S(2)}) collective-permute-start(bf16[288,128]{1,0:T(8,128)(2,1)S(1)} %collective-permute-done.25.refs_15_), channel_id=1, source_target_pairs={{0,32},{16,48},{32,64},{48,80},{64,96},{80,112},{96,128},{112,144}... | collective-permute-start | bytes 221192 | tf_op jit(solution)/shard_map/ppermute | solution.py:397
  130.4 5.9 %collective-permute-start.30 = (bf16[288,128]{1,0:T(8,128)(2,1)S(1)}, bf16[288,128]{1,0:T(8,128)(2,1)S(1)}, u32[]{:S(2)}, u32[]{:S(2)}) collective-permute-start(bf16[288,128]{1,0:T(8,128)(2,1)S(1)} %collective-permute-done.18.refs_2_), channel_id=1, source_target_pairs={{0,32},{16,48},{32,64},{48,80},{64,96},{80,112},{96,128},{112,144}... | collective-permute-start | bytes 221192 | tf_op jit(solution)/shard_map/ppermute | solution.py:397
  130.5 5.8 %collective-permute-start.22 = (bf16[288,128]{1,0:T(8,128)(2,1)S(1)}, bf16[288,128]{1,0:T(8,128)(2,1)S(1)}, u32[]{:S(2)}, u32[]{:S(2)}) collective-permute-start(bf16[288,128]{1,0:T(8,128)(2,1)S(1)} %collective-permute-done.20.refs_4_), channel_id=1, source_target_pairs={{0,224},{16,240},{32,0},{48,16},{64,32},{80,48},{96,64},{112,80},{... | collective-permute-start | bytes 221192 | tf_op jit(solution)/shard_map/ppermute | solution.py:398
  134.2 5.6 %collective-permute-start.21 = (bf16[288,128]{1,0:T(8,128)(2,1)S(1)}, bf16[288,128]{1,0:T(8,128)(2,1)S(1)}, u32[]{:S(2)}, u32[]{:S(2)}) collective-permute-start(bf16[288,128]{1,0:T(8,128)(2,1)S(1)} %collective-permute-done.19.refs_3_), channel_id=1, source_target_pairs={{0,224},{16,240},{32,0},{48,16},{64,32},{80,48},{96,64},{112,80},{... | collective-permute-start | bytes 221192 | tf_op jit(solution)/shard_map/ppermute | solution.py:398
  135.0 5.6 %collective-permute-start.27 = (bf16[288,128]{1,0:T(8,128)(2,1)S(1)}, bf16[288,128]{1,0:T(8,128)(2,1)S(1)}, u32[]{:S(2)}, u32[]{:S(2)}) collective-permute-start(bf16[288,128]{1,0:T(8,128)(2,1)S(1)} %collective-permute-done.26.refs_13_), channel_id=1, source_target_pairs={{0,32},{16,48},{32,64},{48,80},{64,96},{80,112},{96,128},{112,144}... | collective-permute-start | bytes 221192 | tf_op jit(solution)/shard_map/ppermute | solution.py:397
  136.3 5.6 %collective-permute-start.31 = (bf16[288,128]{1,0:T(8,128)(2,1)S(1)}, bf16[288,128]{1,0:T(8,128)(2,1)S(1)}, u32[]{:S(2)}, u32[]{:S(2)}) collective-permute-start(bf16[288,128]{1,0:T(8,128)(2,1)S(1)} %collective-permute-done.30.refs_16_), channel_id=1, source_target_pairs={{0,32},{16,48},{32,64},{48,80},{64,96},{80,112},{96,128},{112,144}... | collective-permute-start | bytes 221192 | tf_op jit(solution)/shard_map/ppermute | solution.py:397
  136.4 5.6 %collective-permute-start.24 = (bf16[288,128]{1,0:T(8,128)(2,1)S(1)}, bf16[288,128]{1,0:T(8,128)(2,1)S(1)}, u32[]{:S(2)}, u32[]{:S(2)}) collective-permute-start(bf16[288,128]{1,0:T(8,128)(2,1)S(1)} %collective-permute-done.22.refs_6_), channel_id=1, source_target_pairs={{0,224},{16,240},{32,0},{48,16},{64,32},{80,48},{96,64},{112,80},{... | collective-permute-start | bytes 221192 | tf_op jit(solution)/shard_map/ppermute | solution.py:398
  139.8 5.6 %collective-permute-start.23 = (bf16[288,128]{1,0:T(8,128)(2,1)S(1)}, bf16[288,128]{1,0:T(8,128)(2,1)S(1)}, u32[]{:S(2)}, u32[]{:S(2)}) collective-permute-start(bf16[288,128]{1,0:T(8,128)(2,1)S(1)} %collective-permute-done.21.refs_5_), channel_id=1, source_target_pairs={{0,224},{16,240},{32,0},{48,16},{64,32},{80,48},{96,64},{112,80},{... | collective-permute-start | bytes 221192 | tf_op jit(solution)/shard_map/ppermute | solution.py:398
  140.6 5.6 %collective-permute-start.28 = (bf16[288,128]{1,0:T(8,128)(2,1)S(1)}, bf16[288,128]{1,0:T(8,128)(2,1)S(1)}, u32[]{:S(2)}, u32[]{:S(2)}) collective-permute-start(bf16[288,128]{1,0:T(8,128)(2,1)S(1)} %collective-permute-done.27.refs_11_), channel_id=1, source_target_pairs={{0,32},{16,48},{32,64},{48,80},{64,96},{80,112},{96,128},{112,144}... | collective-permute-start | bytes 221192 | tf_op jit(solution)/shard_map/ppermute | solution.py:402
  141.8 5.6 %collective-permute-start.32 = (bf16[288,128]{1,0:T(8,128)(2,1)S(1)}, bf16[288,128]{1,0:T(8,128)(2,1)S(1)}, u32[]{:S(2)}, u32[]{:S(2)}) collective-permute-start(bf16[288,128]{1,0:T(8,128)(2,1)S(1)} %collective-permute-done.31.refs_14_), channel_id=1, source_target_pairs={{0,32},{16,48},{32,64},{48,80},{64,96},{80,112},{96,128},{112,144}... | collective-permute-start | bytes 221192 | tf_op jit(solution)/shard_map/ppermute | solution.py:397
  141.9 5.5 %collective-permute-start.29 = (bf16[288,128]{1,0:T(8,128)(2,1)S(1)}, bf16[288,128]{1,0:T(8,128)(2,1)S(1)}, u32[]{:S(2)}, u32[]{:S(2)}) collective-permute-start(bf16[288,128]{1,0:T(8,128)(2,1)S(1)} %collective-permute-done.24.refs_8_), channel_id=1, source_target_pairs={{0,224},{16,240},{32,0},{48,16},{64,32},{80,48},{96,64},{112,80},{... | collective-permute-start | bytes 221192 | tf_op jit(solution)/shard_map/ppermute | solution.py:403

commit v3 on v2

--- a/solution.py
+++ b/solution.py
@@ -126,9 +126,19 @@
     ]
 
 
-def pack_kernel(
-    old_ref, new_ref, cols_ref, master_ref, first_ref, second_ref, table_ref, out_ref, moments_ref, scalars, sem
-):
+def pack(table_ref, pairs):
+    def step(q, carry):
+        slot = table_ref[SEND, q]
+        at = jnp.minimum(slot, SLOTS - 1)
+        some = (jnp.zeros((ROWS, B), jnp.int32) + slot) < SLOTS
+        for ref, out in pairs:
+            out[q] = jnp.where(some, ref[at], 0.0)
+        return carry
+
+    lax.fori_loop(0, OWNERS * KEEP, step, 0, unroll=8)
+
+
+def pack_kernel(old_ref, new_ref, cols_ref, master_ref, table_ref, out_ref, scalars, sem):
     rows = routing_table(lax.axis_index("tensor"), old_ref, new_ref, cols_ref)
     for i, row in enumerate(rows):
         table_ref[i : i + 1, :] = row.astype(jnp.int32)
@@ -136,17 +146,11 @@
     copy = pltpu.make_async_copy(table_ref, scalars, sem)
     copy.start()
     copy.wait()
-
-    def step(q, carry):
-        slot = scalars[SEND, q]
-        at = jnp.minimum(slot, SLOTS - 1)
-        some = (jnp.zeros((ROWS, B), jnp.int32) + slot) < SLOTS
-        out_ref[q] = jnp.where(some, master_ref[at], 0.0)
-        for state, ref in enumerate((first_ref, second_ref)):
-            moments_ref[q, state] = jnp.where(some, ref[at], 0.0)
-        return carry
-
-    lax.fori_loop(0, OWNERS * KEEP, step, 0, unroll=8)
+    pack(scalars, [(master_ref, out_ref)])
+
+
+def pack_moments_kernel(table_ref, first_ref, second_ref, out_ref):
+    pack(table_ref, [(first_ref, out_ref.at[:, 0]), (second_ref, out_ref.at[:, 1])])
 
 
 def place_tile(table_ref, slot, ref, arrived):
@@ -442,18 +446,14 @@
 
     swapped = hop(tokens, X_SWAP)
 
-    table, packed, packed_moments = pl.pallas_call(
+    table, packed = pl.pallas_call(
         pack_kernel,
-        out_shape=(
-            sd((8, 128), jnp.int32),
-            sd((OWNERS * KEEP, ROWS, B), F32),
-            sd((OWNERS * KEEP, 2, ROWS, B), F32),
-        ),
-        in_specs=[vmem()] * 6,
-        out_specs=(vmem(),) * 3,
+        out_shape=(sd((8, 128), jnp.int32), sd((OWNERS * KEEP, ROWS, B), F32)),
+        in_specs=[vmem()] * 4,
+        out_specs=(vmem(),) * 2,
         scratch_shapes=[pltpu.SMEM((8, 128), jnp.int32), pltpu.SemaphoreType.DMA],
         compiler_params=params(56),
-    )(old_blocks, new_blocks, new_columns, *states)
+    )(old_blocks, new_blocks, new_columns, states[0])
     arrived = lax.all_to_all(packed, "tensor", split_axis=0, concat_axis=0, tiled=True)
 
     arrived, swapped = lax.optimization_barrier((arrived, swapped))
@@ -473,10 +473,17 @@
     shards = [pair, lax.ppermute(pair, AXES, NEAR)]
     shards.append(lax.ppermute(jnp.concatenate(shards, axis=0), AXES, FAR))
     shards.append(lax.ppermute(shards[2], AXES, NEAR))
-    shards.append(lax.ppermute(shards[3], AXES, FAR))
-
     def after(value, other):
         return lax.optimization_barrier((value, other))[0]
+
+    packed_moments = pl.pallas_call(
+        pack_moments_kernel,
+        out_shape=sd((OWNERS * KEEP, 2, ROWS, B), F32),
+        in_specs=[smem()] + [vmem()] * 2,
+        out_specs=vmem(),
+        compiler_params=params(56),
+    )(table, states[1], states[2])
+    shards.append(lax.ppermute(after(shards[3], packed_moments), AXES, FAR))
 
     far = hop(jnp.concatenate([start, after(near, shards[1])], axis=0), Y_FAR)
     mine = [start, near, after(far, shards[4])]

time: 151 us -> 150 us (level)
  waiting for transfers between devices: 55.5 us -> 53 us
  Pallas kernels: 22.5 us -> 24.2 us
    ppermute x1, waiting for transfers between devices: 6.72 us -> 4.73 us  [local(): shards.append(lax.ppermute(shards[2], AXES, NEAR))]
    pallas_call x0 -> x1, Pallas kernels: none -> 1.99 us  [local(): pl.pallas_call(pack_moments_kernel, out_shape=sd((OWNERS * KEEP, 2, ROWS,...]
  transfers between devices with their start and end apart: 34 -> 34, of which waited for: 15 -> 14; matrix products, arithmetic and copies ran while one was open for 2% -> 2% of each run, Pallas kernels for 12% -> 13%
where the time goes in v3:
time: 150 us
  starting transfers between devices  54.1 us (36%)
  waiting for transfers between devices  53 us (35%)
  Pallas kernels  24.2 us (16%)
  blocking collectives  11.8 us (8%)
  other arithmetic  4.81 us (3%)
    pallas_call x1, Pallas kernels, local(): pl.pallas_call(main_kernel, out_shape=(sd(upstream.shape, BF16),) + (pair...  12.2 us
    ppermute x3, waiting for transfers between devices, reduce_chunks(): got = [lax.ppermute(a, 'dp', SWAP) for a in send]  12.1 us
    ppermute x6, starting transfers between devices, gather_pieces(): down[j] = lax.ppermute(down[j], 'dp', DOWN)  12 us
    all_to_all x1, blocking collectives, local(): lax.all_to_all(packed, 'tensor', split_axis=0, concat_axis=0, tiled=True)  11.8 us
    ppermute x1, starting transfers between devices, local(): shards.append(lax.ppermute(jnp.concatenate(shards, axis=0), AXES, FAR))  5.94 us
    all_to_all x1, starting transfers between devices, local(): lax.all_to_all(after(packed_moments, shards[4]), 'tensor', split_axis=0,...  5.31 us
    ppermute x1, waiting for transfers between devices, local(): pair = jnp.stack([copy_in, lax.ppermute(copy_in, 'dp', SWAP)])  4.83 us
    ppermute x1, waiting for transfers between devices, gather_pieces(): swapped = lax.ppermute(shard, 'dp', SWAP)  4.74 us
  transfers between devices with their start and end apart: 34, of which 14 were waited for; matrix products, arithmetic and copies ran while one was open for 2% of the time, Pallas kernels for 13%

profile of v3, /device:TPU:6, one launch (start us, length us, event | category | flops | bytes accessed | tf_op | source)
XLA Modules:
  0.0 149.8 jit_solution(11779434568384548670)
XLA Ops:
  0.6 0.0 copy-start.7
  0.7 0.9 collective-permute-start
  1.6 2.8 %shard_map.119 = (s32[8,128]{1,0:T(8,128)}, f32[48,8,128]{2,1,0:T(8,128)}) custom-call(s32[16,60]{1,0:T(8,128)} %old_ref.1, s32[16,60]{1,0:T(8,128)} %new_ref.1, s32[16,12]{1,0:T(8,128)} %cols_ref.1, f32[60,8,128]{2,1,0:T(8,128)} %bitcast.19), custom_call_target="tpu_custom_call" | custom-call | tf_op jit(solution)/shard_map/pallas_call | solution.py:449
  4.4 11.8 %all_to_all.10.arrived_ref = f32[48,8,128]{2,1,0:T(8,128)S(1)} all-to-all(f32[48,8,128]{2,1,0:T(8,128)} %get-tuple-element.35), channel_id=1, replica_groups=mesh['dp'=16,'tensor'=16] {'tensor'}, dimensions={0} | all-to-all | bytes 393216 | tf_op jit(solution)/shard_map/all_to_all | solution.py:457
  16.2 1.1 pad_maximum_fusion.1.refs_3_
  17.3 0.3 collective-permute-start.6
  17.6 0.8 shard_map.120
  18.4 1.7 %collective-permute-start.1 = (bf16[288,128]{1,0:T(8,128)(2,1)S(1)}, bf16[288,128]{1,0:T(8,128)(2,1)S(1)}, u32[]{:S(2)}, u32[]{:S(2)}) collective-permute-start(bf16[288,128]{1,0:T(8,128)(2,1)S(1)} %shard_map.120), channel_id=1, source_target_pairs={{0,16},{16,0},{32,48},{48,32},{64,80},{80,64},{96,112},{112,96},{1... | collective-permute-start | bytes 221192 | tf_op jit(solution)/shard_map/ppermute | solution.py:472
  20.1 4.8 %collective-permute-done.1 = bf16[288,128]{1,0:T(8,128)(2,1)S(1)} collective-permute-done((bf16[288,128]{1,0:T(8,128)(2,1)S(1)}, bf16[288,128]{1,0:T(8,128)(2,1)S(1)}, u32[]{:S(2)}, u32[]{:S(2)}) %collective-permute-start.1) | collective-permute-done | bytes 73760 | tf_op jit(solution)/shard_map/ppermute | solution.py:472
  24.9 2.0 %collective-permute-start.2 = (bf16[2,288,128]{2,1,0:T(8,128)(2,1)S(1)}, bf16[2,288,128]{2,1,0:T(8,128)(2,1)S(1)}, u32[]{:S(2)}, u32[]{:S(2)}) collective-permute-start(bf16[2,288,128]{2,1,0:T(8,128)(2,1)S(1)} %pad_maximum_fusion.3.refs_0_), channel_id=1, source_target_pairs={{0,32},{1,225},{2,34},{3,227},{4,36},{5,229},{6,38},{7,231},{8,40}... | collective-permute-start | bytes 442376 | tf_op jit(solution)/shard_map/ppermute | solution.py:473
  26.9 3.2 %collective-permute-done.2.refs_1_ = bf16[2,288,128]{2,1,0:T(8,128)(2,1)S(1)} collective-permute-done((bf16[2,288,128]{2,1,0:T(8,128)(2,1)S(1)}, bf16[2,288,128]{2,1,0:T(8,128)(2,1)S(1)}, u32[]{:S(2)}, u32[]{:S(2)}) %collective-permute-start.2) | collective-permute-done | bytes 147488 | tf_op jit(solution)/shard_map/ppermute | solution.py:473
  30.2 1.3 pad_maximum_fusion
  31.5 1.3 collective-permute-start.7
  32.8 5.9 %collective-permute-start.3 = (bf16[4,288,128]{2,1,0:T(8,128)(2,1)S(1)}, bf16[4,288,128]{2,1,0:T(8,128)(2,1)S(1)}, u32[]{:S(2)}, u32[]{:S(2)}) collective-permute-start(bf16[4,288,128]{2,1,0:T(8,128)(2,1)S(1)} %pad_maximum_fusion.2), channel_id=1, source_target_pairs={{0,224},{1,33},{2,226},{3,35},{4,228},{5,37},{6,230},{7,39},{8,232... | collective-permute-start | bytes 884744 | tf_op jit(solution)/shard_map/ppermute | solution.py:474
  38.7 4.7 %collective-permute-done.3.refs_2_ = bf16[4,288,128]{2,1,0:T(8,128)(2,1)S(1)} collective-permute-done((bf16[4,288,128]{2,1,0:T(8,128)(2,1)S(1)}, bf16[4,288,128]{2,1,0:T(8,128)(2,1)S(1)}, u32[]{:S(2)}, u32[]{:S(2)}) %collective-permute-start.3) | collective-permute-done | bytes 294944 | tf_op jit(solution)/shard_map/ppermute | solution.py:474
  43.5 2.0 %shard_map.121 = f32[48,2,8,128]{3,2,1,0:T(8,128)} custom-call(s32[8,128]{1,0:T(8,128)} %get-tuple-element.34.table_ref.refs_0_, f32[60,8,128]{2,1,0:T(8,128)} %bitcast.22, f32[60,8,128]{2,1,0:T(8,128)} %bitcast.24), custom_call_target="tpu_custom_call" | custom-call | tf_op jit(solution)/shard_map/pallas_call | solution.py:479
  45.4 4.7 %collective-permute-done.4.refs_3_ = bf16[4,288,128]{2,1,0:T(8,128)(2,1)S(1)} collective-permute-done((bf16[4,288,128]{2,1,0:T(8,128)(2,1)S(1)}, bf16[4,288,128]{2,1,0:T(8,128)(2,1)S(1)}, u32[]{:S(2)}, u32[]{:S(2)}) %collective-permute-start.4) | collective-permute-done | bytes 294944 | tf_op jit(solution)/shard_map/ppermute | solution.py:475
  50.2 3.3 %collective-permute-start.5 = (bf16[4,288,128]{2,1,0:T(8,128)(2,1)S(1)}, bf16[4,288,128]{2,1,0:T(8,128)(2,1)S(1)}, u32[]{:S(2)}, u32[]{:S(2)}) collective-permute-start(bf16[4,288,128]{2,1,0:T(8,128)(2,1)S(1)} %collective-permute-done.4.refs_3_), channel_id=1, source_target_pairs={{0,224},{1,33},{2,226},{3,35},{4,228},{5,37},{6,230},{7,39},{8,232... | collective-permute-start | bytes 884744 | tf_op jit(solution)/shard_map/ppermute | solution.py:486
  53.5 4.7 %collective-permute-done.5.refs_4_ = bf16[4,288,128]{2,1,0:T(8,128)(2,1)S(1)} collective-permute-done((bf16[4,288,128]{2,1,0:T(8,128)(2,1)S(1)}, bf16[4,288,128]{2,1,0:T(8,128)(2,1)S(1)}, u32[]{:S(2)}, u32[]{:S(2)}) %collective-permute-start.5) | collective-permute-done | bytes 294944 | tf_op jit(solution)/shard_map/ppermute | solution.py:486
  58.2 0.5 collective-permute-start.8
  58.7 0.1 collective-permute-start.9
  58.8 5.3 %all-to-all-start.1 = ((f32[48,2,8,128]{3,2,1,0:T(8,128)}), f32[48,2,8,128]{3,2,1,0:T(8,128)S(1)}, u32[]{:S(2)}, u32[]{:S(2)}) async-start(f32[48,2,8,128]{3,2,1,0:T(8,128)} %shard_map.121), calls=%async_computation.1 | async-start | bytes 786432 | tf_op jit(solution)/shard_map/all_to_all | solution.py:500
  64.1 0.4 shard_map.122.refs_2_
  64.5 0.0 copy-start.1
  64.5 1.0 copy-done.1
  65.6 12.2 %shard_map.123 = (bf16[512,1536]{1,0:T(8,128)(2,1)}, f32[2,480,128]{2,1,0:T(8,128)}, f32[2,480,128]{2,1,0:T(8,128)}, f32[2,480,128]{2,1,0:T(8,128)}, f32[2,480,1...) custom-call(s32[8,128]{1,0:T(8,128)} %get-tuple-element.34.table_ref.re, ...), custom_call_target="tpu_custom_call" | custom-call | flops 4000000000 | bytes 20000000 | tf_op jit(solution)/shard_map/pallas_call | solution.py:505
  77.8 1.2 collective-permute-start.13
  79.0 2.4 %collective-permute-start.12 = (bf16[2,480,128]{2,1,0:T(8,128)(2,1)}, bf16[2,480,128]{2,1,0:T(8,128)(2,1)S(1)}, u32[]{:S(2)}, u32[]{:S(2)}) collective-permute-start(bf16[2,480,128]{2,1,0:T(8,128)(2,1)} %get-tuple-element.51), channel_id=1, source_target_pairs={{0,16},{16,0},{32,48},{48,32},{64,80},{80,64},{96,112},{112,96},{1... | collective-permute-start | bytes 737288 | tf_op jit(solution)/shard_map/ppermute | solution.py:430
  81.4 7.0 %collective-permute-done.13 = bf16[2,480,128]{2,1,0:T(8,128)(2,1)S(1)} collective-permute-done((bf16[2,480,128]{2,1,0:T(8,128)(2,1)}, bf16[2,480,128]{2,1,0:T(8,128)(2,1)S(1)}, u32[]{:S(2)}, u32[]{:S(2)}) %collective-permute-start.13) | collective-permute-done | bytes 245792 | tf_op jit(solution)/shard_map/ppermute | solution.py:430
  88.4 1.1 add_convert_fusion.2
  89.4 3.4 %collective-permute-start.14 = (bf16[2,480,128]{2,1,0:T(8,128)(2,1)S(1)}, bf16[2,480,128]{2,1,0:T(8,128)(2,1)S(1)}, u32[]{:S(2)}, u32[]{:S(2)}) collective-permute-start(bf16[2,480,128]{2,1,0:T(8,128)(2,1)S(1)} %add_convert_fusion.2), channel_id=1, source_target_pairs={{0,224},{1,33},{2,226},{3,35},{4,228},{5,37},{6,230},{7,39},{8,232... | collective-permute-start | bytes 737288 | tf_op jit(solution)/shard_map/ppermute | solution.py:437
  92.8 1.1 collective-permute-start.11
  93.9 3.1 %collective-permute-done.14 = bf16[2,480,128]{2,1,0:T(8,128)(2,1)S(1)} collective-permute-done((bf16[2,480,128]{2,1,0:T(8,128)(2,1)S(1)}, bf16[2,480,128]{2,1,0:T(8,128)(2,1)S(1)}, u32[]{:S(2)}, u32[]{:S(2)}) %collective-permute-start.14) | collective-permute-done | bytes 245792 | tf_op jit(solution)/shard_map/ppermute | solution.py:437
  97.0 1.1 add_convert_fusion.1
  98.1 0.1 collective-permute-start.15
  98.2 5.2 %collective-permute-done.11 = bf16[4,480,128]{2,1,0:T(8,128)(2,1)S(1)} collective-permute-done((bf16[4,480,128]{2,1,0:T(8,128)(2,1)}, bf16[4,480,128]{2,1,0:T(8,128)(2,1)S(1)}, u32[]{:S(2)}, u32[]{:S(2)}) %collective-permute-start.11) | collective-permute-done | bytes 491552 | tf_op jit(solution)/shard_map/ppermute | solution.py:430
  103.4 1.0 collective-permute-done.15
  104.4 0.1 add_convert_fusion
  104.5 3.3 %collective-permute-start.16 = (bf16[2,480,128]{2,1,0:T(8,128)(2,1)S(1)}, bf16[2,480,128]{2,1,0:T(8,128)(2,1)S(1)}, u32[]{:S(2)}, u32[]{:S(2)}) collective-permute-start(bf16[2,480,128]{2,1,0:T(8,128)(2,1)S(1)} %add_convert_fusion), channel_id=1, source_target_pairs={{0,224},{1,33},{2,226},{3,35},{4,228},{5,37},{6,230},{7,39},{8,232... | collective-permute-start | bytes 737288 | tf_op jit(solution)/shard_map/ppermute | solution.py:439
  107.8 4.2 %collective-permute-done.16.near_ref = bf16[2,480,128]{2,1,0:T(8,128)(2,1)S(1)} collective-permute-done((bf16[2,480,128]{2,1,0:T(8,128)(2,1)S(1)}, bf16[2,480,128]{2,1,0:T(8,128)(2,1)S(1)}, u32[]{:S(2)}, u32[]{:S(2)}) %collective-permute-start.16) | collective-permute-done | bytes 245792 | tf_op jit(solution)/shard_map/ppermute | solution.py:439
  112.0 0.1 fusion.2
  112.0 0.1 collective-permute-start.17
  112.2 1.2 shard_map.124
  113.4 3.6 %collective-permute-done.17.last_ref = bf16[480,128]{1,0:T(8,128)(2,1)S(1)} collective-permute-done((bf16[480,128]{1,0:T(8,128)(2,1)S(1)}, bf16[480,128]{1,0:T(8,128)(2,1)S(1)}, u32[]{:S(2)}, u32[]{:S(2)}) %collective-permute-start.17) | collective-permute-done | bytes 122912 | tf_op jit(solution)/shard_map/ppermute | solution.py:440
  117.0 1.8 %shard_map.125 = (f32[480,128]{1,0:T(8,128)}, f32[480,128]{1,0:T(8,128)}, f32[480,128]{1,0:T(8,128)}, bf16[288,128]{1,0:T(8,128)(2,1)S(1)}) custom-call(s32[8,128]{1,0:T(8,128)S(1)} %copy-done.6, f32[2,480,128]{2,1,0:T(8,128)S(1)} %copy-done.2, bf16[2,480,128]{2,1,0:T(8,128)(2,1)S(1)} %slice.12.got_ref, ...), custom_call_target="tpu_custom_call" | custom-call | tf_op jit(solution)/shard_map/pallas_call | solution.py:538
  118.9 1.1 collective-permute-start.18
  120.0 0.0 collective-permute-start.25
  120.0 4.7 %collective-permute-done.18.refs_2_ = bf16[288,128]{1,0:T(8,128)(2,1)S(1)} collective-permute-done((bf16[288,128]{1,0:T(8,128)(2,1)S(1)}, bf16[288,128]{1,0:T(8,128)(2,1)S(1)}, u32[]{:S(2)}, u32[]{:S(2)}) %collective-permute-start.18) | collective-permute-done | bytes 73760 | tf_op jit(solution)/shard_map/ppermute | solution.py:395
  124.7 3.3 %collective-permute-start.20 = (bf16[288,128]{1,0:T(8,128)(2,1)S(1)}, bf16[288,128]{1,0:T(8,128)(2,1)S(1)}, u32[]{:S(2)}, u32[]{:S(2)}) collective-permute-start(bf16[288,128]{1,0:T(8,128)(2,1)S(1)} %collective-permute-done.18.refs_2_), channel_id=1, source_target_pairs={{0,224},{16,240},{32,0},{48,16},{64,32},{80,48},{96,64},{112,80},{... | collective-permute-start | bytes 221192 | tf_op jit(solution)/shard_map/ppermute | solution.py:402
  128.0 0.0 collective-permute-start.19
  128.1 2.0 %collective-permute-start.26 = (bf16[288,128]{1,0:T(8,128)(2,1)S(1)}, bf16[288,128]{1,0:T(8,128)(2,1)S(1)}, u32[]{:S(2)}, u32[]{:S(2)}) collective-permute-start(bf16[288,128]{1,0:T(8,128)(2,1)S(1)} %collective-permute-done.25.refs_15_), channel_id=1, source_target_pairs={{0,32},{16,48},{32,64},{48,80},{64,96},{80,112},{96,128},{112,144}... | collective-permute-start | bytes 221192 | tf_op jit(solution)/shard_map/ppermute | solution.py:401
  130.1 0.0 collective-permute-start.30
  130.1 3.7 %collective-permute-start.22 = (bf16[288,128]{1,0:T(8,128)(2,1)S(1)}, bf16[288,128]{1,0:T(8,128)(2,1)S(1)}, u32[]{:S(2)}, u32[]{:S(2)}) collective-permute-start(bf16[288,128]{1,0:T(8,128)(2,1)S(1)} %collective-permute-done.20.refs_4_), channel_id=1, source_target_pairs={{0,224},{16,240},{32,0},{48,16},{64,32},{80,48},{96,64},{112,80},{... | collective-permute-start | bytes 221192 | tf_op jit(solution)/shard_map/ppermute | solution.py:402
  133.8 0.8 collective-permute-start.21
  134.6 1.2 collective-permute-start.27
  135.8 0.1 collective-permute-start.31
  135.9 3.4 %collective-permute-start.24 = (bf16[288,128]{1,0:T(8,128)(2,1)S(1)}, bf16[288,128]{1,0:T(8,128)(2,1)S(1)}, u32[]{:S(2)}, u32[]{:S(2)}) collective-permute-start(bf16[288,128]{1,0:T(8,128)(2,1)S(1)} %collective-permute-done.22.refs_6_), channel_id=1, source_target_pairs={{0,224},{16,240},{32,0},{48,16},{64,32},{80,48},{96,64},{112,80},{... | collective-permute-start | bytes 221192 | tf_op jit(solution)/shard_map/ppermute | solution.py:402
  139.4 0.8 collective-permute-start.23
  140.1 1.2 collective-permute-start.28
  141.4 0.1 collective-permute-start.32
  141.5 3.4 %collective-permute-start.29 = (bf16[288,128]{1,0:T(8,128)(2,1)S(1)}, bf16[288,128]{1,0:T(8,128)(2,1)S(1)}, u32[]{:S(2)}, u32[]{:S(2)}) collective-permute-start(bf16[288,128]{1,0:T(8,128)(2,1)S(1)} %collective-permute-done.24.refs_8_), channel_id=1, source_target_pairs={{0,224},{16,240},{32,0},{48,16},{64,32},{80,48},{96,64},{112,80},{... | collective-permute-start | bytes 221192 | tf_op jit(solution)/shard_map/ppermute | solution.py:407
  144.9 0.8 collective-permute-done.28.refs_9_
  145.7 1.2 collective-permute-done.32.refs_12_
  147.0 2.8 %shard_map.126 = bf16[60,128,128]{2,1,0:T(8,128)(2,1)} custom-call(s32[8,128]{1,0:T(8,128)S(1)} %copy-done.6, bf16[288,128]{1,0:T(8,128)(2,1)S(1)} %get-tuple-element.62.refs_1_, bf16[288,128]{1,0:T(8,128)(2,1)S(1)} %collective-permute-done.18.refs_2_, bf16[288,128]{1,0:T(8,128)(2,1)S(1)} %collective-permute-done.19.refs_3_, ...), custom_call_target="tpu_custom_call" | custom-call | tf_op jit(solution)/shard_map/pallas_call | solution.py:548
  (42 shorter events, 0.2 us)
Async XLA Ops:
  0.6 29.5 %copy-start.7 = (bf16[512,384]{1,0:T(8,128)(2,1)S(1)}, bf16[512,384]{1,0:T(8,128)(2,1)}, u32[]{:S(2)}) copy-start(bf16[512,384]{1,0:T(8,128)(2,1)} %param.8) | copy-start | bytes 1179652
  0.6 16.9 %copy-start = (f32[8,60,128]{2,0,1:T(8,128)S(1)}, f32[8,60,128]{2,0,1:T(8,128)}, u32[]{:S(2)}) copy-start(f32[8,60,128]{2,0,1:T(8,128)} %param.10) | copy-start | bytes 737284
  0.7 15.6 %collective-permute-start = (bf16[512,384]{1,0:T(8,128)(2,1)}, bf16[512,384]{1,0:T(8,128)(2,1)S(1)}, u32[]{:S(2)}, u32[]{:S(2)}) collective-permute-start(bf16[512,384]{1,0:T(8,128)(2,1)} %param.8), channel_id=1, source_target_pairs={{0,2},{1,3},{2,0},{3,1},{4,6},{5,7},{6,4},{7,5},{8,10},{9,11},{10,... | collective-permute-start | bytes 1179656 | tf_op jit(solution)/shard_map/ppermute | solution.py:426
  4.4 13.2 %copy-start.5 = (s32[8,128]{1,0:T(8,128)S(1)}, s32[8,128]{1,0:T(8,128)}, u32[]{:S(2)}) copy-start(s32[8,128]{1,0:T(8,128)} %get-tuple-element.34.table_ref.refs_0_) | copy-start | bytes 12292
  17.3 40.9 %copy-start.8 = (bf16[2,512,384]{2,1,0:T(8,128)(2,1)}, bf16[2,512,384]{2,1,0:T(8,128)(2,1)S(1)}, u32[]{:S(2)}) copy-start(bf16[2,512,384]{2,1,0:T(8,128)(2,1)S(1)} %pad_maximum_fusion.1.refs_3_) | copy-start | bytes 2359300
  17.3 12.9 %collective-permute-start.6 = (bf16[2,512,384]{2,1,0:T(8,128)(2,1)S(1)}, bf16[2,512,384]{2,1,0:T(8,128)(2,1)}, u32[]{:S(2)}, u32[]{:S(2)}) collective-permute-start(bf16[2,512,384]{2,1,0:T(8,128)(2,1)S(1)} %pad_maximum_fusion.1.refs_3_), channel_id=1, source_target_pairs={{0,4},{1,13},{2,6},{3,15},{4,0},{5,9},{6,2},{7,11},{8,12},{9,5},{1... | collective-permute-start | bytes 2359304 | tf_op jit(solution)/shard_map/ppermute | solution.py:426
  18.4 6.5 %collective-permute-start.1 = (bf16[288,128]{1,0:T(8,128)(2,1)S(1)}, bf16[288,128]{1,0:T(8,128)(2,1)S(1)}, u32[]{:S(2)}, u32[]{:S(2)}) collective-permute-start(bf16[288,128]{1,0:T(8,128)(2,1)S(1)} %shard_map.120), channel_id=1, source_target_pairs={{0,16},{16,0},{32,48},{48,32},{64,80},{80,64},{96,112},{112,96},{1... | collective-permute-start | bytes 221192 | tf_op jit(solution)/shard_map/ppermute | solution.py:472
  24.9 5.2 %collective-permute-start.2 = (bf16[2,288,128]{2,1,0:T(8,128)(2,1)S(1)}, bf16[2,288,128]{2,1,0:T(8,128)(2,1)S(1)}, u32[]{:S(2)}, u32[]{:S(2)}) collective-permute-start(bf16[2,288,128]{2,1,0:T(8,128)(2,1)S(1)} %pad_maximum_fusion.3.refs_0_), channel_id=1, source_target_pairs={{0,32},{1,225},{2,34},{3,227},{4,36},{5,229},{6,38},{7,231},{8,40}... | collective-permute-start | bytes 442376 | tf_op jit(solution)/shard_map/ppermute | solution.py:473
  31.5 26.7 %collective-permute-start.7 = (bf16[4,512,384]{2,1,0:T(8,128)(2,1)S(1)}, bf16[4,512,384]{2,1,0:T(8,128)(2,1)}, u32[]{:S(2)}, u32[]{:S(2)}) collective-permute-start(bf16[4,512,384]{2,1,0:T(8,128)(2,1)S(1)} %pad_maximum_fusion), channel_id=1, source_target_pairs={{0,12},{1,5},{2,14},{3,7},{4,8},{5,1},{6,10},{7,3},{8,4},{9,13},{1... | collective-permute-start | bytes 4718600 | tf_op jit(solution)/shard_map/ppermute | solution.py:426
  32.8 10.6 %collective-permute-start.3 = (bf16[4,288,128]{2,1,0:T(8,128)(2,1)S(1)}, bf16[4,288,128]{2,1,0:T(8,128)(2,1)S(1)}, u32[]{:S(2)}, u32[]{:S(2)}) collective-permute-start(bf16[4,288,128]{2,1,0:T(8,128)(2,1)S(1)} %pad_maximum_fusion.2), channel_id=1, source_target_pairs={{0,224},{1,33},{2,226},{3,35},{4,228},{5,37},{6,230},{7,39},{8,232... | collective-permute-start | bytes 884744 | tf_op jit(solution)/shard_map/ppermute | solution.py:474
  43.5 6.7 %collective-permute-start.4 = (bf16[4,288,128]{2,1,0:T(8,128)(2,1)S(1)}, bf16[4,288,128]{2,1,0:T(8,128)(2,1)S(1)}, u32[]{:S(2)}, u32[]{:S(2)}) collective-permute-start(bf16[4,288,128]{2,1,0:T(8,128)(2,1)S(1)} %collective-permute-done.3.refs_2_), channel_id=1, source_target_pairs={{0,32},{1,225},{2,34},{3,227},{4,36},{5,229},{6,38},{7,231},{8,40}... | collective-permute-start | bytes 884744 | tf_op jit(solution)/shard_map/ppermute | solution.py:475
  50.2 8.0 %collective-permute-start.5 = (bf16[4,288,128]{2,1,0:T(8,128)(2,1)S(1)}, bf16[4,288,128]{2,1,0:T(8,128)(2,1)S(1)}, u32[]{:S(2)}, u32[]{:S(2)}) collective-permute-start(bf16[4,288,128]{2,1,0:T(8,128)(2,1)S(1)} %collective-permute-done.4.refs_3_), channel_id=1, source_target_pairs={{0,224},{1,33},{2,226},{3,35},{4,228},{5,37},{6,230},{7,39},{8,232... | collective-permute-start | bytes 884744 | tf_op jit(solution)/shard_map/ppermute | solution.py:486
  58.2 7.4 %collective-permute-start.10 = (bf16[4,512,384]{2,1,0:T(8,128)(2,1)}, bf16[4,512,384]{2,1,0:T(8,128)(2,1)}, u32[]{:S(2)}, u32[]{:S(2)}) collective-permute-start(bf16[4,512,384]{2,1,0:T(8,128)(2,1)} %collective-permute-done.7.refs_5_), channel_id=1, source_target_pairs={{0,1},{1,0},{2,3},{3,2},{4,5},{5,4},{6,7},{7,6},{8,9},{9,8},{10,11... | collective-permute-start | bytes 4718600 | tf_op jit(solution)/shard_map/ppermute | solution.py:426
  58.2 7.4 %collective-permute-start.8 = (bf16[2,512,384]{2,1,0:T(8,128)(2,1)S(1)}, bf16[2,512,384]{2,1,0:T(8,128)(2,1)}, u32[]{:S(2)}, u32[]{:S(2)}) collective-permute-start(bf16[2,512,384]{2,1,0:T(8,128)(2,1)S(1)} %pad_maximum_fusion.1.refs_3_), channel_id=1, source_target_pairs={{0,1},{1,0},{2,3},{3,2},{4,5},{5,4},{6,7},{7,6},{8,9},{9,8},{10,11... | collective-permute-start | bytes 2359304 | tf_op jit(solution)/shard_map/ppermute | solution.py:426
  58.7 6.9 %collective-permute-start.9 = (bf16[2,512,384]{2,1,0:T(8,128)(2,1)}, bf16[2,512,384]{2,1,0:T(8,128)(2,1)}, u32[]{:S(2)}, u32[]{:S(2)}) collective-permute-start(bf16[2,512,384]{2,1,0:T(8,128)(2,1)} %collective-permute-done.6.refs_4_), channel_id=1, source_target_pairs={{0,1},{1,0},{2,3},{3,2},{4,5},{5,4},{6,7},{7,6},{8,9},{9,8},{10,11... | collective-permute-start | bytes 2359304 | tf_op jit(solution)/shard_map/ppermute | solution.py:426
  58.8 20.2 %all-to-all-start.1 = ((f32[48,2,8,128]{3,2,1,0:T(8,128)}), f32[48,2,8,128]{3,2,1,0:T(8,128)S(1)}, u32[]{:S(2)}, u32[]{:S(2)}) async-start(f32[48,2,8,128]{3,2,1,0:T(8,128)} %shard_map.121), calls=%async_computation.1 | async-start | bytes 786432 | tf_op jit(solution)/shard_map/all_to_all | solution.py:500
  64.5 1.0 copy-start.1
  77.7 26.7 %copy-start.9 = (f32[2,480,128]{2,1,0:T(8,128)S(1)}, f32[2,480,128]{2,1,0:T(8,128)}, u32[]{:S(2)}) copy-start(f32[2,480,128]{2,1,0:T(8,128)} %get-tuple-element.49) | copy-start | bytes 1474564
  77.8 10.6 %collective-permute-start.13 = (bf16[2,480,128]{2,1,0:T(8,128)(2,1)}, bf16[2,480,128]{2,1,0:T(8,128)(2,1)S(1)}, u32[]{:S(2)}, u32[]{:S(2)}) collective-permute-start(bf16[2,480,128]{2,1,0:T(8,128)(2,1)} %get-tuple-element.53), channel_id=1, source_target_pairs={{0,16},{16,0},{32,48},{48,32},{64,80},{80,64},{96,112},{112,96},{1... | collective-permute-start | bytes 737288 | tf_op jit(solution)/shard_map/ppermute | solution.py:430
  79.0 14.9 %collective-permute-start.12 = (bf16[2,480,128]{2,1,0:T(8,128)(2,1)}, bf16[2,480,128]{2,1,0:T(8,128)(2,1)S(1)}, u32[]{:S(2)}, u32[]{:S(2)}) collective-permute-start(bf16[2,480,128]{2,1,0:T(8,128)(2,1)} %get-tuple-element.51), channel_id=1, source_target_pairs={{0,16},{16,0},{32,48},{48,32},{64,80},{80,64},{96,112},{112,96},{1... | collective-permute-start | bytes 737288 | tf_op jit(solution)/shard_map/ppermute | solution.py:430
  89.4 22.6 %copy-start.2 = (f32[2,480,128]{2,1,0:T(8,128)S(1)}, f32[2,480,128]{2,1,0:T(8,128)}, u32[]{:S(2)}) copy-start(f32[2,480,128]{2,1,0:T(8,128)} %get-tuple-element.47.own_ref) | copy-start | bytes 1474564
  89.4 7.5 %collective-permute-start.14 = (bf16[2,480,128]{2,1,0:T(8,128)(2,1)S(1)}, bf16[2,480,128]{2,1,0:T(8,128)(2,1)S(1)}, u32[]{:S(2)}, u32[]{:S(2)}) collective-permute-start(bf16[2,480,128]{2,1,0:T(8,128)(2,1)S(1)} %add_convert_fusion.2), channel_id=1, source_target_pairs={{0,224},{1,33},{2,226},{3,35},{4,228},{5,37},{6,230},{7,39},{8,232... | collective-permute-start | bytes 737288 | tf_op jit(solution)/shard_map/ppermute | solution.py:437
  92.8 19.3 %copy-start.3 = (f32[8,60,128]{2,0,1:T(8,128)S(1)}, f32[8,60,128]{2,0,1:T(8,128)}, u32[]{:S(2)}) copy-start(f32[8,60,128]{2,0,1:T(8,128)} %param.11) | copy-start | bytes 737284
  92.8 19.4 %copy-start.4 = (f32[8,60,128]{2,0,1:T(8,128)S(1)}, f32[8,60,128]{2,0,1:T(8,128)}, u32[]{:S(2)}) copy-start(f32[8,60,128]{2,0,1:T(8,128)} %param.12) | copy-start | bytes 737284
  92.8 19.4 %copy-start.6 = (s32[8,128]{1,0:T(8,128)S(1)}, s32[8,128]{1,0:T(8,128)}, u32[]{:S(2)}) copy-start(s32[8,128]{1,0:T(8,128)} %get-tuple-element.34.table_ref.refs_0_) | copy-start | bytes 12292
  92.8 10.6 %collective-permute-start.11 = (bf16[4,480,128]{2,1,0:T(8,128)(2,1)}, bf16[4,480,128]{2,1,0:T(8,128)(2,1)S(1)}, u32[]{:S(2)}, u32[]{:S(2)}) collective-permute-start(bf16[4,480,128]{2,1,0:T(8,128)(2,1)} %get-tuple-element.48), channel_id=1, source_target_pairs={{0,16},{16,0},{32,48},{48,32},{64,80},{80,64},{96,112},{112,96},{1... | collective-permute-start | bytes 1474568 | tf_op jit(solution)/shard_map/ppermute | solution.py:430
  98.1 6.3 %collective-permute-start.15 = (bf16[2,480,128]{2,1,0:T(8,128)(2,1)S(1)}, bf16[2,480,128]{2,1,0:T(8,128)(2,1)S(1)}, u32[]{:S(2)}, u32[]{:S(2)}) collective-permute-start(bf16[2,480,128]{2,1,0:T(8,128)(2,1)S(1)} %add_convert_fusion.1), channel_id=1, source_target_pairs={{0,32},{1,225},{2,34},{3,227},{4,36},{5,229},{6,38},{7,231},{8,40}... | collective-permute-start | bytes 737288 | tf_op jit(solution)/shard_map/ppermute | solution.py:438
  104.5 7.5 %collective-permute-start.16 = (bf16[2,480,128]{2,1,0:T(8,128)(2,1)S(1)}, bf16[2,480,128]{2,1,0:T(8,128)(2,1)S(1)}, u32[]{:S(2)}, u32[]{:S(2)}) collective-permute-start(bf16[2,480,128]{2,1,0:T(8,128)(2,1)S(1)} %add_convert_fusion), channel_id=1, source_target_pairs={{0,224},{1,33},{2,226},{3,35},{4,228},{5,37},{6,230},{7,39},{8,232... | collective-permute-start | bytes 737288 | tf_op jit(solution)/shard_map/ppermute | solution.py:439
  112.0 5.0 %collective-permute-start.17 = (bf16[480,128]{1,0:T(8,128)(2,1)S(1)}, bf16[480,128]{1,0:T(8,128)(2,1)S(1)}, u32[]{:S(2)}, u32[]{:S(2)}) collective-permute-start(bf16[480,128]{1,0:T(8,128)(2,1)S(1)} %fusion.2), channel_id=1, source_target_pairs={{0,32},{1,225},{2,34},{3,227},{4,36},{5,229},{6,38},{7,231},{8,40}... | collective-permute-start | bytes 368648 | tf_op jit(solution)/shard_map/ppermute | solution.py:440
  118.9 5.9 %collective-permute-start.18 = (bf16[288,128]{1,0:T(8,128)(2,1)S(1)}, bf16[288,128]{1,0:T(8,128)(2,1)S(1)}, u32[]{:S(2)}, u32[]{:S(2)}) collective-permute-start(bf16[288,128]{1,0:T(8,128)(2,1)S(1)} %get-tuple-element.62.refs_1_), channel_id=1, source_target_pairs={{0,16},{16,0},{32,48},{48,32},{64,80},{80,64},{96,112},{112,96},{1... | collective-permute-start | bytes 221192 | tf_op jit(solution)/shard_map/ppermute | solution.py:395
  120.0 8.1 %collective-permute-start.25 = (bf16[288,128]{1,0:T(8,128)(2,1)S(1)}, bf16[288,128]{1,0:T(8,128)(2,1)S(1)}, u32[]{:S(2)}, u32[]{:S(2)}) collective-permute-start(bf16[288,128]{1,0:T(8,128)(2,1)S(1)} %get-tuple-element.62.refs_1_), channel_id=1, source_target_pairs={{0,32},{16,48},{32,64},{48,80},{64,96},{80,112},{96,128},{112,144}... | collective-permute-start | bytes 221192 | tf_op jit(solution)/shard_map/ppermute | solution.py:401
  124.7 5.4 %collective-permute-start.20 = (bf16[288,128]{1,0:T(8,128)(2,1)S(1)}, bf16[288,128]{1,0:T(8,128)(2,1)S(1)}, u32[]{:S(2)}, u32[]{:S(2)}) collective-permute-start(bf16[288,128]{1,0:T(8,128)(2,1)S(1)} %collective-permute-done.18.refs_2_), channel_id=1, source_target_pairs={{0,224},{16,240},{32,0},{48,16},{64,32},{80,48},{96,64},{112,80},{... | collective-permute-start | bytes 221192 | tf_op jit(solution)/shard_map/ppermute | solution.py:402
  128.0 5.8 %collective-permute-start.19 = (bf16[288,128]{1,0:T(8,128)(2,1)S(1)}, bf16[288,128]{1,0:T(8,128)(2,1)S(1)}, u32[]{:S(2)}, u32[]{:S(2)}) collective-permute-start(bf16[288,128]{1,0:T(8,128)(2,1)S(1)} %get-tuple-element.62.refs_1_), channel_id=1, source_target_pairs={{0,224},{16,240},{32,0},{48,16},{64,32},{80,48},{96,64},{112,80},{... | collective-permute-start | bytes 221192 | tf_op jit(solution)/shard_map/ppermute | solution.py:402
  128.1 6.5 %collective-permute-start.26 = (bf16[288,128]{1,0:T(8,128)(2,1)S(1)}, bf16[288,128]{1,0:T(8,128)(2,1)S(1)}, u32[]{:S(2)}, u32[]{:S(2)}) collective-permute-start(bf16[288,128]{1,0:T(8,128)(2,1)S(1)} %collective-permute-done.25.refs_15_), channel_id=1, source_target_pairs={{0,32},{16,48},{32,64},{48,80},{64,96},{80,112},{96,128},{112,144}... | collective-permute-start | bytes 221192 | tf_op jit(solution)/shard_map/ppermute | solution.py:401
  130.1 5.8 %collective-permute-start.30 = (bf16[288,128]{1,0:T(8,128)(2,1)S(1)}, bf16[288,128]{1,0:T(8,128)(2,1)S(1)}, u32[]{:S(2)}, u32[]{:S(2)}) collective-permute-start(bf16[288,128]{1,0:T(8,128)(2,1)S(1)} %collective-permute-done.18.refs_2_), channel_id=1, source_target_pairs={{0,32},{16,48},{32,64},{48,80},{64,96},{80,112},{96,128},{112,144}... | collective-permute-start | bytes 221192 | tf_op jit(solution)/shard_map/ppermute | solution.py:401
  130.1 5.8 %collective-permute-start.22 = (bf16[288,128]{1,0:T(8,128)(2,1)S(1)}, bf16[288,128]{1,0:T(8,128)(2,1)S(1)}, u32[]{:S(2)}, u32[]{:S(2)}) collective-permute-start(bf16[288,128]{1,0:T(8,128)(2,1)S(1)} %collective-permute-done.20.refs_4_), channel_id=1, source_target_pairs={{0,224},{16,240},{32,0},{48,16},{64,32},{80,48},{96,64},{112,80},{... | collective-permute-start | bytes 221192 | tf_op jit(solution)/shard_map/ppermute | solution.py:402
  133.8 5.6 %collective-permute-start.21 = (bf16[288,128]{1,0:T(8,128)(2,1)S(1)}, bf16[288,128]{1,0:T(8,128)(2,1)S(1)}, u32[]{:S(2)}, u32[]{:S(2)}) collective-permute-start(bf16[288,128]{1,0:T(8,128)(2,1)S(1)} %collective-permute-done.19.refs_3_), channel_id=1, source_target_pairs={{0,224},{16,240},{32,0},{48,16},{64,32},{80,48},{96,64},{112,80},{... | collective-permute-start | bytes 221192 | tf_op jit(solution)/shard_map/ppermute | solution.py:402
  134.6 5.6 %collective-permute-start.27 = (bf16[288,128]{1,0:T(8,128)(2,1)S(1)}, bf16[288,128]{1,0:T(8,128)(2,1)S(1)}, u32[]{:S(2)}, u32[]{:S(2)}) collective-permute-start(bf16[288,128]{1,0:T(8,128)(2,1)S(1)} %collective-permute-done.26.refs_13_), channel_id=1, source_target_pairs={{0,32},{16,48},{32,64},{48,80},{64,96},{80,112},{96,128},{112,144}... | collective-permute-start | bytes 221192 | tf_op jit(solution)/shard_map/ppermute | solution.py:401
  135.8 5.6 %collective-permute-start.31 = (bf16[288,128]{1,0:T(8,128)(2,1)S(1)}, bf16[288,128]{1,0:T(8,128)(2,1)S(1)}, u32[]{:S(2)}, u32[]{:S(2)}) collective-permute-start(bf16[288,128]{1,0:T(8,128)(2,1)S(1)} %collective-permute-done.30.refs_16_), channel_id=1, source_target_pairs={{0,32},{16,48},{32,64},{48,80},{64,96},{80,112},{96,128},{112,144}... | collective-permute-start | bytes 221192 | tf_op jit(solution)/shard_map/ppermute | solution.py:401
  135.9 5.6 %collective-permute-start.24 = (bf16[288,128]{1,0:T(8,128)(2,1)S(1)}, bf16[288,128]{1,0:T(8,128)(2,1)S(1)}, u32[]{:S(2)}, u32[]{:S(2)}) collective-permute-start(bf16[288,128]{1,0:T(8,128)(2,1)S(1)} %collective-permute-done.22.refs_6_), channel_id=1, source_target_pairs={{0,224},{16,240},{32,0},{48,16},{64,32},{80,48},{96,64},{112,80},{... | collective-permute-start | bytes 221192 | tf_op jit(solution)/shard_map/ppermute | solution.py:402
  139.4 5.6 %collective-permute-start.23 = (bf16[288,128]{1,0:T(8,128)(2,1)S(1)}, bf16[288,128]{1,0:T(8,128)(2,1)S(1)}, u32[]{:S(2)}, u32[]{:S(2)}) collective-permute-start(bf16[288,128]{1,0:T(8,128)(2,1)S(1)} %collective-permute-done.21.refs_5_), channel_id=1, source_target_pairs={{0,224},{16,240},{32,0},{48,16},{64,32},{80,48},{96,64},{112,80},{... | collective-permute-start | bytes 221192 | tf_op jit(solution)/shard_map/ppermute | solution.py:402
  140.1 5.6 %collective-permute-start.28 = (bf16[288,128]{1,0:T(8,128)(2,1)S(1)}, bf16[288,128]{1,0:T(8,128)(2,1)S(1)}, u32[]{:S(2)}, u32[]{:S(2)}) collective-permute-start(bf16[288,128]{1,0:T(8,128)(2,1)S(1)} %collective-permute-done.27.refs_11_), channel_id=1, source_target_pairs={{0,32},{16,48},{32,64},{48,80},{64,96},{80,112},{96,128},{112,144}... | collective-permute-start | bytes 221192 | tf_op jit(solution)/shard_map/ppermute | solution.py:406
  141.4 5.6 %collective-permute-start.32 = (bf16[288,128]{1,0:T(8,128)(2,1)S(1)}, bf16[288,128]{1,0:T(8,128)(2,1)S(1)}, u32[]{:S(2)}, u32[]{:S(2)}) collective-permute-start(bf16[288,128]{1,0:T(8,128)(2,1)S(1)} %collective-permute-done.31.refs_14_), channel_id=1, source_target_pairs={{0,32},{16,48},{32,64},{48,80},{64,96},{80,112},{96,128},{112,144}... | collective-permute-start | bytes 221192 | tf_op jit(solution)/shard_map/ppermute | solution.py:401
  141.5 5.5 %collective-permute-start.29 = (bf16[288,128]{1,0:T(8,128)(2,1)S(1)}, bf16[288,128]{1,0:T(8,128)(2,1)S(1)}, u32[]{:S(2)}, u32[]{:S(2)}) collective-permute-start(bf16[288,128]{1,0:T(8,128)(2,1)S(1)} %collective-permute-done.24.refs_8_), channel_id=1, source_target_pairs={{0,224},{16,240},{32,0},{48,16},{64,32},{80,48},{96,64},{112,80},{... | collective-permute-start | bytes 221192 | tf_op jit(solution)/shard_map/ppermute | solution.py:407
